TPU v7x, 768 devices: a whole 4x8x12 slice. The times are simulated.
768 devices in a mesh: row: 12 (over z_lo, core), col: 64 (over x, z_hi, y).
Axes of the slice: x: 4, y: 8, z: 12 (z_hi: 2, z_lo: 6; z = z_hi * 6 + z_lo), core: 2. Of those that a mesh axis runs over, the one named last changes fastest.
Arguments:
- tiles: bfloat16 [12, 64, 64, 64, 128], P('row', 'col'), may hold values from -6 to 6
- dest_col: int32 [12, 64, 64, 1], P('row', 'col'), may hold values from 0 to 63, as said below
- mu_block: int32 [12, 64, 64], P('row', 'col'), may hold values from 0 to 31, as said below
- col_block: int32 [12, 64, 64], P('row', 'col'), may hold values from 0 to 3, as said below
- coeff: bfloat16 [24576, 1536], P('row', 'col'), may hold values from -0.0390625 to 0.0390625
Outputs:
- contracted: bfloat16 [1536, 32768], P('row', 'col')
Inputs may be any that keep to these rules, and one draw needn't show every extreme that they name: `dest_col`: among the 64 blocks of one device at most 2 name the same column device, and in every draw some device sends exactly 2 to one column device. Every column device receives exactly 64 blocks from the devices of its row group. Blocks of one row group that name the same column device have distinct pairs (mu_block, col_block). `col_block`: see mu_block.
All inputs are finite; a program needn't handle non-finite values.
Results may differ from a plain program's by a relative error of at most 0.001.
Values may be sent and summed in bfloat16 or wider, within the bound.
No kernel may reach another device: no remote copies, remote signals or barrier semaphores. Data moves between devices by JAX's collectives and lax.ppermute only.
A program may use at most 32 MiB of HBM per device.

v0:
```python
import jax
import jax.numpy as jnp
from jax import lax
from jax.sharding import PartitionSpec as P

CB = 4


def per_device(tiles, dest_col, mu_block, col_block, coeff):
    col_count = lax.axis_size("col")
    held_tiles = tiles.shape[2]
    block_rows = tiles.shape[3]
    block_cols = tiles.shape[4]
    capacity = max(2, (2 * held_tiles + col_count - 1) // col_count)
    flattened = tiles.reshape(held_tiles, block_rows * block_cols)
    target = dest_col.reshape(held_tiles)
    local_mu = mu_block.reshape(held_tiles)
    local_column = col_block.reshape(held_tiles)
    position = jnp.arange(held_tiles)
    earlier = (target[:, None] == target[None, :]) & (position[None, :] < position[:, None])
    slot_rank = jnp.sum(earlier.astype(jnp.int32), axis=1)
    send_slot = target * capacity + slot_rank
    select = jnp.arange(col_count * capacity)[:, None] == send_slot[None, :]
    outgoing = jnp.dot(select.astype(jnp.bfloat16), flattened, preferred_element_type=jnp.float32)
    outgoing = outgoing.astype(jnp.bfloat16).reshape(col_count, capacity, block_rows, block_cols)
    cell_label = local_mu * CB + local_column + 1
    labels = jnp.sum(select.astype(jnp.int32) * cell_label[None, :], axis=1)
    labels = labels.astype(jnp.bfloat16).reshape(col_count, capacity)
    arrived, arrived_tags = (
        lax.all_to_all(outgoing, "col", split_axis=0, concat_axis=0, tiled=True),
        lax.all_to_all(labels, "col", split_axis=0, concat_axis=0, tiled=True),
    )
    recv_slots = col_count * capacity
    blocks_mu = coeff.shape[0] // block_rows
    tag_values = arrived_tags.reshape(recv_slots).astype(jnp.float32)
    cell_values = jnp.arange(blocks_mu * CB).astype(jnp.float32) + 1.0
    placing = (cell_values[:, None] == tag_values[None, :]).astype(jnp.bfloat16)
    dense_block = jnp.dot(
        placing,
        arrived.reshape(recv_slots, block_rows * block_cols),
        preferred_element_type=jnp.float32,
    )
    dense_block = dense_block.reshape(blocks_mu, CB, block_rows, block_cols).transpose(0, 2, 1, 3)
    dense_block = dense_block.reshape(blocks_mu * block_rows, CB * block_cols).astype(jnp.bfloat16)
    partial_value = lax.dot_general(
        lax.all_gather(coeff, "col", axis=1, tiled=True),
        dense_block,
        (((0,), (0,)), ((), ())),
        preferred_element_type=jnp.float32,
    )
    result = lax.psum_scatter(partial_value, "row", scatter_dimension=0, tiled=True)
    return result.astype(jnp.bfloat16)


def solution(mesh):
    in_specs = (
        P("row", "col", None, None, None),
        P("row", "col", None, None),
        P("row", "col", None),
        P("row", "col", None),
        P("row", "col"),
    )
    out_specs = P("row", "col")
    return jax.shard_map(
        per_device, mesh=mesh, in_specs=in_specs, out_specs=out_specs, check_vma=False
    )
```

profile of v0, /device:TPU:6, one launch (start us, length us, event | category | flops | bytes accessed | tf_op | source)
XLA Modules:
  0.0 371.9 jit_solution(3986047740648456031)
XLA Ops:
  6.5 0.0 all-gather.2.cloned.1.call-start
  6.5 0.7 all-gather.2.cloned.1.call-update
  7.3 0.9 convert_reduce_fusion.1
  8.2 0.7 multiply_add_fusion
  8.8 0.7 add_bitcast_fusion
  9.5 0.1 select_reduce_fusion
  9.6 0.8 convert_element_type.64
  10.4 23.5 %all-to-all-start = ((bf16[64,1,2]{2,1,0:T(2,128)(2,1)}), bf16[64,1,2]{2,1,0:T(2,128)(2,1)S(1)}, u32[]{:S(2)}, u32[]{:S(2)}) async-start(bf16[64,1,2]{2,1,0:T(2,128)(2,1)} %convert_element_type.64), calls=%async_computation | async-start | bytes 65536 | tf_op jit(solution)/shard_map/all_to_all | solution.py:31
  33.9 2.1 fusion.2
  36.0 1.9 copy.21
  38.0 10.5 %all-to-all-done = bf16[64,1,2]{2,1,0:T(2,128)(2,1)S(1)} async-done(((bf16[64,1,2]{2,1,0:T(2,128)(2,1)}), bf16[64,1,2]{2,1,0:T(2,128)(2,1)S(1)}, u32[]{:S(2)}, u32[]{:S(2)}) %all-to-all-start) | async-done | bytes 288 | tf_op jit(solution)/shard_map/all_to_all | solution.py:31
  48.5 7.0 %all-to-all-start.1 = ((bf16[64,2,64,128]{3,2,1,0:T(8,128)(2,1)}), bf16[64,2,64,128]{3,2,1,0:T(8,128)(2,1)S(1)}, u32[]{:S(2)}, u32[]{:S(2)}) async-start(bf16[64,2,64,128]{3,2,1,0:T(8,128)(2,1)} %bitcast.17), calls=%async_computation.1 | async-start | bytes 4194304 | tf_op jit(solution)/shard_map/all_to_all | solution.py:30
  55.6 0.2 reduce-scatter.2.cloned.1.call-start
  55.8 0.1 convert_reduce_fusion
  55.9 0.1 reshape.91
  56.0 49.2 %all-to-all-done.1 = bf16[64,2,64,128]{3,2,1,0:T(8,128)(2,1)S(1)} async-done(((bf16[64,2,64,128]{3,2,1,0:T(8,128)(2,1)}), bf16[64,2,64,128]{3,2,1,0:T(8,128)(2,1)S(1)}, u32[]{:S(2)}, u32[]{:S(2)}) %all-to-all-start.1) | async-done | bytes 2097184 | tf_op jit(solution)/shard_map/all_to_all | solution.py:30
  105.2 3.1 copy.33
  108.4 3.2 copy.16
  111.6 0.8 convert_bitcast_fusion
  112.4 1.6 copy.17
  114.0 169.9 %all-gather.2.cloned.1.call-done = bf16[2048,1536]{0,1:T(8,128)(2,1)} async-done(((bf16[2048,24]{0,1:T(8,128)(2,1)}), bf16[2048,1536]{0,1:T(8,128)(2,1)}) %all-gather.2.cloned.1.call-update) | async-done | bytes 6291472 | tf_op jit(solution)/shard_map/all_gather | solution.py:46
  283.9 7.9 %convolution_bitcast_fusion = f32[1536,512]{0,1:T(8,128)} fusion(bf16[2048,1536]{0,1:T(8,128)(2,1)} %all-gather.2.cloned.1.call-done, bf16[256,8,4,128]{3,2,1,0:T(4,128)(2,1)S(1)} %bitcast.42), kind=kOutput, calls=%fused_computation.1 | convolution fusion | flops 3221225472 | bytes 11534336 | tf_op jit(solution)/shard_map/dot_general | solution.py:45
  291.8 0.0 reduce-scatter.2.cloned.1.call-update
  291.9 71.4 %reduce-scatter.2.cloned.1.call-done = f32[128,512]{0,1:T(8,128)} async-done(((f32[1536,512]{0,1:T(8,128)}), f32[128,512]{0,1:T(8,128)}) %reduce-scatter.2.cloned.1.call-update) | async-done | bytes 262160 | tf_op jit(solution)/shard_map/reduce_scatter | solution.py:51
  363.3 1.0 convert_element_type.62
  364.3 0.8 copy.18
  (2 shorter events, 0.0 us)
Async XLA Ops:
  6.5 277.3 %all-gather.2.cloned.1.call-start = ((), (), s32[]{:S(2)}) async-start(), calls=%async_computation.3 | async-start | bytes 6389760 | tf_op jit(solution)/shard_map/all_gather | solution.py:46
  10.4 38.1 %all-to-all-start = ((bf16[64,1,2]{2,1,0:T(2,128)(2,1)}), bf16[64,1,2]{2,1,0:T(2,128)(2,1)S(1)}, u32[]{:S(2)}, u32[]{:S(2)}) async-start(bf16[64,1,2]{2,1,0:T(2,128)(2,1)} %convert_element_type.64), calls=%async_computation | async-start | bytes 65536 | tf_op jit(solution)/shard_map/all_to_all | solution.py:31
  48.5 56.7 %all-to-all-start.1 = ((bf16[64,2,64,128]{3,2,1,0:T(8,128)(2,1)}), bf16[64,2,64,128]{3,2,1,0:T(8,128)(2,1)S(1)}, u32[]{:S(2)}, u32[]{:S(2)}) async-start(bf16[64,2,64,128]{3,2,1,0:T(8,128)(2,1)} %bitcast.17), calls=%async_computation.1 | async-start | bytes 4194304 | tf_op jit(solution)/shard_map/all_to_all | solution.py:30
  55.6 307.7 %reduce-scatter.2.cloned.1.call-start = ((), (), s32[]{:S(2)}) async-start(), calls=%async_computation.4 | async-start | bytes 3407872 | tf_op jit(solution)/shard_map/reduce_scatter | solution.py:51
Sparse Core Ops, SparseCore 0:
  12.7 271.1 all-gather.1
  292.0 71.2 reduce-scatter.1
where the time goes:
time: 372 us
  waiting for transfers between devices  302 us (81%)
  starting transfers between devices  30.7 us (8%)
  between operations  13.5 us (4%)
  local copies, waits for them, and re-layouts  11.6 us (3%)
  matrix products  10.9 us (3%)
    all_gather x1, waiting for transfers between devices, per_device(): lax.all_gather(coeff, 'col', axis=1, tiled=True)  170 us
    reduce_scatter x1, waiting for transfers between devices, per_device(): lax.psum_scatter(partial_value, 'row', scatter_dimension=0, tiled=True)  71.4 us
    all_to_all x1, waiting for transfers between devices, per_device(): lax.all_to_all(outgoing, 'col', split_axis=0, concat_axis=0, tiled=True)  49.2 us
    all_to_all x1, starting transfers between devices, per_device(): lax.all_to_all(labels, 'col', split_axis=0, concat_axis=0, tiled=True)  23.5 us
    all_to_all x1, waiting for transfers between devices, per_device(): lax.all_to_all(labels, 'col', split_axis=0, concat_axis=0, tiled=True)  10.5 us
    dot_general x1, matrix products, per_device(): lax.dot_general(lax.all_gather(coeff, 'col', axis=1, tiled=True), dense_b...  7.95 us
  transfers between devices with their start and end apart: 4, of which 4 were waited for; matrix products, arithmetic and copies ran while one was open for 4% of the time, Pallas kernels for 0%

commit v1 on v0

v1 whole, which is shorter than its diff:
```python
import functools

import jax
import jax.numpy as jnp
from jax import lax
from jax.experimental import pallas as pl
from jax.experimental.pallas import tpu as pltpu
from jax.sharding import PartitionSpec as P

CB = 4
CAP = 2
NX, NZH, NY = 4, 2, 8
NZL, NCORE = 6, 2
LABEL_ROWS = 16


def device(zl, core, x, zh, y):
    return (((zl * NCORE + core) * NX + x) * NZH + zh) * NY + y


def plane_groups():
    return [
        [device(zl, core, x, zh, y) for x in range(NX) for y in range(NY)]
        for zl in range(NZL)
        for core in range(NCORE)
        for zh in range(NZH)
    ]


def column_groups():
    return [
        [
            device(zl, core, x, zh, y)
            for zh in range(NZH)
            for zl in range(NZL)
            for core in range(NCORE)
        ]
        for x in range(NX)
        for y in range(NY)
    ]


def pack_kernel(dest, mu, colb, tiles, out, count):
    held, rows, cols = tiles.shape
    label_at = NZH * CAP * rows

    @pl.loop(0, NX * NZH * NY)
    def _(c):
        count[c] = 0

    @pl.loop(0, NX * NY)
    def _(j):
        out[j, pl.ds(label_at, LABEL_ROWS), :] = jnp.zeros((LABEL_ROWS, cols), out.dtype)

    lane = lax.broadcasted_iota(jnp.int32, (LABEL_ROWS, cols), 1)

    @pl.loop(0, held)
    def _(t):
        c = dest[t]
        rank = count[c]
        count[c] = rank + 1
        j = (c // (NZH * NY)) * NY + c % NY
        slot = ((c // NY) % NZH) * CAP + rank
        out[j, pl.ds(pl.multiple_of(slot * rows, rows), rows), :] = tiles[t]
        label = (mu[t] * CB + colb[t] + 1).astype(jnp.float32)
        old = out[j, pl.ds(label_at, LABEL_ROWS), :].astype(jnp.float32)
        out[j, pl.ds(label_at, LABEL_ROWS), :] = jnp.where(lane == slot, label, old).astype(out.dtype)


def pack(tiles, dest, mu, colb):
    held, rows, cols = tiles.shape
    smem = pl.BlockSpec(memory_space=pltpu.SMEM)
    vmem = pl.BlockSpec(memory_space=pltpu.VMEM)
    return pl.pallas_call(
        pack_kernel,
        out_shape=jax.ShapeDtypeStruct((NX * NY, NZH * CAP * rows + LABEL_ROWS, cols), tiles.dtype),
        in_specs=[smem, smem, smem, vmem],
        out_specs=vmem,
        scratch_shapes=[pltpu.SMEM((NX * NZH * NY,), jnp.int32)],
        compiler_params=pltpu.CompilerParams(vmem_limit_bytes=24 << 20),
        cost_estimate=pl.CostEstimate(flops=0, bytes_accessed=4 << 20, transcendentals=0),
        name="pack",
    )(dest, mu, colb, tiles)


def contract_kernel(labels, plane, arrived, own, other, out, dense):
    rows = 64
    cols = arrived.shape[2]
    slots = NZH * CAP

    @pl.when(pl.program_id(0) == 0)
    def _():
        @pl.loop(0, dense.shape[0] // rows)
        def _(m):
            dense[pl.ds(pl.multiple_of(m * rows, rows), rows), :] = jnp.zeros((rows, dense.shape[1]), dense.dtype)

        @pl.loop(0, NX * NY)
        def _(j):
            for slot in range(slots):
                label = labels[j, slot]

                @pl.when(label > 0)
                def _():
                    cell = label - 1
                    row = pl.multiple_of((cell // CB) * rows, rows)
                    col = pl.multiple_of((slot // CAP * CB + cell % CB) * cols, cols)
                    dense[pl.ds(row, rows), pl.ds(col, cols)] = arrived[j, pl.ds(slot * rows, rows), :]

    width = CB * cols

    def multiply(a):
        for h in range(NZH):
            out[h] = jnp.dot(a[...], dense[:, h * width : (h + 1) * width], preferred_element_type=jnp.float32)

    @pl.when(pl.program_id(0) < NX)
    def _():
        multiply(own)

    @pl.when(pl.program_id(0) >= NX)
    def _():
        multiply(other)


def contract(labels, plane, arrived, own, other):
    occ, mu_rows = own.shape
    cols = arrived.shape[2]
    step = occ // NX

    def rows_of(i, labels, plane):
        return 0, i % NX * NZH + jnp.where(i < NX, plane[0], 1 - plane[0]), 0

    return pl.pallas_call(
        contract_kernel,
        out_shape=jax.ShapeDtypeStruct((NZH, occ * NZH, CB * cols), jnp.float32),
        grid_spec=pltpu.PrefetchScalarGridSpec(
            num_scalar_prefetch=2,
            grid=(NX * NZH,),
            in_specs=[
                pl.BlockSpec(arrived.shape, lambda i, labels, plane: (0, 0, 0)),
                pl.BlockSpec((step, mu_rows), lambda i, labels, plane: (jnp.minimum(i, NX - 1), 0)),
                pl.BlockSpec((step, mu_rows), lambda i, labels, plane: (jnp.maximum(i - NX, 0), 0)),
            ],
            out_specs=pl.BlockSpec((NZH, step, CB * cols), rows_of),
            scratch_shapes=[pltpu.VMEM((mu_rows, NZH * CB * cols), own.dtype)],
        ),
        compiler_params=pltpu.CompilerParams(vmem_limit_bytes=40 << 20),
        cost_estimate=pl.CostEstimate(
            flops=4 * occ * mu_rows * NZH * CB * cols, bytes_accessed=15 << 20, transcendentals=0
        ),
        name="contract",
    )(labels, plane, arrived, own, other)


AXES = ("row", "col")


def per_device(tiles, dest_col, mu_block, col_block, coeff):
    held, rows, cols = tiles.shape[2:]
    plane = (lax.axis_index("col") // NY % NZH).reshape(1)
    mine = coeff.T
    groups = plane_groups()
    swap = [(c, (c // NY // NZH * NZH + 1 - c // NY % NZH) * NY + c % NY) for c in range(NX * NZH * NY)]
    theirs = lax.ppermute(mine, "col", swap)
    own = lax.all_gather(mine, AXES, axis=0, tiled=True, axis_index_groups=groups)
    other = lax.all_gather(theirs, AXES, axis=0, tiled=True, axis_index_groups=groups)
    outgoing = pack(
        tiles.reshape(held, rows, cols), dest_col.reshape(held), mu_block.reshape(held), col_block.reshape(held)
    )
    arrived = lax.all_to_all(outgoing, AXES, split_axis=0, concat_axis=0, tiled=True, axis_index_groups=groups)
    labels = arrived[:, NZH * CAP * rows, : NZH * CAP].astype(jnp.int32)
    share = contract(labels, plane, arrived, own, other)
    share = share.reshape(-1, share.shape[2])
    result = lax.psum_scatter(share, AXES, scatter_dimension=0, tiled=True, axis_index_groups=column_groups())
    return result.astype(jnp.bfloat16)


def solution(mesh):
    in_specs = (
        P("row", "col", None, None, None),
        P("row", "col", None, None),
        P("row", "col", None),
        P("row", "col", None),
        P("row", "col"),
    )
    return jax.shard_map(per_device, mesh=mesh, in_specs=in_specs, out_specs=P("row", "col"), check_vma=False)
```

time: 372 us -> 330 us (0.89)
  waiting for transfers between devices: 302 us -> 266 us
  Pallas kernels: 0 us -> 16.2 us
  matrix products: 10.9 us -> 0 us
  starting transfers between devices: 30.7 us -> 25.5 us
  local copies, waits for them, and re-layouts: 11.6 us -> 7.6 us
    all_gather x1 -> x2, waiting for transfers between devices: 170 us -> 111 us  [the longest x1 92.2 us: per_device(): lax.all_gather(theirs, AXES, axis=0, tiled=True, axis_index_groups=groups)]
    reduce_scatter x1, waiting for transfers between devices: 71.4 us -> 94.6 us  [per_device(): lax.psum_scatter(share, AXES, scatter_dimension=0, tiled=True, axis_index...]
    all_to_all x2 -> x1, starting transfers between devices: 30.5 us -> 10.2 us  [per_device(): lax.all_to_all(outgoing, AXES, split_axis=0, concat_axis=0, tiled=True, a...]
    pallas_call x0 -> x2, Pallas kernels: none -> 16.2 us  [the longest x1 12.1 us: contract(): pl.pallas_call(contract_kernel, out_shape=jax.ShapeDtypeStruct((NZH, occ...]
    ppermute x0 -> x1, starting transfers between devices: none -> 15.1 us  [per_device(): theirs = lax.ppermute(mine, 'col', swap)]
    dot_general x3 -> x0, matrix products: 10.9 us -> none  [the longest x1 7.95 us: per_device(): lax.dot_general(lax.all_gather(coeff, 'col', axis=1, tiled=True), dense_b...]
    all_to_all x2 -> x1, waiting for transfers between devices: 59.7 us -> 56.6 us  [per_device(): lax.all_to_all(outgoing, AXES, split_axis=0, concat_axis=0, tiled=True, a...]
    unnamed x2 -> x14, local copies, waits for them, and re-layouts: 5.09 us -> 7.6 us
  transfers between devices with their start and end apart: 4 -> 5, of which waited for: 4 -> 5; matrix products, arithmetic and copies ran while one was open for 4% -> 0% of each run, Pallas kernels for 0% -> 1%
where the time goes in v1:
time: 330 us
  waiting for transfers between devices  266 us (81%)
  starting transfers between devices  25.5 us (8%)
  Pallas kernels  16.2 us (5%)
  between operations  13.2 us (4%)
  local copies, waits for them, and re-layouts  7.6 us (2%)
    reduce_scatter x1, waiting for transfers between devices, per_device(): lax.psum_scatter(share, AXES, scatter_dimension=0, tiled=True, axis_index...  94.6 us
    all_gather x1, waiting for transfers between devices, per_device(): lax.all_gather(theirs, AXES, axis=0, tiled=True, axis_index_groups=groups)  92.2 us
    all_to_all x1, waiting for transfers between devices, per_device(): lax.all_to_all(outgoing, AXES, split_axis=0, concat_axis=0, tiled=True, a...  56.6 us
    all_gather x1, waiting for transfers between devices, per_device(): lax.all_gather(mine, AXES, axis=0, tiled=True, axis_index_groups=groups)  18.4 us
    ppermute x1, starting transfers between devices, per_device(): theirs = lax.ppermute(mine, 'col', swap)  15.1 us
    pallas_call x1, Pallas kernels, contract(): pl.pallas_call(contract_kernel, out_shape=jax.ShapeDtypeStruct((NZH, occ...  12.1 us
    all_to_all x1, starting transfers between devices, per_device(): lax.all_to_all(outgoing, AXES, split_axis=0, concat_axis=0, tiled=True, a...  10.2 us
    unnamed x14, local copies, waits for them, and re-layouts  7.6 us
  transfers between devices with their start and end apart: 5, of which 5 were waited for; matrix products, arithmetic and copies ran while one was open for 0% of the time, Pallas kernels for 1%

profile of v1, /device:TPU:6, one launch (start us, length us, event | category | flops | bytes accessed | tf_op | source)
XLA Modules:
  0.0 329.8 jit_solution(11355283017908962001)
XLA Ops:
  6.5 0.0 all-gather.3.cloned.1.call-start
  6.5 0.7 all-gather.3.cloned.1.call-update
  7.3 0.0 all-gather.5.cloned.1.call-start
  7.3 15.1 %collective-permute-start = (bf16[24,2048]{1,0:T(8,128)(2,1)}, bf16[24,2048]{1,0:T(8,128)(2,1)S(1)}, u32[]{:S(2)}, u32[]{:S(2)}) collective-permute-start(bf16[24,2048]{1,0:T(8,128)(2,1)} %bitcast.15), channel_id=1, source_target_pairs={{0,8},{1,9},{2,10},{3,11},{4,12},{5,13},{6,14},{7,15},{8,0},{9,1},... | collective-permute-start | bytes 294920 | tf_op jit(solution)/shard_map/ppermute | solution.py:163
  22.4 3.2 collective-permute-done
  25.6 0.0 copy-start.6
  25.6 0.6 copy-done.6
  26.3 0.0 all-gather.5.cloned.1.call-update
  26.3 0.0 copy-start
  26.3 1.2 copy-done
  27.5 0.0 copy-start.1
  27.5 0.7 copy-done.1
  28.2 0.0 copy-start.2
  28.2 0.7 copy-done.2
  28.8 0.0 copy-start.3
  28.8 0.7 copy-done.3
  29.5 4.1 %pack.1 = bf16[32,272,128]{2,1,0:T(8,128)(2,1)} custom-call(s32[64]{0:T(128)S(1)} %bitcast.10, s32[64]{0:T(128)S(1)} %bitcast.11, s32[64]{0:T(128)S(1)} %bitcast.12, bf16[64,64,128]{2,1,0:T(8,128)(2,1)S(1)} %bitcast.8), custom_call_target="tpu_custom_call" | custom-call | bytes 4194304 | tf_op jit(solution)/shard_map/pack/pallas_call | solution.py:74
  33.6 10.2 %all-to-all-start = ((bf16[32,272,128]{2,1,0:T(8,128)(2,1)}), bf16[32,272,128]{2,1,0:T(8,128)(2,1)S(1)}, u32[]{:S(2)}, u32[]{:S(2)}) async-start(bf16[32,272,128]{2,1,0:T(8,128)(2,1)} %pack.1), calls=%async_computation | async-start | bytes 4456448 | tf_op jit(solution)/shard_map/all_to_all | solution.py:169
  43.9 0.0 reduce-scatter.2.cloned.1.call-start
  44.0 56.6 %all-to-all-done.arrived = bf16[32,272,128]{2,1,0:T(8,128)(2,1)S(1)} async-done(((bf16[32,272,128]{2,1,0:T(8,128)(2,1)}), bf16[32,272,128]{2,1,0:T(8,128)(2,1)S(1)}, u32[]{:S(2)}, u32[]{:S(2)}) %all-to-all-start) | async-done | bytes 2228256 | tf_op jit(solution)/shard_map/all_to_all | solution.py:169
  100.5 18.4 %all-gather.3.cloned.1.call-done.own = bf16[768,2048]{1,0:T(8,128)(2,1)} async-done(((bf16[24,2048]{1,0:T(8,128)(2,1)}), bf16[768,2048]{1,0:T(8,128)(2,1)}) %all-gather.3.cloned.1.call-update) | async-done | bytes 3145744 | tf_op jit(solution)/shard_map/all_gather | solution.py:164
  118.9 92.2 %all-gather.5.cloned.1.call-done.other = bf16[768,2048]{1,0:T(8,128)(2,1)} async-done(((bf16[24,2048]{1,0:T(8,128)(2,1)}), bf16[768,2048]{1,0:T(8,128)(2,1)}) %all-gather.5.cloned.1.call-update) | async-done | bytes 3145744 | tf_op jit(solution)/shard_map/all_gather | solution.py:165
  211.2 0.0 copy-start.4
  211.2 1.9 copy-done.4
  213.1 0.0 copy-start.5
  213.1 1.9 copy-done.5
  214.9 12.1 %contract.1 = f32[2,1536,512]{2,1,0:T(8,128)} custom-call(s32[32,4]{1,0:T(8,128)S(1)} %bitcast.9, s32[1]{0:T(128)} %bitcast.5.plane, bf16[32,272,128]{2,1,0:T(8,128)(2,1)S(1)} %all-to-all-done.arrived, bf16[768,2048]{1,0:T(8,128)(2,1)S(1)} %copy-done.4, bf16[768,2048]{1,0:T(8,128)(2,1)S(1)} %copy-done.5), custom_call_target="tpu_custom_call" | custom-call | flops 6442450944 | bytes 15728640 | tf_op jit(solution)/shard_map/contract/pallas_call | solution.py:132
  227.0 0.0 reduce-scatter.2.cloned.1.call-update
  227.1 94.6 %reduce-scatter.2.cloned.1.call-done = f32[128,512]{1,0:T(8,128)} async-done(((f32[3072,512]{1,0:T(8,128)}), f32[128,512]{1,0:T(8,128)}) %reduce-scatter.2.cloned.1.call-update) | async-done | bytes 262160 | tf_op jit(solution)/shard_map/reduce_scatter | solution.py:173
  321.7 1.6 convert_element_type.10
  (1 shorter events, 0.0 us)
Async XLA Ops:
  6.5 112.4 %all-gather.3.cloned.1.call-start = ((), (), s32[]{:S(2)}) async-start(), calls=%async_computation.2 | async-start | bytes 3244032 | tf_op jit(solution)/shard_map/all_gather | solution.py:164
  7.3 203.9 %all-gather.5.cloned.1.call-start = ((), (), s32[]{:S(2)}) async-start(), calls=%async_computation.3 | async-start | bytes 3244032 | tf_op jit(solution)/shard_map/all_gather | solution.py:165
  7.3 18.3 %collective-permute-start = (bf16[24,2048]{1,0:T(8,128)(2,1)}, bf16[24,2048]{1,0:T(8,128)(2,1)S(1)}, u32[]{:S(2)}, u32[]{:S(2)}) collective-permute-start(bf16[24,2048]{1,0:T(8,128)(2,1)} %bitcast.15), channel_id=1, source_target_pairs={{0,8},{1,9},{2,10},{3,11},{4,12},{5,13},{6,14},{7,15},{8,0},{9,1},... | collective-permute-start | bytes 294920 | tf_op jit(solution)/shard_map/ppermute | solution.py:163
  25.6 0.6 copy-start.6
  26.3 1.2 copy-start
  27.5 0.7 copy-start.1
  28.2 0.7 copy-start.2
  28.8 0.7 copy-start.3
  33.6 66.9 %all-to-all-start = ((bf16[32,272,128]{2,1,0:T(8,128)(2,1)}), bf16[32,272,128]{2,1,0:T(8,128)(2,1)S(1)}, u32[]{:S(2)}, u32[]{:S(2)}) async-start(bf16[32,272,128]{2,1,0:T(8,128)(2,1)} %pack.1), calls=%async_computation | async-start | bytes 4456448 | tf_op jit(solution)/shard_map/all_to_all | solution.py:169
  43.9 277.8 %reduce-scatter.2.cloned.1.call-start = ((), (), s32[]{:S(2)}) async-start(), calls=%async_computation.4 | async-start | bytes 6553600 | tf_op jit(solution)/shard_map/reduce_scatter | solution.py:173
  211.2 1.9 copy-start.4
  213.1 1.9 copy-start.5
Sparse Core Ops, SparseCore 0:
  11.1 107.7 all-gather.2
  122.7 88.4 all-gather.4
  227.2 94.4 reduce-scatter.1

commit v2 on v0

v2 whole, which is shorter than its diff:
```python
import jax
import jax.numpy as jnp
from jax import lax
from jax.experimental import pallas as pl
from jax.experimental.pallas import tpu as pltpu
from jax.sharding import PartitionSpec as P

CB = 4
CAP = 2
NX, NZH, NY = 4, 2, 8
NZL, NCORE = 6, 2
N_COL = NX * NZH * NY
LABEL_ROWS = 16
CELLS = 128
GROUP = 8
OUT_ROWS = 128


def device(zl, core, x, zh, y):
    return (((zl * NCORE + core) * NX + x) * NZH + zh) * NY + y


def column(x, zh, y):
    return (x * NZH + zh) * NY + y


X_GROUPS = [[column(x, zh, y) for x in range(NX)] for zh in range(NZH) for y in range(NY)]
Y_GROUPS = [[column(x, zh, y) for y in range(NY)] for x in range(NX) for zh in range(NZH)]
ZL_GROUPS = [[zl * NCORE + core for zl in range(NZL)] for core in range(NCORE)]
PLANE_SWAP = [
    (column(x, zh, y), column(x, 1 - zh, y)) for x in range(NX) for zh in range(NZH) for y in range(NY)
]
CORE_SWAP = [(zl * NCORE + core, zl * NCORE + 1 - core) for zl in range(NZL) for core in range(NCORE)]


def x_shift(by):
    return [
        (column(x, zh, y), column((x + by) % NX, zh, y))
        for x in range(NX)
        for zh in range(NZH)
        for y in range(NY)
    ]


def pack_kernel(route, tiles, out, count):
    held, rows, cols = tiles.shape
    label_at = CAP * rows

    @pl.loop(0, N_COL)
    def _(c):
        count[c] = 0
        out[c, pl.ds(label_at, LABEL_ROWS), :] = jnp.zeros((LABEL_ROWS, cols), out.dtype)

    lane = lax.broadcasted_iota(jnp.int32, (LABEL_ROWS, cols), 1)

    @pl.loop(0, held)
    def _(t):
        c = route[t] // CELLS
        slot = count[c]
        count[c] = slot + 1
        out[c, pl.ds(pl.multiple_of(slot * rows, rows), rows), :] = tiles[t]
        label = (route[t] % CELLS + 1).astype(jnp.float32)
        old = out[c, pl.ds(label_at, LABEL_ROWS), :].astype(jnp.float32)
        out[c, pl.ds(label_at, LABEL_ROWS), :] = jnp.where(lane == slot, label, old).astype(out.dtype)


SMEM = pl.BlockSpec(memory_space=pltpu.SMEM)
VMEM = pl.BlockSpec(memory_space=pltpu.VMEM)
ANY = pl.BlockSpec(memory_space=pl.ANY)


def pack(tiles, route):
    held, rows, cols = tiles.shape
    return pl.pallas_call(
        pack_kernel,
        out_shape=jax.ShapeDtypeStruct((N_COL, CAP * rows + LABEL_ROWS, cols), tiles.dtype),
        in_specs=[SMEM, VMEM],
        out_specs=VMEM,
        scratch_shapes=[pltpu.SMEM((N_COL,), jnp.int32)],
        compiler_params=pltpu.CompilerParams(vmem_limit_bytes=24 << 20),
        cost_estimate=pl.CostEstimate(flops=0, bytes_accessed=4 << 20, transcendentals=0),
        name="pack",
    )(route, tiles)


def place_kernel(labels, arrived, dense):
    rows = (arrived.shape[1] - LABEL_ROWS) // CAP
    cols = arrived.shape[2]

    @pl.loop(0, dense.shape[0] // rows)
    def _(m):
        dense[pl.ds(pl.multiple_of(m * rows, rows), rows), :] = jnp.zeros((rows, dense.shape[1]), dense.dtype)

    @pl.loop(0, N_COL)
    def _(j):
        for slot in range(CAP):
            label = labels[j, slot]

            @pl.when(label > 0)
            def _():
                cell = label - 1
                row = pl.multiple_of((cell // CB) * rows, rows)
                col = pl.multiple_of(cell % CB * cols, cols)
                dense[pl.ds(row, rows), pl.ds(col, cols)] = arrived[j, pl.ds(slot * rows, rows), :]


def place(labels, arrived, mu_rows):
    return pl.pallas_call(
        place_kernel,
        out_shape=jax.ShapeDtypeStruct((mu_rows, CB * arrived.shape[2]), arrived.dtype),
        in_specs=[SMEM, VMEM],
        out_specs=VMEM,
        compiler_params=pltpu.CompilerParams(vmem_limit_bytes=24 << 20),
        cost_estimate=pl.CostEstimate(flops=0, bytes_accessed=4 << 20, transcendentals=0),
        name="place",
    )(labels, arrived)


def contract_kernel(where, own, near, left, right, far0, far1, dense, keep, send, total, sem):
    x, plane, core = where[0], where[1], where[2]
    per = near.shape[0] // NY
    groups = OUT_ROWS // GROUP

    def store(c, block):
        for i in range(per // GROUP):
            g = c * (per // GROUP) + i
            away = jnp.where(g // groups % NCORE == core, 0, 1)
            row = pl.multiple_of((g // (groups * NCORE) * groups + g % groups) * GROUP, GROUP)
            total[away, pl.ds(row, GROUP), :] = block[i * GROUP : (i + 1) * GROUP]

    half = NY // 2
    for h in range(2):
        a = own[h * half : (h + 1) * half].reshape(half * NX * per, own.shape[2])
        product = jnp.dot(a, dense[...], preferred_element_type=jnp.float32)
        for y in range(half):
            for xx in range(NX):
                at = (y * NX + xx) * per
                store((xx * NZH + plane) * NY + h * half + y, product[at : at + per])
    for by, parts in ((0, (near,)), (NX - 1, (left,)), (1, (right,)), (2, (far0, far1))):
        a = parts[0][...] if len(parts) == 1 else jnp.concatenate([p[...] for p in parts], axis=0)
        product = jnp.dot(a, dense[...], preferred_element_type=jnp.float32)
        for y in range(NY):
            store(((x + by) % NX * NZH + 1 - plane) * NY + y, product[y * per : (y + 1) * per])
    copies = [pltpu.make_async_copy(total.at[k], ref, sem.at[k]) for k, ref in enumerate((keep, send))]
    for copy in copies:
        copy.start()
    for copy in copies:
        copy.wait()


def contract(where, own, near, left, right, far0, far1, dense):
    occ = own.shape[0] * own.shape[1] * NZH
    shape = jax.ShapeDtypeStruct((occ // NCORE, dense.shape[1]), jnp.float32)
    return pl.pallas_call(
        contract_kernel,
        out_shape=(shape, shape),
        in_specs=[SMEM] + [VMEM] * 7,
        out_specs=(ANY, ANY),
        scratch_shapes=[
            pltpu.VMEM((NCORE, *shape.shape), jnp.float32),
            pltpu.SemaphoreType.DMA((NCORE,)),
        ],
        compiler_params=pltpu.CompilerParams(vmem_limit_bytes=40 << 20),
        cost_estimate=pl.CostEstimate(
            flops=2 * occ * dense.shape[0] * dense.shape[1], bytes_accessed=12 << 20, transcendentals=0
        ),
        name="contract",
    )(where, own, near, left, right, far0, far1, dense)


def per_device(tiles, dest_col, mu_block, col_block, coeff):
    held, rows, cols = tiles.shape[2:]
    mu_rows, per = coeff.shape
    here = lax.axis_index("col")
    where = jnp.stack([here // (NZH * NY), here // NY % NZH, lax.axis_index("row") % NCORE]).astype(jnp.int32)
    route = dest_col.reshape(held) * CELLS + mu_block.reshape(held) * CB + col_block.reshape(held)
    outgoing = pack(tiles.reshape(held, rows, cols), route)
    outgoing, mine = lax.optimization_barrier((outgoing, coeff.T))
    arrived = lax.all_to_all(outgoing, "col", split_axis=0, concat_axis=0, tiled=True)
    theirs = lax.ppermute(mine, "col", PLANE_SWAP)

    own = lax.all_gather(mine, "col", axis=0, tiled=True, axis_index_groups=X_GROUPS)
    own = lax.all_gather(own, "col", axis=0, tiled=True, axis_index_groups=Y_GROUPS)
    own = own.reshape(NY, NX * per, mu_rows)

    near = lax.all_gather(theirs, "col", axis=0, tiled=True, axis_index_groups=Y_GROUPS)
    left = lax.ppermute(near, "col", x_shift(1))
    right = lax.ppermute(near, "col", x_shift(-1))
    cut = near.shape[0] // 2
    far0 = lax.ppermute(left[:cut], "col", x_shift(1))
    far1 = lax.ppermute(right[cut:], "col", x_shift(-1))

    labels = arrived[:, CAP * rows, :CAP].astype(jnp.int32)
    dense = place(labels, arrived, mu_rows)
    keep, send = contract(where, own, near, left, right, far0, far1, dense)
    share = keep + lax.ppermute(send, "row", CORE_SWAP)
    result = lax.psum_scatter(share, "row", scatter_dimension=0, tiled=True, axis_index_groups=ZL_GROUPS)
    return result.astype(jnp.bfloat16)


def solution(mesh):
    in_specs = (
        P("row", "col", None, None, None),
        P("row", "col", None, None),
        P("row", "col", None),
        P("row", "col", None),
        P("row", "col"),
    )
    return jax.shard_map(per_device, mesh=mesh, in_specs=in_specs, out_specs=P("row", "col"), check_vma=False)
```

time: 372 us -> 264 us (0.71)
  waiting for transfers between devices: 302 us -> 104 us
  blocking collectives: 0 us -> 62.3 us
  starting transfers between devices: 30.7 us -> 56.7 us
  Pallas kernels: 0 us -> 11.1 us
  matrix products: 10.9 us -> 0 us
    all_gather x1, waiting for transfers between devices: 170 us -> 0.01 us  [per_device(): lax.all_gather(own, 'col', axis=0, tiled=True, axis_index_groups=Y_GROUPS)]
    all_gather x0 -> x2, blocking collectives: none -> 62.3 us  [the longest x1 47.4 us: per_device(): lax.all_gather(theirs, 'col', axis=0, tiled=True, axis_index_groups=Y_GRO...]
    all_to_all x1, waiting for transfers between devices: 49.2 us -> 0.01 us  [per_device(): lax.all_to_all(outgoing, 'col', split_axis=0, concat_axis=0, tiled=True)]
    ppermute x0 -> x6, starting transfers between devices: none -> 33 us  [the longest x1 17 us: per_device(): theirs = lax.ppermute(mine, 'col', PLANE_SWAP)]
    all_to_all x1 -> x0, starting transfers between devices: 23.5 us -> none  [per_device(): lax.all_to_all(labels, 'col', split_axis=0, concat_axis=0, tiled=True)]
    ppermute x0 -> x6, waiting for transfers between devices: none -> 21 us  [the longest x1 11 us: per_device(): right = lax.ppermute(near, 'col', x_shift(-1))]
    all_to_all x1, starting transfers between devices: 7.03 us -> 23.6 us  [per_device(): lax.all_to_all(outgoing, 'col', split_axis=0, concat_axis=0, tiled=True)]
    reduce_scatter x1, waiting for transfers between devices: 71.4 us -> 83 us  [per_device(): lax.psum_scatter(share, 'row', scatter_dimension=0, tiled=True, axis_inde...]
  transfers between devices with their start and end apart: 4 -> 9, of which waited for: 4 -> 5; matrix products, arithmetic and copies ran while one was open for 4% -> 1% of each run, Pallas kernels for 0% -> 1%
where the time goes in v2:
time: 264 us; the launch traced here: 263 us
  waiting for transfers between devices  104 us (39%)
  blocking collectives  62.3 us (24%)
  starting transfers between devices  56.7 us (21%)
  between operations  13.6 us (5%)
  local copies, waits for them, and re-layouts  11.7 us (4%)
  Pallas kernels  11.1 us (4%)
  other arithmetic  3.92 us (1%)
    reduce_scatter x1, waiting for transfers between devices, per_device(): lax.psum_scatter(share, 'row', scatter_dimension=0, tiled=True, axis_inde...  83 us
    all_gather x1, blocking collectives, per_device(): lax.all_gather(theirs, 'col', axis=0, tiled=True, axis_index_groups=Y_GRO...  47.4 us
    all_to_all x1, starting transfers between devices, per_device(): lax.all_to_all(outgoing, 'col', split_axis=0, concat_axis=0, tiled=True)  23.6 us
    ppermute x1, starting transfers between devices, per_device(): theirs = lax.ppermute(mine, 'col', PLANE_SWAP)  17 us
    all_gather x1, blocking collectives, per_device(): lax.all_gather(mine, 'col', axis=0, tiled=True, axis_index_groups=X_GROUPS)  14.9 us
    ppermute x1, waiting for transfers between devices, per_device(): right = lax.ppermute(near, 'col', x_shift(-1))  11 us
    unnamed x20, local copies, waits for them, and re-layouts  9.95 us
    ppermute x1, waiting for transfers between devices, per_device(): theirs = lax.ppermute(mine, 'col', PLANE_SWAP)  5.88 us
  transfers between devices with their start and end apart: 9, of which 5 were waited for; matrix products, arithmetic and copies ran while one was open for 1% of the time, Pallas kernels for 1%

profile of v2, /device:TPU:6, one launch (start us, length us, event | category | flops | bytes accessed | tf_op | source)
XLA Modules:
  0.0 263.3 jit_solution(14628454691291134795)
XLA Ops:
  6.5 0.7 bitcast_add_fusion.route
  7.2 0.0 copy-start.3
  7.2 1.2 copy-done.3
  8.5 2.3 pack.1
  10.7 0.0 copy-start
  10.7 1.4 copy-done
  12.2 0.0 copy-start.9
  12.2 23.6 %all-to-all-start = ((bf16[64,144,128]{2,1,0:T(8,128)(2,1)}), bf16[64,144,128]{2,1,0:T(8,128)(2,1)S(1)}, u32[]{:S(2)}, u32[]{:S(2)}) async-start(bf16[64,144,128]{2,1,0:T(8,128)(2,1)} %copy-done), calls=%async_computation | async-start | bytes 4718592 | tf_op jit(solution)/shard_map/all_to_all | solution.py:179
  35.8 0.0 all-gather.2.cloned.1.call-start
  35.8 0.0 copy-done.9
  35.8 14.9 %all_gather.9 = bf16[96,2048]{1,0:T(8,128)(2,1)} all-gather(bf16[24,2048]{1,0:T(8,128)(2,1)S(1)} %bitcast.18), channel_id=1, replica_groups={{0,16,32,48},{1,17,33,49},{2,18,34,50},{3,19,35,51},{4,20,36,52},{5,21,..., dimensions={0}, use_global_device_ids=true | all-gather | bytes 491520 | tf_op jit(solution)/shard_map/all_gather | solution.py:182
  50.7 0.0 all-gather.2.cloned.1.call-update
  50.7 0.0 reduce-scatter.2.cloned.1.call-start
  50.8 17.0 %collective-permute-start = (bf16[24,2048]{1,0:T(8,128)(2,1)S(1)}, bf16[24,2048]{1,0:T(8,128)(2,1)S(1)}, u32[]{:S(2)}, u32[]{:S(2)}) collective-permute-start(bf16[24,2048]{1,0:T(8,128)(2,1)S(1)} %bitcast.19), channel_id=1, source_target_pairs={{0,8},{1,9},{2,10},{3,11},{4,12},{5,13},{6,14},{7,15},{8,0},{9,1},... | collective-permute-start | bytes 294920 | tf_op jit(solution)/shard_map/ppermute | solution.py:180
  67.8 5.9 %collective-permute-done = bf16[24,2048]{1,0:T(8,128)(2,1)S(1)} collective-permute-done((bf16[24,2048]{1,0:T(8,128)(2,1)S(1)}, bf16[24,2048]{1,0:T(8,128)(2,1)S(1)}, u32[]{:S(2)}, u32[]{:S(2)}) %collective-permute-start) | collective-permute-done | bytes 98336 | tf_op jit(solution)/shard_map/ppermute | solution.py:180
  73.7 47.4 %all_gather.11.near = bf16[192,2048]{1,0:T(8,128)(2,1)S(1)} all-gather(bf16[24,2048]{1,0:T(8,128)(2,1)S(1)} %collective-permute-done), channel_id=1, replica_groups={{0,1,2,3,4,5,6,7},{8,9,10,11,12,13,14,15},{16,17,18,19,20,21,22,23},{24..., dimensions={0}, use_global_device_ids=true | all-gather | bytes 884736 | tf_op jit(solution)/shard_map/all_gather | solution.py:186
  121.1 2.6 %collective-permute-start.2 = (bf16[192,2048]{1,0:T(8,128)(2,1)S(1)}, bf16[192,2048]{1,0:T(8,128)(2,1)S(1)}, u32[]{:S(2)}, u32[]{:S(2)}) collective-permute-start(bf16[192,2048]{1,0:T(8,128)(2,1)S(1)} %all_gather.11.near), channel_id=1, source_target_pairs={{0,48},{1,49},{2,50},{3,51},{4,52},{5,53},{6,54},{7,55},{8,56},{9,... | collective-permute-start | bytes 2359304 | tf_op jit(solution)/shard_map/ppermute | solution.py:188
  123.8 4.4 %collective-permute-start.1 = (bf16[192,2048]{1,0:T(8,128)(2,1)S(1)}, bf16[192,2048]{1,0:T(8,128)(2,1)S(1)}, u32[]{:S(2)}, u32[]{:S(2)}) collective-permute-start(bf16[192,2048]{1,0:T(8,128)(2,1)S(1)} %all_gather.11.near), channel_id=1, source_target_pairs={{0,16},{1,17},{2,18},{3,19},{4,20},{5,21},{6,22},{7,23},{8,24},{9,... | collective-permute-start | bytes 2359304 | tf_op jit(solution)/shard_map/ppermute | solution.py:187
  128.2 11.0 %collective-permute-done.2.right = bf16[192,2048]{1,0:T(8,128)(2,1)S(1)} collective-permute-done((bf16[192,2048]{1,0:T(8,128)(2,1)S(1)}, bf16[192,2048]{1,0:T(8,128)(2,1)S(1)}, u32[]{:S(2)}, u32[]{:S(2)}) %collective-permute-start.2) | collective-permute-done | bytes 786464 | tf_op jit(solution)/shard_map/ppermute | solution.py:188
  139.2 0.0 copy-start.4
  139.2 0.9 slice.13
  140.0 1.9 collective-permute-start.4
  142.0 0.0 collective-permute-done.1.left
  142.0 0.0 copy-done.4
  142.0 0.0 copy-start.6
  142.0 0.8 slice.12
  142.8 0.2 copy-done.6
  143.0 5.1 %collective-permute-start.3 = (bf16[96,2048]{1,0:T(8,128)(2,1)}, bf16[96,2048]{1,0:T(8,128)(2,1)}, u32[]{:S(2)}, u32[]{:S(2)}) collective-permute-start(bf16[96,2048]{1,0:T(8,128)(2,1)} %slice.12), channel_id=1, source_target_pairs={{0,16},{1,17},{2,18},{3,19},{4,20},{5,21},{6,22},{7,23},{8,24},{9,... | collective-permute-start | bytes 1179656 | tf_op jit(solution)/shard_map/ppermute | solution.py:190
  148.2 0.1 pad_add_fusion.where
  148.3 0.0 all-to-all-done.arrived
  148.3 3.3 %place.1.dense = bf16[2048,512]{1,0:T(8,128)(2,1)S(1)} custom-call(s32[64,2]{1,0:T(8,128)S(1)} %bitcast.16, bf16[64,144,128]{2,1,0:T(8,128)(2,1)S(1)} %all-to-all-done.arrived), custom_call_target="tpu_custom_call" | custom-call | bytes 4194304 | tf_op jit(solution)/shard_map/place/pallas_call | solution.py:108
  151.6 0.0 copy-start.1
  151.6 1.3 copy-done.1
  153.0 0.0 collective-permute-done.4.far1
  153.0 0.7 collective-permute-done.3.far0
  153.7 0.0 all-gather.2.cloned.1.call-done
  153.7 0.0 copy-start.2
  153.7 1.6 copy-done.2
  155.3 0.0 copy-start.5
  155.3 1.1 copy-done.5
  156.5 0.0 copy-start.7
  156.5 1.1 copy-done.7
  157.6 0.0 copy-start.8
  157.6 1.9 copy-done.8
  159.5 5.5 %contract.1 = (f32[768,512]{1,0:T(8,128)S(1)}, f32[768,512]{1,0:T(8,128)S(1)}) custom-call(s32[3]{0:T(128)S(1)} %pad_add_fusion.where, bf16[8,96,2048]{2,1,0:T(8,128)(2,1)S(1)} %bitcast.17, bf16[192,2048]{1,0:T(8,128)(2,1)S(1)} %all_gather.11.near, bf16[192,2048]{1,0:T(8,128)(2,1)S(1)} %copy-done.7, bf16[192,2048]{1,0:T(8,128)(2,1)S(1)} %copy-done.5, ...), custom_call_target="tpu_custom_call" | custom-call | flops 3221225472 | bytes 12582912 | tf_op jit(solution)/shard_map/contract/pallas_call | solution.py:154
  165.0 1.9 collective-permute-start.5
  166.9 3.4 %collective-permute-done.5 = f32[768,512]{1,0:T(8,128)S(1)} collective-permute-done((f32[768,512]{1,0:T(8,128)S(1)}, f32[768,512]{1,0:T(8,128)S(1)}, u32[]{:S(2)}, u32[]{:S(2)}) %collective-permute-start.5) | collective-permute-done | bytes 1572896 | tf_op jit(solution)/shard_map/ppermute | solution.py:196
  170.3 1.5 add.24
  171.8 0.0 reduce-scatter.2.cloned.1.call-update
  171.8 83.0 %reduce-scatter.2.cloned.1.call-done = f32[128,512]{1,0:T(8,128)} async-done(((f32[768,512]{1,0:T(8,128)}), f32[128,512]{1,0:T(8,128)}) %reduce-scatter.2.cloned.1.call-update) | async-done | bytes 262160 | tf_op jit(solution)/shard_map/reduce_scatter | solution.py:197
  254.9 1.6 convert_element_type.10
  (1 shorter events, 0.0 us)
Async XLA Ops:
  7.2 1.2 copy-start.3
  10.7 1.4 copy-start
  12.2 23.7 %copy-start.9 = (bf16[2048,24]{0,1:T(8,128)(2,1)S(1)}, bf16[2048,24]{0,1:T(8,128)(2,1)}, u32[]{:S(2)}) copy-start(bf16[2048,24]{0,1:T(8,128)(2,1)} %param.9) | copy-start | bytes 294916
  12.2 136.1 %all-to-all-start = ((bf16[64,144,128]{2,1,0:T(8,128)(2,1)}), bf16[64,144,128]{2,1,0:T(8,128)(2,1)S(1)}, u32[]{:S(2)}, u32[]{:S(2)}) async-start(bf16[64,144,128]{2,1,0:T(8,128)(2,1)} %copy-done), calls=%async_computation | async-start | bytes 4718592 | tf_op jit(solution)/shard_map/all_to_all | solution.py:179
  35.8 118.0 %all-gather.2.cloned.1.call-start = ((), (), s32[]{:S(2)}) async-start(), calls=%async_computation.2 | async-start | bytes 3538944 | tf_op jit(solution)/shard_map/all_gather | solution.py:183
  50.7 204.1 %reduce-scatter.2.cloned.1.call-start = ((), (), s32[]{:S(2)}) async-start(), calls=%async_computation.3 | async-start | bytes 1835008 | tf_op jit(solution)/shard_map/reduce_scatter | solution.py:197
  50.8 22.9 %collective-permute-start = (bf16[24,2048]{1,0:T(8,128)(2,1)S(1)}, bf16[24,2048]{1,0:T(8,128)(2,1)S(1)}, u32[]{:S(2)}, u32[]{:S(2)}) collective-permute-start(bf16[24,2048]{1,0:T(8,128)(2,1)S(1)} %bitcast.19), channel_id=1, source_target_pairs={{0,8},{1,9},{2,10},{3,11},{4,12},{5,13},{6,14},{7,15},{8,0},{9,1},... | collective-permute-start | bytes 294920 | tf_op jit(solution)/shard_map/ppermute | solution.py:180
  121.1 18.0 %collective-permute-start.2 = (bf16[192,2048]{1,0:T(8,128)(2,1)S(1)}, bf16[192,2048]{1,0:T(8,128)(2,1)S(1)}, u32[]{:S(2)}, u32[]{:S(2)}) collective-permute-start(bf16[192,2048]{1,0:T(8,128)(2,1)S(1)} %all_gather.11.near), channel_id=1, source_target_pairs={{0,48},{1,49},{2,50},{3,51},{4,52},{5,53},{6,54},{7,55},{8,56},{9,... | collective-permute-start | bytes 2359304 | tf_op jit(solution)/shard_map/ppermute | solution.py:188
  123.8 18.2 %collective-permute-start.1 = (bf16[192,2048]{1,0:T(8,128)(2,1)S(1)}, bf16[192,2048]{1,0:T(8,128)(2,1)S(1)}, u32[]{:S(2)}, u32[]{:S(2)}) collective-permute-start(bf16[192,2048]{1,0:T(8,128)(2,1)S(1)} %all_gather.11.near), channel_id=1, source_target_pairs={{0,16},{1,17},{2,18},{3,19},{4,20},{5,21},{6,22},{7,23},{8,24},{9,... | collective-permute-start | bytes 2359304 | tf_op jit(solution)/shard_map/ppermute | solution.py:187
  139.2 2.8 %copy-start.4 = (bf16[192,2048]{1,0:T(8,128)(2,1)}, bf16[192,2048]{1,0:T(8,128)(2,1)S(1)}, u32[]{:S(2)}) copy-start(bf16[192,2048]{1,0:T(8,128)(2,1)S(1)} %collective-permute-done.2.right) | copy-start | bytes 2359300
  140.0 12.9 %collective-permute-start.4 = (bf16[96,2048]{1,0:T(8,128)(2,1)}, bf16[96,2048]{1,0:T(8,128)(2,1)S(1)}, u32[]{:S(2)}, u32[]{:S(2)}) collective-permute-start(bf16[96,2048]{1,0:T(8,128)(2,1)} %slice.13), channel_id=1, source_target_pairs={{0,48},{1,49},{2,50},{3,51},{4,52},{5,53},{6,54},{7,55},{8,56},{9,... | collective-permute-start | bytes 1179656 | tf_op jit(solution)/shard_map/ppermute | solution.py:191
  142.0 1.0 copy-start.6
  143.0 10.7 %collective-permute-start.3 = (bf16[96,2048]{1,0:T(8,128)(2,1)}, bf16[96,2048]{1,0:T(8,128)(2,1)}, u32[]{:S(2)}, u32[]{:S(2)}) collective-permute-start(bf16[96,2048]{1,0:T(8,128)(2,1)} %slice.12), channel_id=1, source_target_pairs={{0,16},{1,17},{2,18},{3,19},{4,20},{5,21},{6,22},{7,23},{8,24},{9,... | collective-permute-start | bytes 1179656 | tf_op jit(solution)/shard_map/ppermute | solution.py:190
  151.6 1.4 copy-start.1
  153.7 1.6 copy-start.2
  155.3 1.1 copy-start.5
  156.5 1.1 copy-start.7
  157.6 1.9 copy-start.8
  165.0 5.3 %collective-permute-start.5 = (f32[768,512]{1,0:T(8,128)S(1)}, f32[768,512]{1,0:T(8,128)S(1)}, u32[]{:S(2)}, u32[]{:S(2)}) collective-permute-start(f32[768,512]{1,0:T(8,128)S(1)} %get-tuple-element.12), channel_id=1, source_target_pairs={{0,64},{64,0},{128,192},{192,128},{256,320},{320,256},{384,448},{4... | collective-permute-start | bytes 4718600 | tf_op jit(solution)/shard_map/ppermute | solution.py:196
Sparse Core Ops, SparseCore 0:
  50.8 76.1 all-gather.1
  171.9 82.8 reduce-scatter.1

commit v3 on v2

--- a/solution.py
+++ b/solution.py
@@ -9,6 +9,7 @@
 CAP = 2
 NX, NZH, NY = 4, 2, 8
 NZL, NCORE = 6, 2
+NEAR = NZL // 2
 N_COL = NX * NZH * NY
 LABEL_ROWS = 16
 CELLS = 128
@@ -24,9 +25,15 @@
     return (x * NZH + zh) * NY + y
 
 
-X_GROUPS = [[column(x, zh, y) for x in range(NX)] for zh in range(NZH) for y in range(NY)]
 Y_GROUPS = [[column(x, zh, y) for y in range(NY)] for x in range(NX) for zh in range(NZH)]
-ZL_GROUPS = [[zl * NCORE + core for zl in range(NZL)] for core in range(NCORE)]
+NEAR_GROUPS = [
+    [zl * NCORE + core for zl in range(half * NEAR, (half + 1) * NEAR)]
+    for half in range(NZL // NEAR)
+    for core in range(NCORE)
+]
+FAR_SWAP = [
+    (zl * NCORE + core, (zl + NEAR) % NZL * NCORE + core) for zl in range(NZL) for core in range(NCORE)
+]
 PLANE_SWAP = [
     (column(x, zh, y), column(x, 1 - zh, y)) for x in range(NX) for zh in range(NZH) for y in range(NY)
 ]
@@ -116,51 +123,71 @@
     )(labels, arrived)
 
 
-def contract_kernel(where, own, near, left, right, far0, far1, dense, keep, send, total, sem):
-    x, plane, core = where[0], where[1], where[2]
-    per = near.shape[0] // NY
+def contract_kernel(where, own, near, left, right, far0, far1, dense, keep, send, a, b, total, loads, stores):
+    x, plane, zl, core = where[0], where[1], where[2], where[3]
+    step = near.shape[0]
+    per = step // NY
     groups = OUT_ROWS // GROUP
+
+    parts = [(0, near, 0), (1, left, 0), (2, right, 0), (3, far0, 0), (3, far1, far0.shape[0])]
+    copies = []
+    for n, (slot, ref, at) in enumerate(parts):
+        copies.append(pltpu.make_async_copy(ref, b.at[pl.ds(slot * step + at, ref.shape[0])], loads.at[n]))
+    copies.append(pltpu.make_async_copy(own, a, loads.at[len(parts)]))
+    for copy in copies:
+        copy.start()
 
     def store(c, block):
         for i in range(per // GROUP):
             g = c * (per // GROUP) + i
             away = jnp.where(g // groups % NCORE == core, 0, 1)
-            row = pl.multiple_of((g // (groups * NCORE) * groups + g % groups) * GROUP, GROUP)
+            to = g // (groups * NCORE)
+            slot = to % NEAR * 2 + jnp.where(to // NEAR == zl // NEAR, 0, 1)
+            row = pl.multiple_of((slot * groups + g % groups) * GROUP, GROUP)
             total[away, pl.ds(row, GROUP), :] = block[i * GROUP : (i + 1) * GROUP]
 
-    half = NY // 2
-    for h in range(2):
-        a = own[h * half : (h + 1) * half].reshape(half * NX * per, own.shape[2])
-        product = jnp.dot(a, dense[...], preferred_element_type=jnp.float32)
-        for y in range(half):
-            for xx in range(NX):
-                at = (y * NX + xx) * per
-                store((xx * NZH + plane) * NY + h * half + y, product[at : at + per])
-    for by, parts in ((0, (near,)), (NX - 1, (left,)), (1, (right,)), (2, (far0, far1))):
-        a = parts[0][...] if len(parts) == 1 else jnp.concatenate([p[...] for p in parts], axis=0)
-        product = jnp.dot(a, dense[...], preferred_element_type=jnp.float32)
-        for y in range(NY):
-            store(((x + by) % NX * NZH + 1 - plane) * NY + y, product[y * per : (y + 1) * per])
-    copies = [pltpu.make_async_copy(total.at[k], ref, sem.at[k]) for k, ref in enumerate((keep, send))]
-    for copy in copies:
+    def multiply(rows, columns):
+        product = jnp.dot(rows, dense[...], preferred_element_type=jnp.float32)
+        for n, c in enumerate(columns):
+            store(c, product[n * per : (n + 1) * per])
+
+    def at_column(by, side, y):
+        return ((x + by) % NX * NZH + side) * NY + y
+
+    for copy in copies[:3]:
+        copy.wait()
+    multiply(b[: 2 * step, :], [at_column(by, 1 - plane, y) for by in (0, NX - 1) for y in range(NY)])
+    for copy in copies[3:5]:
+        copy.wait()
+    multiply(b[2 * step :, :], [at_column(by, 1 - plane, y) for by in (1, 2) for y in range(NY)])
+    copies[5].wait()
+    half = max(NY // 2, 1)
+    for y0 in range(0, NY, half):
+        rows = a[y0 * NX * per : (y0 + half) * NX * per, :]
+        multiply(rows, [at_column(by, plane, y0 + y) for y in range(half) for by in (0, NX - 1, 1, 2)])
+    out = [pltpu.make_async_copy(total.at[k], ref, stores.at[k]) for k, ref in enumerate((keep, send))]
+    for copy in out:
         copy.start()
-    for copy in copies:
+    for copy in out:
         copy.wait()
 
 
 def contract(where, own, near, left, right, far0, far1, dense):
-    occ = own.shape[0] * own.shape[1] * NZH
+    occ = own.shape[0] * NZH
     shape = jax.ShapeDtypeStruct((occ // NCORE, dense.shape[1]), jnp.float32)
     return pl.pallas_call(
         contract_kernel,
         out_shape=(shape, shape),
-        in_specs=[SMEM] + [VMEM] * 7,
+        in_specs=[SMEM] + [ANY] * 6 + [VMEM],
         out_specs=(ANY, ANY),
         scratch_shapes=[
+            pltpu.VMEM(own.shape, own.dtype),
+            pltpu.VMEM(own.shape, own.dtype),
             pltpu.VMEM((NCORE, *shape.shape), jnp.float32),
+            pltpu.SemaphoreType.DMA((6,)),
             pltpu.SemaphoreType.DMA((NCORE,)),
         ],
-        compiler_params=pltpu.CompilerParams(vmem_limit_bytes=40 << 20),
+        compiler_params=pltpu.CompilerParams(vmem_limit_bytes=56 << 20),
         cost_estimate=pl.CostEstimate(
             flops=2 * occ * dense.shape[0] * dense.shape[1], bytes_accessed=12 << 20, transcendentals=0
         ),
@@ -171,18 +198,18 @@
 def per_device(tiles, dest_col, mu_block, col_block, coeff):
     held, rows, cols = tiles.shape[2:]
     mu_rows, per = coeff.shape
-    here = lax.axis_index("col")
-    where = jnp.stack([here // (NZH * NY), here // NY % NZH, lax.axis_index("row") % NCORE]).astype(jnp.int32)
+    here, row = lax.axis_index("col"), lax.axis_index("row")
+    where = jnp.stack([here // (NZH * NY), here // NY % NZH, row // NCORE, row % NCORE]).astype(jnp.int32)
+
+    mine = coeff.T
+    theirs = lax.ppermute(mine, "col", PLANE_SWAP)
+    own = jnp.concatenate([mine] + [lax.ppermute(mine, "col", x_shift(by)) for by in (1, -1, 2)], axis=0)
     route = dest_col.reshape(held) * CELLS + mu_block.reshape(held) * CB + col_block.reshape(held)
     outgoing = pack(tiles.reshape(held, rows, cols), route)
-    outgoing, mine = lax.optimization_barrier((outgoing, coeff.T))
+    outgoing, theirs, own = lax.optimization_barrier((outgoing, theirs, own))
     arrived = lax.all_to_all(outgoing, "col", split_axis=0, concat_axis=0, tiled=True)
-    theirs = lax.ppermute(mine, "col", PLANE_SWAP)
-
-    own = lax.all_gather(mine, "col", axis=0, tiled=True, axis_index_groups=X_GROUPS)
+
     own = lax.all_gather(own, "col", axis=0, tiled=True, axis_index_groups=Y_GROUPS)
-    own = own.reshape(NY, NX * per, mu_rows)
-
     near = lax.all_gather(theirs, "col", axis=0, tiled=True, axis_index_groups=Y_GROUPS)
     left = lax.ppermute(near, "col", x_shift(1))
     right = lax.ppermute(near, "col", x_shift(-1))
@@ -194,7 +221,11 @@
     dense = place(labels, arrived, mu_rows)
     keep, send = contract(where, own, near, left, right, far0, far1, dense)
     share = keep + lax.ppermute(send, "row", CORE_SWAP)
-    result = lax.psum_scatter(share, "row", scatter_dimension=0, tiled=True, axis_index_groups=ZL_GROUPS)
+    share = lax.all_to_all(
+        share.reshape(NEAR, 2 * OUT_ROWS, -1), "row", split_axis=0, concat_axis=0, tiled=True, axis_index_groups=NEAR_GROUPS
+    )
+    away = jnp.sum(share[:, OUT_ROWS:], axis=0)
+    result = jnp.sum(share[:, :OUT_ROWS], axis=0) + lax.ppermute(away, "row", FAR_SWAP)
     return result.astype(jnp.bfloat16)
 
 

time: 264 us -> 254 us (0.962)
  waiting for transfers between devices: 104 us -> 36.5 us
  blocking collectives: 62.3 us -> 113 us
  local copies, waits for them, and re-layouts: 11.7 us -> 5.08 us
  Pallas kernels: 11.1 us -> 17.4 us
  starting transfers between devices: 56.7 us -> 61.3 us
    reduce_scatter x1 -> x0, waiting for transfers between devices: 83 us -> none  [per_device(): lax.psum_scatter(share, 'row', scatter_dimension=0, tiled=True, axis_inde...]
    all_gather x1, blocking collectives: 47.4 us -> 84.6 us  [per_device(): lax.all_gather(theirs, 'col', axis=0, tiled=True, axis_index_groups=Y_GRO...]
    all_to_all x0 -> x1, blocking collectives: none -> 28.4 us  [per_device(): lax.all_to_all(share.reshape(NEAR, 2 * OUT_ROWS, -1), 'row', split_axis=0...]
    ppermute x0 -> x4, waiting for transfers between devices: none -> 20.2 us  [the longest x1 20.2 us: per_device(): lax.ppermute(away, 'row', FAR_SWAP)]
    ppermute x0 -> x4, starting transfers between devices: none -> 18 us  [the longest x3 16.1 us: per_device(): lax.ppermute(mine, 'col', x_shift(by))]
    all_gather x1 -> x0, blocking collectives: 14.9 us -> none  [per_device(): lax.all_gather(mine, 'col', axis=0, tiled=True, axis_index_groups=X_GROUPS)]
    ppermute x1, starting transfers between devices: 17 us -> 9.42 us  [per_device(): theirs = lax.ppermute(mine, 'col', PLANE_SWAP)]
    pallas_call x1, Pallas kernels: 5.49 us -> 11.8 us  [contract(): pl.pallas_call(contract_kernel, out_shape=(shape, shape), in_specs=[SMEM]...]
  transfers between devices with their start and end apart: 9 -> 12, of which waited for: 5 -> 4; matrix products, arithmetic and copies ran while one was open for 1% -> 1% of each run, Pallas kernels for 1% -> 2%
where the time goes in v3:
time: 254 us; the launch traced here: 251 us
  blocking collectives  113 us (44%)
  starting transfers between devices  61.3 us (24%)
  waiting for transfers between devices  36.5 us (14%)
  Pallas kernels  17.4 us (7%)
  between operations  13.6 us (5%)
  local copies, waits for them, and re-layouts  5.08 us (2%)
  other arithmetic  4.68 us (2%)
    all_gather x1, blocking collectives, per_device(): lax.all_gather(theirs, 'col', axis=0, tiled=True, axis_index_groups=Y_GRO...  84.6 us
    all_to_all x1, blocking collectives, per_device(): lax.all_to_all(share.reshape(NEAR, 2 * OUT_ROWS, -1), 'row', split_axis=0...  28.4 us
    ppermute x1, waiting for transfers between devices, per_device(): lax.ppermute(away, 'row', FAR_SWAP)  20.2 us
    all_to_all x1, starting transfers between devices, per_device(): lax.all_to_all(outgoing, 'col', split_axis=0, concat_axis=0, tiled=True)  17.4 us
    ppermute x3, starting transfers between devices, per_device(): lax.ppermute(mine, 'col', x_shift(by))  16.1 us
    ppermute x1, waiting for transfers between devices, per_device(): right = lax.ppermute(near, 'col', x_shift(-1))  11.8 us
    pallas_call x1, Pallas kernels, contract(): pl.pallas_call(contract_kernel, out_shape=(shape, shape), in_specs=[SMEM]...  11.8 us
    ppermute x1, starting transfers between devices, per_device(): theirs = lax.ppermute(mine, 'col', PLANE_SWAP)  9.42 us
  transfers between devices with their start and end apart: 12, of which 4 were waited for; matrix products, arithmetic and copies ran while one was open for 1% of the time, Pallas kernels for 2%

profile of v3, /device:TPU:6, one launch (start us, length us, event | category | flops | bytes accessed | tf_op | source)
XLA Modules:
  0.0 251.5 jit_solution(342675170684498137)
XLA Ops:
  6.5 3.3 %collective-permute-start.3 = (bf16[24,2048]{1,0:T(8,128)(2,1)}, bf16[24,2048]{1,0:T(8,128)(2,1)S(1)}, u32[]{:S(2)}, u32[]{:S(2)}) collective-permute-start(bf16[24,2048]{1,0:T(8,128)(2,1)} %bitcast.19), channel_id=1, source_target_pairs={{0,32},{1,33},{2,34},{3,35},{4,36},{5,37},{6,38},{7,39},{8,40},{9,... | collective-permute-start | bytes 294920 | tf_op jit(solution)/shard_map/ppermute | solution.py:206
  9.8 10.9 %collective-permute-start.2 = (bf16[24,2048]{1,0:T(8,128)(2,1)}, bf16[24,2048]{1,0:T(8,128)(2,1)S(1)}, u32[]{:S(2)}, u32[]{:S(2)}) collective-permute-start(bf16[24,2048]{1,0:T(8,128)(2,1)} %bitcast.20), channel_id=1, source_target_pairs={{0,48},{1,49},{2,50},{3,51},{4,52},{5,53},{6,54},{7,55},{8,56},{9,... | collective-permute-start | bytes 294920 | tf_op jit(solution)/shard_map/ppermute | solution.py:206
  20.7 1.9 collective-permute-start.1
  22.6 9.4 %collective-permute-start = (bf16[24,2048]{1,0:T(8,128)(2,1)}, bf16[24,2048]{1,0:T(8,128)(2,1)S(1)}, u32[]{:S(2)}, u32[]{:S(2)}) collective-permute-start(bf16[24,2048]{1,0:T(8,128)(2,1)} %bitcast.22), channel_id=1, source_target_pairs={{0,8},{1,9},{2,10},{3,11},{4,12},{5,13},{6,14},{7,15},{8,0},{9,1},... | collective-permute-start | bytes 294920 | tf_op jit(solution)/shard_map/ppermute | solution.py:205
  32.1 0.7 bitcast_add_fusion.route
  32.8 0.0 copy-start.2
  32.8 1.2 copy-done.2
  34.0 0.0 copy-start.6
  34.0 2.3 pack.1
  36.3 0.0 copy-start
  36.3 1.4 copy-done
  37.7 0.0 collective-permute-done.3
  37.7 0.0 collective-permute-done.2
  37.7 0.0 collective-permute-done.1
  37.7 0.0 copy-done.6
  37.7 0.8 pad_maximum_fusion
  38.5 0.0 collective-permute-done
  38.5 17.4 %all-to-all-start = ((bf16[64,144,128]{2,1,0:T(8,128)(2,1)}), bf16[64,144,128]{2,1,0:T(8,128)(2,1)S(1)}, u32[]{:S(2)}, u32[]{:S(2)}) async-start(bf16[64,144,128]{2,1,0:T(8,128)(2,1)} %copy-done), calls=%async_computation | async-start | bytes 4718592 | tf_op jit(solution)/shard_map/all_to_all | solution.py:210
  56.0 0.0 all-gather.2.cloned.1.call-start
  56.0 0.7 all-gather.2.cloned.1.call-update
  56.7 84.6 %all_gather.7.near = bf16[192,2048]{1,0:T(8,128)(2,1)S(1)} all-gather(bf16[24,2048]{1,0:T(8,128)(2,1)S(1)} %collective-permute-done), channel_id=1, replica_groups={{0,1,2,3,4,5,6,7},{8,9,10,11,12,13,14,15},{16,17,18,19,20,21,22,23},{24..., dimensions={0}, use_global_device_ids=true | all-gather | bytes 884736 | tf_op jit(solution)/shard_map/all_gather | solution.py:213
  141.2 0.0 copy-start.3
  141.2 2.6 %collective-permute-start.5 = (bf16[192,2048]{1,0:T(8,128)(2,1)S(1)}, bf16[192,2048]{1,0:T(8,128)(2,1)S(1)}, u32[]{:S(2)}, u32[]{:S(2)}) collective-permute-start(bf16[192,2048]{1,0:T(8,128)(2,1)S(1)} %all_gather.7.near), channel_id=1, source_target_pairs={{0,48},{1,49},{2,50},{3,51},{4,52},{5,53},{6,54},{7,55},{8,56},{9,... | collective-permute-start | bytes 2359304 | tf_op jit(solution)/shard_map/ppermute | solution.py:215
  143.9 4.4 %collective-permute-start.4 = (bf16[192,2048]{1,0:T(8,128)(2,1)S(1)}, bf16[192,2048]{1,0:T(8,128)(2,1)S(1)}, u32[]{:S(2)}, u32[]{:S(2)}) collective-permute-start(bf16[192,2048]{1,0:T(8,128)(2,1)S(1)} %all_gather.7.near), channel_id=1, source_target_pairs={{0,16},{1,17},{2,18},{3,19},{4,20},{5,21},{6,22},{7,23},{8,24},{9,... | collective-permute-start | bytes 2359304 | tf_op jit(solution)/shard_map/ppermute | solution.py:214
  148.3 11.8 %collective-permute-done.5.right = bf16[192,2048]{1,0:T(8,128)(2,1)S(1)} collective-permute-done((bf16[192,2048]{1,0:T(8,128)(2,1)S(1)}, bf16[192,2048]{1,0:T(8,128)(2,1)S(1)}, u32[]{:S(2)}, u32[]{:S(2)}) %collective-permute-start.5) | collective-permute-done | bytes 786464 | tf_op jit(solution)/shard_map/ppermute | solution.py:215
  160.1 0.0 copy-start.4
  160.2 1.9 collective-permute-start.7
  162.1 0.0 collective-permute-done.4.left
  162.1 0.0 copy-done.4
  162.1 0.0 copy-start.5
  162.1 0.8 slice.20
  163.0 0.2 copy-done.5
  163.1 5.5 %collective-permute-start.6 = (bf16[96,2048]{1,0:T(8,128)(2,1)}, bf16[96,2048]{1,0:T(8,128)(2,1)}, u32[]{:S(2)}, u32[]{:S(2)}) collective-permute-start(bf16[96,2048]{1,0:T(8,128)(2,1)} %slice.20), channel_id=1, source_target_pairs={{0,16},{1,17},{2,18},{3,19},{4,20},{5,21},{6,22},{7,23},{8,24},{9,... | collective-permute-start | bytes 1179656 | tf_op jit(solution)/shard_map/ppermute | solution.py:217
  168.7 0.6 pad_add_fusion.where
  169.3 0.0 all-to-all-done.arrived
  169.3 3.3 %place.1.dense = bf16[2048,512]{1,0:T(8,128)(2,1)S(1)} custom-call(s32[64,2]{1,0:T(8,128)S(1)} %bitcast.17, bf16[64,144,128]{2,1,0:T(8,128)(2,1)S(1)} %all-to-all-done.arrived), custom_call_target="tpu_custom_call" | custom-call | bytes 4194304 | tf_op jit(solution)/shard_map/place/pallas_call | solution.py:115
  172.6 0.0 copy-done.3
  172.6 0.0 copy-start.1
  172.7 1.4 copy-done.1
  174.0 0.0 collective-permute-done.7.far1
  174.0 0.2 collective-permute-done.6.far0
  174.2 0.0 all-gather.2.cloned.1.call-done.own
  174.2 11.8 %contract.1 = (f32[768,512]{1,0:T(8,128)}, f32[768,512]{1,0:T(8,128)}) custom-call(s32[4]{0:T(128)} %pad_add_fusion.where, bf16[768,2048]{1,0:T(8,128)(2,1)} %all-gather.2.cloned.1.call-done.own, bf16[192,2048]{1,0:T(8,128)(2,1)} %copy-done.3, bf16[192,2048]{1,0:T(8,128)(2,1)} %copy-done.5, bf16[192,2048]{1,0:T(8,128)(2,1)} %copy-done.4, ...), custom_call_target="tpu_custom_call" | custom-call | flops 3221225472 | bytes 12582912 | tf_op jit(solution)/shard_map/contract/pallas_call | solution.py:178
  186.0 1.9 collective-permute-start.8
  187.9 3.6 %collective-permute-done.8 = f32[768,512]{1,0:T(8,128)S(1)} collective-permute-done((f32[768,512]{1,0:T(8,128)}, f32[768,512]{1,0:T(8,128)S(1)}, u32[]{:S(2)}, u32[]{:S(2)}) %collective-permute-start.8) | collective-permute-done | bytes 1572896 | tf_op jit(solution)/shard_map/ppermute | solution.py:223
  191.5 1.8 add.26
  193.3 28.4 %all_to_all.10 = f32[3,256,512]{2,1,0:T(8,128)S(1)} all-to-all(f32[3,256,512]{2,1,0:T(8,128)S(1)} %bitcast.18), channel_id=1, replica_groups={{0,128,256},{64,192,320},{384,512,640},{448,576,704},{1,129,257},{65,19..., dimensions={0} | all-to-all | bytes 3145728 | tf_op jit(solution)/shard_map/all_to_all | solution.py:224
  221.7 0.1 slice_reduce_fusion
  221.9 1.9 collective-permute-start.9
  223.8 20.2 %collective-permute-done.9 = f32[128,512]{1,0:T(8,128)S(1)} collective-permute-done((f32[128,512]{1,0:T(8,128)S(1)}, f32[128,512]{1,0:T(8,128)S(1)}, u32[]{:S(2)}, u32[]{:S(2)}) %collective-permute-start.9) | collective-permute-done | bytes 262176 | tf_op jit(solution)/shard_map/ppermute | solution.py:228
  244.0 0.7 add_convert_fusion
  (2 shorter events, 0.1 us)
Async XLA Ops:
  6.5 31.2 %collective-permute-start.3 = (bf16[24,2048]{1,0:T(8,128)(2,1)}, bf16[24,2048]{1,0:T(8,128)(2,1)S(1)}, u32[]{:S(2)}, u32[]{:S(2)}) collective-permute-start(bf16[24,2048]{1,0:T(8,128)(2,1)} %bitcast.19), channel_id=1, source_target_pairs={{0,32},{1,33},{2,34},{3,35},{4,36},{5,37},{6,38},{7,39},{8,40},{9,... | collective-permute-start | bytes 294920 | tf_op jit(solution)/shard_map/ppermute | solution.py:206
  9.8 27.9 %collective-permute-start.2 = (bf16[24,2048]{1,0:T(8,128)(2,1)}, bf16[24,2048]{1,0:T(8,128)(2,1)S(1)}, u32[]{:S(2)}, u32[]{:S(2)}) collective-permute-start(bf16[24,2048]{1,0:T(8,128)(2,1)} %bitcast.20), channel_id=1, source_target_pairs={{0,48},{1,49},{2,50},{3,51},{4,52},{5,53},{6,54},{7,55},{8,56},{9,... | collective-permute-start | bytes 294920 | tf_op jit(solution)/shard_map/ppermute | solution.py:206
  20.7 17.0 %collective-permute-start.1 = (bf16[24,2048]{1,0:T(8,128)(2,1)}, bf16[24,2048]{1,0:T(8,128)(2,1)S(1)}, u32[]{:S(2)}, u32[]{:S(2)}) collective-permute-start(bf16[24,2048]{1,0:T(8,128)(2,1)} %bitcast.21), channel_id=1, source_target_pairs={{0,16},{1,17},{2,18},{3,19},{4,20},{5,21},{6,22},{7,23},{8,24},{9,... | collective-permute-start | bytes 294920 | tf_op jit(solution)/shard_map/ppermute | solution.py:206
  22.6 15.9 %collective-permute-start = (bf16[24,2048]{1,0:T(8,128)(2,1)}, bf16[24,2048]{1,0:T(8,128)(2,1)S(1)}, u32[]{:S(2)}, u32[]{:S(2)}) collective-permute-start(bf16[24,2048]{1,0:T(8,128)(2,1)} %bitcast.22), channel_id=1, source_target_pairs={{0,8},{1,9},{2,10},{3,11},{4,12},{5,13},{6,14},{7,15},{8,0},{9,1},... | collective-permute-start | bytes 294920 | tf_op jit(solution)/shard_map/ppermute | solution.py:205
  32.8 1.2 copy-start.2
  34.0 3.7 %copy-start.6 = (bf16[2048,24]{0,1:T(8,128)(2,1)S(1)}, bf16[2048,24]{0,1:T(8,128)(2,1)}, u32[]{:S(2)}) copy-start(bf16[2048,24]{0,1:T(8,128)(2,1)} %param.9) | copy-start | bytes 294916
  36.3 1.5 copy-start
  38.5 130.8 %all-to-all-start = ((bf16[64,144,128]{2,1,0:T(8,128)(2,1)}), bf16[64,144,128]{2,1,0:T(8,128)(2,1)S(1)}, u32[]{:S(2)}, u32[]{:S(2)}) async-start(bf16[64,144,128]{2,1,0:T(8,128)(2,1)} %copy-done), calls=%async_computation | async-start | bytes 4718592 | tf_op jit(solution)/shard_map/all_to_all | solution.py:210
  56.0 118.3 %all-gather.2.cloned.1.call-start = ((), (), s32[]{:S(2)}) async-start(), calls=%async_computation.2 | async-start | bytes 3538944 | tf_op jit(solution)/shard_map/all_gather | solution.py:212
  141.2 31.4 %copy-start.3 = (bf16[192,2048]{1,0:T(8,128)(2,1)}, bf16[192,2048]{1,0:T(8,128)(2,1)S(1)}, u32[]{:S(2)}) copy-start(bf16[192,2048]{1,0:T(8,128)(2,1)S(1)} %all_gather.7.near) | copy-start | bytes 2359300
  141.2 18.9 %collective-permute-start.5 = (bf16[192,2048]{1,0:T(8,128)(2,1)S(1)}, bf16[192,2048]{1,0:T(8,128)(2,1)S(1)}, u32[]{:S(2)}, u32[]{:S(2)}) collective-permute-start(bf16[192,2048]{1,0:T(8,128)(2,1)S(1)} %all_gather.7.near), channel_id=1, source_target_pairs={{0,48},{1,49},{2,50},{3,51},{4,52},{5,53},{6,54},{7,55},{8,56},{9,... | collective-permute-start | bytes 2359304 | tf_op jit(solution)/shard_map/ppermute | solution.py:215
  143.9 18.2 %collective-permute-start.4 = (bf16[192,2048]{1,0:T(8,128)(2,1)S(1)}, bf16[192,2048]{1,0:T(8,128)(2,1)S(1)}, u32[]{:S(2)}, u32[]{:S(2)}) collective-permute-start(bf16[192,2048]{1,0:T(8,128)(2,1)S(1)} %all_gather.7.near), channel_id=1, source_target_pairs={{0,16},{1,17},{2,18},{3,19},{4,20},{5,21},{6,22},{7,23},{8,24},{9,... | collective-permute-start | bytes 2359304 | tf_op jit(solution)/shard_map/ppermute | solution.py:214
  160.1 2.0 copy-start.4
  160.2 13.9 %collective-permute-start.7 = (bf16[96,2048]{1,0:T(8,128)(2,1)S(1)}, bf16[96,2048]{1,0:T(8,128)(2,1)}, u32[]{:S(2)}, u32[]{:S(2)}) collective-permute-start(bf16[96,2048]{1,0:T(8,128)(2,1)S(1)} %slice.21), channel_id=1, source_target_pairs={{0,48},{1,49},{2,50},{3,51},{4,52},{5,53},{6,54},{7,55},{8,56},{9,... | collective-permute-start | bytes 1179656 | tf_op jit(solution)/shard_map/ppermute | solution.py:218
  162.1 1.0 copy-start.5
  163.1 11.1 %collective-permute-start.6 = (bf16[96,2048]{1,0:T(8,128)(2,1)}, bf16[96,2048]{1,0:T(8,128)(2,1)}, u32[]{:S(2)}, u32[]{:S(2)}) collective-permute-start(bf16[96,2048]{1,0:T(8,128)(2,1)} %slice.20), channel_id=1, source_target_pairs={{0,16},{1,17},{2,18},{3,19},{4,20},{5,21},{6,22},{7,23},{8,24},{9,... | collective-permute-start | bytes 1179656 | tf_op jit(solution)/shard_map/ppermute | solution.py:217
  172.6 1.4 copy-start.1
  186.0 5.5 %collective-permute-start.8 = (f32[768,512]{1,0:T(8,128)}, f32[768,512]{1,0:T(8,128)S(1)}, u32[]{:S(2)}, u32[]{:S(2)}) collective-permute-start(f32[768,512]{1,0:T(8,128)} %get-tuple-element.14), channel_id=1, source_target_pairs={{0,64},{64,0},{128,192},{192,128},{256,320},{320,256},{384,448},{4... | collective-permute-start | bytes 4718600 | tf_op jit(solution)/shard_map/ppermute | solution.py:223
  221.9 22.1 %collective-permute-start.9 = (f32[128,512]{1,0:T(8,128)S(1)}, f32[128,512]{1,0:T(8,128)S(1)}, u32[]{:S(2)}, u32[]{:S(2)}) collective-permute-start(f32[128,512]{1,0:T(8,128)S(1)} %get-tuple-element.15), channel_id=1, source_target_pairs={{0,384},{64,448},{128,512},{192,576},{256,640},{320,704},{384,0},{... | collective-permute-start | bytes 786440 | tf_op jit(solution)/shard_map/ppermute | solution.py:228
Sparse Core Ops, SparseCore 0:
  59.2 82.8 all-gather.1

commit v4 on v3

--- a/solution.py
+++ b/solution.py
@@ -15,6 +15,7 @@
 CELLS = 128
 GROUP = 8
 OUT_ROWS = 128
+WIDE = 32
 
 
 def device(zl, core, x, zh, y):
@@ -123,17 +124,16 @@
     )(labels, arrived)
 
 
-def contract_kernel(where, own, near, left, right, far0, far1, dense, keep, send, a, b, total, loads, stores):
+def contract_kernel(where, near, left, right, far0, far1, dense, keep, send, a, total, loads, stores):
     x, plane, zl, core = where[0], where[1], where[2], where[3]
     step = near.shape[0]
-    per = step // NY
+    per = step // (NZH * NY)
     groups = OUT_ROWS // GROUP
 
-    parts = [(0, near, 0), (1, left, 0), (2, right, 0), (3, far0, 0), (3, far1, far0.shape[0])]
-    copies = []
-    for n, (slot, ref, at) in enumerate(parts):
-        copies.append(pltpu.make_async_copy(ref, b.at[pl.ds(slot * step + at, ref.shape[0])], loads.at[n]))
-    copies.append(pltpu.make_async_copy(own, a, loads.at[len(parts)]))
+    parts = [(0, near), (step, left), (2 * step, right), (3 * step, far0), (3 * step + far0.shape[0], far1)]
+    copies = [
+        pltpu.make_async_copy(ref, a.at[pl.ds(at, ref.shape[0])], loads.at[n]) for n, (at, ref) in enumerate(parts)
+    ]
     for copy in copies:
         copy.start()
 
@@ -146,25 +146,14 @@
             row = pl.multiple_of((slot * groups + g % groups) * GROUP, GROUP)
             total[away, pl.ds(row, GROUP), :] = block[i * GROUP : (i + 1) * GROUP]
 
-    def multiply(rows, columns):
-        product = jnp.dot(rows, dense[...], preferred_element_type=jnp.float32)
-        for n, c in enumerate(columns):
-            store(c, product[n * per : (n + 1) * per])
-
-    def at_column(by, side, y):
-        return ((x + by) % NX * NZH + side) * NY + y
-
-    for copy in copies[:3]:
-        copy.wait()
-    multiply(b[: 2 * step, :], [at_column(by, 1 - plane, y) for by in (0, NX - 1) for y in range(NY)])
-    for copy in copies[3:5]:
-        copy.wait()
-    multiply(b[2 * step :, :], [at_column(by, 1 - plane, y) for by in (1, 2) for y in range(NY)])
-    copies[5].wait()
-    half = max(NY // 2, 1)
-    for y0 in range(0, NY, half):
-        rows = a[y0 * NX * per : (y0 + half) * NX * per, :]
-        multiply(rows, [at_column(by, plane, y0 + y) for y in range(half) for by in (0, NX - 1, 1, 2)])
+    for n, by in enumerate((0, NX - 1, 1, 2)):
+        for copy in copies[n : n + 1 if n < 3 else n + 2]:
+            copy.wait()
+        product = jnp.dot(a[n * step : (n + 1) * step, :], dense[...], preferred_element_type=jnp.float32)
+        for m, side in enumerate((plane, 1 - plane)):
+            for y in range(NY):
+                row = (m * NY + y) * per
+                store(((x + by) % NX * NZH + side) * NY + y, product[row : row + per])
     out = [pltpu.make_async_copy(total.at[k], ref, stores.at[k]) for k, ref in enumerate((keep, send))]
     for copy in out:
         copy.start()
@@ -172,19 +161,18 @@
         copy.wait()
 
 
-def contract(where, own, near, left, right, far0, far1, dense):
-    occ = own.shape[0] * NZH
+def contract(where, near, left, right, far0, far1, dense):
+    occ = near.shape[0] * NX
     shape = jax.ShapeDtypeStruct((occ // NCORE, dense.shape[1]), jnp.float32)
     return pl.pallas_call(
         contract_kernel,
         out_shape=(shape, shape),
-        in_specs=[SMEM] + [ANY] * 6 + [VMEM],
+        in_specs=[SMEM] + [ANY] * 5 + [VMEM],
         out_specs=(ANY, ANY),
         scratch_shapes=[
-            pltpu.VMEM(own.shape, own.dtype),
-            pltpu.VMEM(own.shape, own.dtype),
+            pltpu.VMEM((occ, dense.shape[0]), near.dtype),
             pltpu.VMEM((NCORE, *shape.shape), jnp.float32),
-            pltpu.SemaphoreType.DMA((6,)),
+            pltpu.SemaphoreType.DMA((5,)),
             pltpu.SemaphoreType.DMA((NCORE,)),
         ],
         compiler_params=pltpu.CompilerParams(vmem_limit_bytes=56 << 20),
@@ -192,7 +180,7 @@
             flops=2 * occ * dense.shape[0] * dense.shape[1], bytes_accessed=12 << 20, transcendentals=0
         ),
         name="contract",
-    )(where, own, near, left, right, far0, far1, dense)
+    )(where, near, left, right, far0, far1, dense)
 
 
 def per_device(tiles, dest_col, mu_block, col_block, coeff):
@@ -202,15 +190,17 @@
     where = jnp.stack([here // (NZH * NY), here // NY % NZH, row // NCORE, row % NCORE]).astype(jnp.int32)
 
     mine = coeff.T
+    padded = jnp.pad(mine, ((0, WIDE - per), (0, 0)))
+    own = lax.all_gather(padded, "col", axis=0, tiled=True, axis_index_groups=Y_GROUPS)
+    own = own.reshape(NY, WIDE, mu_rows)[:, :per].reshape(NY * per, mu_rows)
     theirs = lax.ppermute(mine, "col", PLANE_SWAP)
-    own = jnp.concatenate([mine] + [lax.ppermute(mine, "col", x_shift(by)) for by in (1, -1, 2)], axis=0)
     route = dest_col.reshape(held) * CELLS + mu_block.reshape(held) * CB + col_block.reshape(held)
     outgoing = pack(tiles.reshape(held, rows, cols), route)
-    outgoing, theirs, own = lax.optimization_barrier((outgoing, theirs, own))
+    theirs = lax.all_gather(theirs, "col", axis=0, tiled=True, axis_index_groups=Y_GROUPS)
+    near = jnp.concatenate([own, theirs], axis=0)
+    outgoing, near = lax.optimization_barrier((outgoing, near))
     arrived = lax.all_to_all(outgoing, "col", split_axis=0, concat_axis=0, tiled=True)
 
-    own = lax.all_gather(own, "col", axis=0, tiled=True, axis_index_groups=Y_GROUPS)
-    near = lax.all_gather(theirs, "col", axis=0, tiled=True, axis_index_groups=Y_GROUPS)
     left = lax.ppermute(near, "col", x_shift(1))
     right = lax.ppermute(near, "col", x_shift(-1))
     cut = near.shape[0] // 2
@@ -219,7 +209,7 @@
 
     labels = arrived[:, CAP * rows, :CAP].astype(jnp.int32)
     dense = place(labels, arrived, mu_rows)
-    keep, send = contract(where, own, near, left, right, far0, far1, dense)
+    keep, send = contract(where, near, left, right, far0, far1, dense)
     share = keep + lax.ppermute(send, "row", CORE_SWAP)
     share = lax.all_to_all(
         share.reshape(NEAR, 2 * OUT_ROWS, -1), "row", split_axis=0, concat_axis=0, tiled=True, axis_index_groups=NEAR_GROUPS

time: 254 us -> 247 us (0.972)
  waiting for transfers between devices: 36.5 us -> 86 us
  blocking collectives: 113 us -> 63.9 us
  starting transfers between devices: 61.3 us -> 53.4 us
    all_gather x1, blocking collectives: 84.6 us -> 28.5 us  [per_device(): lax.all_gather(theirs, 'col', axis=0, tiled=True, axis_index_groups=Y_GRO...]
    ppermute x1, waiting for transfers between devices: 11.8 us -> 51.4 us  [per_device(): right = lax.ppermute(near, 'col', x_shift(-1))]
    ppermute x3 -> x0, starting transfers between devices: 16.1 us -> none  [per_device(): lax.ppermute(mine, 'col', x_shift(by))]
    all_to_all x1, blocking collectives: 28.4 us -> 35.5 us  [per_device(): lax.all_to_all(share.reshape(NEAR, 2 * OUT_ROWS, -1), 'row', split_axis=0...]
    all_gather x1, waiting for transfers between devices: 0.01 us -> 5.81 us  [per_device(): lax.all_gather(padded, 'col', axis=0, tiled=True, axis_index_groups=Y_GRO...]
    ppermute x1, starting transfers between devices: 9.42 us -> 15.1 us  [per_device(): theirs = lax.ppermute(mine, 'col', PLANE_SWAP)]
    ppermute x1, waiting for transfers between devices: 0.01 us -> 5.66 us  [per_device(): far1 = lax.ppermute(right[cut:], 'col', x_shift(-1))]
    ppermute x1, starting transfers between devices: 1.92 us -> 6.47 us  [per_device(): lax.ppermute(away, 'row', FAR_SWAP)]
  transfers between devices with their start and end apart: 12 -> 9, of which waited for: 4 -> 6; matrix products, arithmetic and copies ran while one was open for 1% -> 1% of each run, Pallas kernels for 2% -> 2%
where the time goes in v4:
time: 247 us; the launch traced here: 245 us
  waiting for transfers between devices  86 us (35%)
  blocking collectives  63.9 us (26%)
  starting transfers between devices  53.4 us (22%)
  Pallas kernels  16 us (6%)
  between operations  13.6 us (6%)
  local copies, waits for them, and re-layouts  6.4 us (3%)
  other arithmetic  5.27 us (2%)
    ppermute x1, waiting for transfers between devices, per_device(): right = lax.ppermute(near, 'col', x_shift(-1))  51.4 us
    all_to_all x1, blocking collectives, per_device(): lax.all_to_all(share.reshape(NEAR, 2 * OUT_ROWS, -1), 'row', split_axis=0...  35.5 us
    all_gather x1, blocking collectives, per_device(): lax.all_gather(theirs, 'col', axis=0, tiled=True, axis_index_groups=Y_GRO...  28.5 us
    ppermute x1, waiting for transfers between devices, per_device(): lax.ppermute(away, 'row', FAR_SWAP)  16 us
    all_to_all x1, starting transfers between devices, per_device(): lax.all_to_all(outgoing, 'col', split_axis=0, concat_axis=0, tiled=True)  15.8 us
    ppermute x1, starting transfers between devices, per_device(): theirs = lax.ppermute(mine, 'col', PLANE_SWAP)  15.1 us
    pallas_call x1, Pallas kernels, contract(): pl.pallas_call(contract_kernel, out_shape=(shape, shape), in_specs=[SMEM]...  10.4 us
    ppermute x1, starting transfers between devices, per_device(): lax.ppermute(away, 'row', FAR_SWAP)  6.47 us
  transfers between devices with their start and end apart: 9, of which 6 were waited for; matrix products, arithmetic and copies ran while one was open for 1% of the time, Pallas kernels for 2%

profile of v4, /device:TPU:6, one launch (start us, length us, event | category | flops | bytes accessed | tf_op | source)
XLA Modules:
  0.0 244.7 jit_solution(12430605924302808160)
XLA Ops:
  6.5 0.0 all-gather.2.cloned.1.call-start
  6.5 1.6 pad.4
  8.1 0.0 all-gather.2.cloned.1.call-update
  8.1 15.1 %collective-permute-start = (bf16[24,2048]{1,0:T(8,128)(2,1)}, bf16[24,2048]{1,0:T(8,128)(2,1)S(1)}, u32[]{:S(2)}, u32[]{:S(2)}) collective-permute-start(bf16[24,2048]{1,0:T(8,128)(2,1)} %bitcast.24), channel_id=1, source_target_pairs={{0,8},{1,9},{2,10},{3,11},{4,12},{5,13},{6,14},{7,15},{8,0},{9,1},... | collective-permute-start | bytes 294920 | tf_op jit(solution)/shard_map/ppermute | solution.py:196
  23.3 0.7 bitcast_add_fusion.route
  24.0 0.0 copy-start.2
  24.0 1.2 copy-done.2
  25.2 2.3 pack.1
  27.5 0.0 copy-start
  27.5 0.0 collective-permute-done
  27.5 28.5 %all_gather.7 = bf16[192,2048]{1,0:T(8,128)(2,1)S(1)} all-gather(bf16[24,2048]{1,0:T(8,128)(2,1)S(1)} %collective-permute-done), channel_id=1, replica_groups={{0,1,2,3,4,5,6,7},{8,9,10,11,12,13,14,15},{16,17,18,19,20,21,22,23},{24..., dimensions={0}, use_global_device_ids=true | all-gather | bytes 884736 | tf_op jit(solution)/shard_map/all_gather | solution.py:199
  55.9 5.8 %all-gather.2.cloned.1.call-done = bf16[256,2048]{1,0:T(8,128)(2,1)} async-done(((bf16[32,2048]{1,0:T(8,128)(2,1)}), bf16[256,2048]{1,0:T(8,128)(2,1)}) %all-gather.2.cloned.1.call-update) | async-done | bytes 1048592 | tf_op jit(solution)/shard_map/all_gather | solution.py:194
  61.7 1.2 slice.24
  62.9 0.0 copy-done
  62.9 1.3 pad_maximum_fusion.near
  64.2 15.8 %all-to-all-start = ((bf16[64,144,128]{2,1,0:T(8,128)(2,1)}), bf16[64,144,128]{2,1,0:T(8,128)(2,1)S(1)}, u32[]{:S(2)}, u32[]{:S(2)}) async-start(bf16[64,144,128]{2,1,0:T(8,128)(2,1)} %copy-done), calls=%async_computation | async-start | bytes 4718592 | tf_op jit(solution)/shard_map/all_to_all | solution.py:202
  80.1 2.7 %collective-permute-start.2 = (bf16[384,2048]{1,0:T(8,128)(2,1)}, bf16[384,2048]{1,0:T(8,128)(2,1)S(1)}, u32[]{:S(2)}, u32[]{:S(2)}) collective-permute-start(bf16[384,2048]{1,0:T(8,128)(2,1)} %pad_maximum_fusion.near), channel_id=1, source_target_pairs={{0,48},{1,49},{2,50},{3,51},{4,52},{5,53},{6,54},{7,55},{8,56},{9,... | collective-permute-start | bytes 4718600 | tf_op jit(solution)/shard_map/ppermute | solution.py:205
  82.7 4.4 %collective-permute-start.1 = (bf16[384,2048]{1,0:T(8,128)(2,1)}, bf16[384,2048]{1,0:T(8,128)(2,1)S(1)}, u32[]{:S(2)}, u32[]{:S(2)}) collective-permute-start(bf16[384,2048]{1,0:T(8,128)(2,1)} %pad_maximum_fusion.near), channel_id=1, source_target_pairs={{0,16},{1,17},{2,18},{3,19},{4,20},{5,21},{6,22},{7,23},{8,24},{9,... | collective-permute-start | bytes 4718600 | tf_op jit(solution)/shard_map/ppermute | solution.py:204
  87.1 51.4 %collective-permute-done.2.right = bf16[384,2048]{1,0:T(8,128)(2,1)S(1)} collective-permute-done((bf16[384,2048]{1,0:T(8,128)(2,1)}, bf16[384,2048]{1,0:T(8,128)(2,1)S(1)}, u32[]{:S(2)}, u32[]{:S(2)}) %collective-permute-start.2) | collective-permute-done | bytes 1572896 | tf_op jit(solution)/shard_map/ppermute | solution.py:205
  138.5 0.0 copy-start.3
  138.5 0.1 slice.26
  138.6 2.0 collective-permute-start.4
  140.6 0.0 collective-permute-done.1.left
  140.6 0.0 copy-start.4
  140.6 1.0 slice.25
  141.6 0.0 copy-done.3
  141.6 5.0 %collective-permute-start.3 = (bf16[192,2048]{1,0:T(8,128)(2,1)}, bf16[192,2048]{1,0:T(8,128)(2,1)}, u32[]{:S(2)}, u32[]{:S(2)}) collective-permute-start(bf16[192,2048]{1,0:T(8,128)(2,1)} %slice.25), channel_id=1, source_target_pairs={{0,16},{1,17},{2,18},{3,19},{4,20},{5,21},{6,22},{7,23},{8,24},{9,... | collective-permute-start | bytes 2359304 | tf_op jit(solution)/shard_map/ppermute | solution.py:207
  146.7 0.0 copy-done.4
  146.8 0.7 pad_add_fusion.where
  147.4 0.0 all-to-all-done.arrived
  147.5 3.3 %place.1.dense = bf16[2048,512]{1,0:T(8,128)(2,1)S(1)} custom-call(s32[64,2]{1,0:T(8,128)S(1)} %bitcast.19, bf16[64,144,128]{2,1,0:T(8,128)(2,1)S(1)} %all-to-all-done.arrived), custom_call_target="tpu_custom_call" | custom-call | bytes 4194304 | tf_op jit(solution)/shard_map/place/pallas_call | solution.py:116
  150.8 0.0 copy-start.1
  150.8 1.3 copy-done.1
  152.1 5.7 %collective-permute-done.4.far1 = bf16[192,2048]{1,0:T(8,128)(2,1)} collective-permute-done((bf16[192,2048]{1,0:T(8,128)(2,1)S(1)}, bf16[192,2048]{1,0:T(8,128)(2,1)}, u32[]{:S(2)}, u32[]{:S(2)}) %collective-permute-start.4) | collective-permute-done | bytes 786464 | tf_op jit(solution)/shard_map/ppermute | solution.py:208
  157.8 3.6 %collective-permute-done.3.far0 = bf16[192,2048]{1,0:T(8,128)(2,1)} collective-permute-done((bf16[192,2048]{1,0:T(8,128)(2,1)}, bf16[192,2048]{1,0:T(8,128)(2,1)}, u32[]{:S(2)}, u32[]{:S(2)}) %collective-permute-start.3) | collective-permute-done | bytes 786464 | tf_op jit(solution)/shard_map/ppermute | solution.py:207
  161.3 10.4 %contract.1 = (f32[768,512]{1,0:T(8,128)}, f32[768,512]{1,0:T(8,128)}) custom-call(s32[4]{0:T(128)} %pad_add_fusion.where, bf16[384,2048]{1,0:T(8,128)(2,1)} %pad_maximum_fusion.near, bf16[384,2048]{1,0:T(8,128)(2,1)} %copy-done.4, bf16[384,2048]{1,0:T(8,128)(2,1)} %copy-done.3, bf16[192,2048]{1,0:T(8,128)(2,1)} %collective-permute-done.3.far0, ...), custom_call_target="tpu_custom_call" | custom-call | flops 3221225472 | bytes 12582912 | tf_op jit(solution)/shard_map/contract/pallas_call | solution.py:167
  171.8 1.9 collective-permute-start.5
  173.7 3.6 %collective-permute-done.5 = f32[768,512]{1,0:T(8,128)S(1)} collective-permute-done((f32[768,512]{1,0:T(8,128)}, f32[768,512]{1,0:T(8,128)S(1)}, u32[]{:S(2)}, u32[]{:S(2)}) %collective-permute-start.5) | collective-permute-done | bytes 1572896 | tf_op jit(solution)/shard_map/ppermute | solution.py:213
  177.3 1.8 add.28
  179.0 35.5 %all_to_all.10 = f32[3,256,512]{2,1,0:T(8,128)S(1)} all-to-all(f32[3,256,512]{2,1,0:T(8,128)S(1)} %bitcast.20), channel_id=1, replica_groups={{0,128,256},{64,192,320},{384,512,640},{448,576,704},{1,129,257},{65,19..., dimensions={0} | all-to-all | bytes 3145728 | tf_op jit(solution)/shard_map/all_to_all | solution.py:214
  214.5 0.1 slice_reduce_fusion
  214.7 6.5 %collective-permute-start.6 = (f32[128,512]{1,0:T(8,128)S(1)}, f32[128,512]{1,0:T(8,128)S(1)}, u32[]{:S(2)}, u32[]{:S(2)}) collective-permute-start(f32[128,512]{1,0:T(8,128)S(1)} %get-tuple-element.13), channel_id=1, source_target_pairs={{0,384},{64,448},{128,512},{192,576},{256,640},{320,704},{384,0},{... | collective-permute-start | bytes 786440 | tf_op jit(solution)/shard_map/ppermute | solution.py:218
  221.1 16.0 %collective-permute-done.6 = f32[128,512]{1,0:T(8,128)S(1)} collective-permute-done((f32[128,512]{1,0:T(8,128)S(1)}, f32[128,512]{1,0:T(8,128)S(1)}, u32[]{:S(2)}, u32[]{:S(2)}) %collective-permute-start.6) | collective-permute-done | bytes 262176 | tf_op jit(solution)/shard_map/ppermute | solution.py:218
  237.2 0.7 add_convert_fusion
  (1 shorter events, 0.0 us)
Async XLA Ops:
  6.5 55.2 %all-gather.2.cloned.1.call-start = ((), (), s32[]{:S(2)}) async-start(), calls=%async_computation.2 | async-start | bytes 1179648 | tf_op jit(solution)/shard_map/all_gather | solution.py:194
  8.1 19.3 %collective-permute-start = (bf16[24,2048]{1,0:T(8,128)(2,1)}, bf16[24,2048]{1,0:T(8,128)(2,1)S(1)}, u32[]{:S(2)}, u32[]{:S(2)}) collective-permute-start(bf16[24,2048]{1,0:T(8,128)(2,1)} %bitcast.24), channel_id=1, source_target_pairs={{0,8},{1,9},{2,10},{3,11},{4,12},{5,13},{6,14},{7,15},{8,0},{9,1},... | collective-permute-start | bytes 294920 | tf_op jit(solution)/shard_map/ppermute | solution.py:196
  24.0 1.2 copy-start.2
  27.5 35.5 %copy-start = (bf16[64,144,128]{2,1,0:T(8,128)(2,1)}, bf16[64,144,128]{2,1,0:T(8,128)(2,1)S(1)}, u32[]{:S(2)}) copy-start(bf16[64,144,128]{2,1,0:T(8,128)(2,1)S(1)} %pack.1) | copy-start | bytes 7077892
  64.2 83.2 %all-to-all-start = ((bf16[64,144,128]{2,1,0:T(8,128)(2,1)}), bf16[64,144,128]{2,1,0:T(8,128)(2,1)S(1)}, u32[]{:S(2)}, u32[]{:S(2)}) async-start(bf16[64,144,128]{2,1,0:T(8,128)(2,1)} %copy-done), calls=%async_computation | async-start | bytes 4718592 | tf_op jit(solution)/shard_map/all_to_all | solution.py:202
  80.1 58.4 %collective-permute-start.2 = (bf16[384,2048]{1,0:T(8,128)(2,1)}, bf16[384,2048]{1,0:T(8,128)(2,1)S(1)}, u32[]{:S(2)}, u32[]{:S(2)}) collective-permute-start(bf16[384,2048]{1,0:T(8,128)(2,1)} %pad_maximum_fusion.near), channel_id=1, source_target_pairs={{0,48},{1,49},{2,50},{3,51},{4,52},{5,53},{6,54},{7,55},{8,56},{9,... | collective-permute-start | bytes 4718600 | tf_op jit(solution)/shard_map/ppermute | solution.py:205
  82.7 57.9 %collective-permute-start.1 = (bf16[384,2048]{1,0:T(8,128)(2,1)}, bf16[384,2048]{1,0:T(8,128)(2,1)S(1)}, u32[]{:S(2)}, u32[]{:S(2)}) collective-permute-start(bf16[384,2048]{1,0:T(8,128)(2,1)} %pad_maximum_fusion.near), channel_id=1, source_target_pairs={{0,16},{1,17},{2,18},{3,19},{4,20},{5,21},{6,22},{7,23},{8,24},{9,... | collective-permute-start | bytes 4718600 | tf_op jit(solution)/shard_map/ppermute | solution.py:204
  138.5 3.1 %copy-start.3 = (bf16[384,2048]{1,0:T(8,128)(2,1)}, bf16[384,2048]{1,0:T(8,128)(2,1)S(1)}, u32[]{:S(2)}) copy-start(bf16[384,2048]{1,0:T(8,128)(2,1)S(1)} %collective-permute-done.2.right) | copy-start | bytes 4718596
  138.6 19.2 %collective-permute-start.4 = (bf16[192,2048]{1,0:T(8,128)(2,1)S(1)}, bf16[192,2048]{1,0:T(8,128)(2,1)}, u32[]{:S(2)}, u32[]{:S(2)}) collective-permute-start(bf16[192,2048]{1,0:T(8,128)(2,1)S(1)} %slice.26), channel_id=1, source_target_pairs={{0,48},{1,49},{2,50},{3,51},{4,52},{5,53},{6,54},{7,55},{8,56},{9,... | collective-permute-start | bytes 2359304 | tf_op jit(solution)/shard_map/ppermute | solution.py:208
  140.6 6.1 %copy-start.4 = (bf16[384,2048]{1,0:T(8,128)(2,1)}, bf16[384,2048]{1,0:T(8,128)(2,1)S(1)}, u32[]{:S(2)}) copy-start(bf16[384,2048]{1,0:T(8,128)(2,1)S(1)} %collective-permute-done.1.left) | copy-start | bytes 4718596
  141.6 19.7 %collective-permute-start.3 = (bf16[192,2048]{1,0:T(8,128)(2,1)}, bf16[192,2048]{1,0:T(8,128)(2,1)}, u32[]{:S(2)}, u32[]{:S(2)}) collective-permute-start(bf16[192,2048]{1,0:T(8,128)(2,1)} %slice.25), channel_id=1, source_target_pairs={{0,16},{1,17},{2,18},{3,19},{4,20},{5,21},{6,22},{7,23},{8,24},{9,... | collective-permute-start | bytes 2359304 | tf_op jit(solution)/shard_map/ppermute | solution.py:207
  150.8 1.3 copy-start.1
  171.8 5.5 %collective-permute-start.5 = (f32[768,512]{1,0:T(8,128)}, f32[768,512]{1,0:T(8,128)S(1)}, u32[]{:S(2)}, u32[]{:S(2)}) collective-permute-start(f32[768,512]{1,0:T(8,128)} %get-tuple-element.12), channel_id=1, source_target_pairs={{0,64},{64,0},{128,192},{192,128},{256,320},{320,256},{384,448},{4... | collective-permute-start | bytes 4718600 | tf_op jit(solution)/shard_map/ppermute | solution.py:213
  214.7 22.5 %collective-permute-start.6 = (f32[128,512]{1,0:T(8,128)S(1)}, f32[128,512]{1,0:T(8,128)S(1)}, u32[]{:S(2)}, u32[]{:S(2)}) collective-permute-start(f32[128,512]{1,0:T(8,128)S(1)} %get-tuple-element.13), channel_id=1, source_target_pairs={{0,384},{64,448},{128,512},{192,576},{256,640},{320,704},{384,0},{... | collective-permute-start | bytes 786440 | tf_op jit(solution)/shard_map/ppermute | solution.py:218
Sparse Core Ops, SparseCore 0:
  9.7 51.9 all-gather.1

commit v5 on v4

--- a/solution.py
+++ b/solution.py
@@ -26,6 +26,7 @@
     return (x * NZH + zh) * NY + y
 
 
+X_GROUPS = [[column(x, zh, y) for x in range(NX)] for zh in range(NZH) for y in range(NY)]
 Y_GROUPS = [[column(x, zh, y) for y in range(NY)] for x in range(NX) for zh in range(NZH)]
 NEAR_GROUPS = [
     [zl * NCORE + core for zl in range(half * NEAR, (half + 1) * NEAR)]
@@ -91,7 +92,20 @@
     )(route, tiles)
 
 
-def place_kernel(labels, arrived, dense):
+def contract_kernel(where, labels, own, near, left, right, far0, far1, arrived, keep, send, dense, a, b, total, loads, stores):
+    x, plane, zl, core = where[0], where[1], where[2], where[3]
+    step = near.shape[0]
+    per = step // NY
+    groups = OUT_ROWS // GROUP
+
+    parts = [(0, near), (step, left), (2 * step, right), (3 * step, far0), (3 * step + far0.shape[0], far1)]
+    copies = [
+        pltpu.make_async_copy(ref, b.at[pl.ds(at, ref.shape[0])], loads.at[n]) for n, (at, ref) in enumerate(parts)
+    ]
+    copies.append(pltpu.make_async_copy(own, a, loads.at[len(parts)]))
+    for copy in copies:
+        copy.start()
+
     rows = (arrived.shape[1] - LABEL_ROWS) // CAP
     cols = arrived.shape[2]
 
@@ -110,32 +124,6 @@
                 row = pl.multiple_of((cell // CB) * rows, rows)
                 col = pl.multiple_of(cell % CB * cols, cols)
                 dense[pl.ds(row, rows), pl.ds(col, cols)] = arrived[j, pl.ds(slot * rows, rows), :]
-
-
-def place(labels, arrived, mu_rows):
-    return pl.pallas_call(
-        place_kernel,
-        out_shape=jax.ShapeDtypeStruct((mu_rows, CB * arrived.shape[2]), arrived.dtype),
-        in_specs=[SMEM, VMEM],
-        out_specs=VMEM,
-        compiler_params=pltpu.CompilerParams(vmem_limit_bytes=24 << 20),
-        cost_estimate=pl.CostEstimate(flops=0, bytes_accessed=4 << 20, transcendentals=0),
-        name="place",
-    )(labels, arrived)
-
-
-def contract_kernel(where, near, left, right, far0, far1, dense, keep, send, a, total, loads, stores):
-    x, plane, zl, core = where[0], where[1], where[2], where[3]
-    step = near.shape[0]
-    per = step // (NZH * NY)
-    groups = OUT_ROWS // GROUP
-
-    parts = [(0, near), (step, left), (2 * step, right), (3 * step, far0), (3 * step + far0.shape[0], far1)]
-    copies = [
-        pltpu.make_async_copy(ref, a.at[pl.ds(at, ref.shape[0])], loads.at[n]) for n, (at, ref) in enumerate(parts)
-    ]
-    for copy in copies:
-        copy.start()
 
     def store(c, block):
         for i in range(per // GROUP):
@@ -146,14 +134,19 @@
             row = pl.multiple_of((slot * groups + g % groups) * GROUP, GROUP)
             total[away, pl.ds(row, GROUP), :] = block[i * GROUP : (i + 1) * GROUP]
 
-    for n, by in enumerate((0, NX - 1, 1, 2)):
-        for copy in copies[n : n + 1 if n < 3 else n + 2]:
-            copy.wait()
-        product = jnp.dot(a[n * step : (n + 1) * step, :], dense[...], preferred_element_type=jnp.float32)
-        for m, side in enumerate((plane, 1 - plane)):
+    def multiply(block, columns, side):
+        product = jnp.dot(block, dense[...], preferred_element_type=jnp.float32)
+        for n, xx in enumerate(columns):
             for y in range(NY):
-                row = (m * NY + y) * per
-                store(((x + by) % NX * NZH + side) * NY + y, product[row : row + per])
+                row = n * step + y * per
+                store((xx * NZH + side) * NY + y, product[row : row + per])
+
+    for copy in copies:
+        copy.wait()
+    for n in range(0, NX, 2):
+        multiply(a[n * step : (n + 2) * step, :], (n, n + 1), plane)
+    multiply(b[: 2 * step, :], (x, (x + NX - 1) % NX), 1 - plane)
+    multiply(b[2 * step :, :], ((x + 1) % NX, (x + 2) % NX), 1 - plane)
     out = [pltpu.make_async_copy(total.at[k], ref, stores.at[k]) for k, ref in enumerate((keep, send))]
     for copy in out:
         copy.start()
@@ -161,26 +154,27 @@
         copy.wait()
 
 
-def contract(where, near, left, right, far0, far1, dense):
-    occ = near.shape[0] * NX
-    shape = jax.ShapeDtypeStruct((occ // NCORE, dense.shape[1]), jnp.float32)
+def contract(where, labels, own, near, left, right, far0, far1, arrived):
+    occ, mu_rows = own.shape[0] * NZH, own.shape[1]
+    width = CB * arrived.shape[2]
+    shape = jax.ShapeDtypeStruct((occ // NCORE, width), jnp.float32)
     return pl.pallas_call(
         contract_kernel,
         out_shape=(shape, shape),
-        in_specs=[SMEM] + [ANY] * 5 + [VMEM],
+        in_specs=[SMEM] * 2 + [ANY] * 6 + [VMEM],
         out_specs=(ANY, ANY),
         scratch_shapes=[
-            pltpu.VMEM((occ, dense.shape[0]), near.dtype),
+            pltpu.VMEM((mu_rows, width), own.dtype),
+            pltpu.VMEM(own.shape, own.dtype),
+            pltpu.VMEM(own.shape, own.dtype),
             pltpu.VMEM((NCORE, *shape.shape), jnp.float32),
-            pltpu.SemaphoreType.DMA((5,)),
+            pltpu.SemaphoreType.DMA((6,)),
             pltpu.SemaphoreType.DMA((NCORE,)),
         ],
         compiler_params=pltpu.CompilerParams(vmem_limit_bytes=56 << 20),
-        cost_estimate=pl.CostEstimate(
-            flops=2 * occ * dense.shape[0] * dense.shape[1], bytes_accessed=12 << 20, transcendentals=0
-        ),
+        cost_estimate=pl.CostEstimate(flops=2 * occ * mu_rows * width, bytes_accessed=12 << 20, transcendentals=0),
         name="contract",
-    )(where, near, left, right, far0, far1, dense)
+    )(where, labels, own, near, left, right, far0, far1, arrived)
 
 
 def per_device(tiles, dest_col, mu_block, col_block, coeff):
@@ -196,11 +190,11 @@
     theirs = lax.ppermute(mine, "col", PLANE_SWAP)
     route = dest_col.reshape(held) * CELLS + mu_block.reshape(held) * CB + col_block.reshape(held)
     outgoing = pack(tiles.reshape(held, rows, cols), route)
-    theirs = lax.all_gather(theirs, "col", axis=0, tiled=True, axis_index_groups=Y_GROUPS)
-    near = jnp.concatenate([own, theirs], axis=0)
-    outgoing, near = lax.optimization_barrier((outgoing, near))
+    near = lax.all_gather(theirs, "col", axis=0, tiled=True, axis_index_groups=Y_GROUPS)
+    outgoing, own, near = lax.optimization_barrier((outgoing, own, near))
     arrived = lax.all_to_all(outgoing, "col", split_axis=0, concat_axis=0, tiled=True)
 
+    own = lax.all_gather(own, "col", axis=0, tiled=True, axis_index_groups=X_GROUPS)
     left = lax.ppermute(near, "col", x_shift(1))
     right = lax.ppermute(near, "col", x_shift(-1))
     cut = near.shape[0] // 2
@@ -208,8 +202,7 @@
     far1 = lax.ppermute(right[cut:], "col", x_shift(-1))
 
     labels = arrived[:, CAP * rows, :CAP].astype(jnp.int32)
-    dense = place(labels, arrived, mu_rows)
-    keep, send = contract(where, near, left, right, far0, far1, dense)
+    keep, send = contract(where, labels, own, near, left, right, far0, far1, arrived)
     share = keep + lax.ppermute(send, "row", CORE_SWAP)
     share = lax.all_to_all(
         share.reshape(NEAR, 2 * OUT_ROWS, -1), "row", split_axis=0, concat_axis=0, tiled=True, axis_index_groups=NEAR_GROUPS

time: 247 us -> 246 us (level)
    ppermute x1, waiting for transfers between devices: 51.4 us -> 45.9 us  [per_device(): right = lax.ppermute(near, 'col', x_shift(-1))]
    ppermute x1, waiting for transfers between devices: 5.66 us -> 10.8 us  [per_device(): far1 = lax.ppermute(right[cut:], 'col', x_shift(-1))]
    pallas_call x1 -> x0, Pallas kernels: 3.31 us -> none  [place(): pl.pallas_call(place_kernel, out_shape=jax.ShapeDtypeStruct((mu_rows, CB...]
    all_gather x0 -> x1, waiting for transfers between devices: none -> 2.68 us  [per_device(): lax.all_gather(own, 'col', axis=0, tiled=True, axis_index_groups=X_GROUPS)]
  transfers between devices with their start and end apart: 9 -> 10, of which waited for: 6 -> 7; matrix products, arithmetic and copies ran while one was open for 1% -> 1% of each run, Pallas kernels for 2% -> 2%
where the time goes in v5:
time: 246 us; the launch traced here: 244 us
  waiting for transfers between devices  84.8 us (34%)
  blocking collectives  64.9 us (26%)
  starting transfers between devices  54.3 us (22%)
  Pallas kernels  16.6 us (7%)
  between operations  13.6 us (6%)
  local copies, waits for them, and re-layouts  4.95 us (2%)
  other arithmetic  4.66 us (2%)
    ppermute x1, waiting for transfers between devices, per_device(): right = lax.ppermute(near, 'col', x_shift(-1))  45.9 us
    all_to_all x1, blocking collectives, per_device(): lax.all_to_all(share.reshape(NEAR, 2 * OUT_ROWS, -1), 'row', split_axis=0...  36.4 us
    all_gather x1, blocking collectives, per_device(): lax.all_gather(theirs, 'col', axis=0, tiled=True, axis_index_groups=Y_GRO...  28.5 us
    all_to_all x1, starting transfers between devices, per_device(): lax.all_to_all(outgoing, 'col', split_axis=0, concat_axis=0, tiled=True)  16.4 us
    ppermute x1, waiting for transfers between devices, per_device(): lax.ppermute(away, 'row', FAR_SWAP)  16 us
    ppermute x1, starting transfers between devices, per_device(): theirs = lax.ppermute(mine, 'col', PLANE_SWAP)  15.1 us
    pallas_call x1, Pallas kernels, contract(): pl.pallas_call(contract_kernel, out_shape=(shape, shape), in_specs=[SMEM]...  12.9 us
    ppermute x1, waiting for transfers between devices, per_device(): far1 = lax.ppermute(right[cut:], 'col', x_shift(-1))  10.8 us
  transfers between devices with their start and end apart: 10, of which 7 were waited for; matrix products, arithmetic and copies ran while one was open for 1% of the time, Pallas kernels for 2%

profile of v5, /device:TPU:6, one launch (start us, length us, event | category | flops | bytes accessed | tf_op | source)
XLA Modules:
  0.0 243.8 jit_solution(205872749961993945)
XLA Ops:
  6.5 0.0 all-gather.3.cloned.1.call-start
  6.5 1.6 pad.4
  8.1 0.0 all-gather.3.cloned.1.call-update
  8.1 15.1 %collective-permute-start = (bf16[24,2048]{1,0:T(8,128)(2,1)}, bf16[24,2048]{1,0:T(8,128)(2,1)S(1)}, u32[]{:S(2)}, u32[]{:S(2)}) collective-permute-start(bf16[24,2048]{1,0:T(8,128)(2,1)} %bitcast.23), channel_id=1, source_target_pairs={{0,8},{1,9},{2,10},{3,11},{4,12},{5,13},{6,14},{7,15},{8,0},{9,1},... | collective-permute-start | bytes 294920 | tf_op jit(solution)/shard_map/ppermute | solution.py:190
  23.3 0.7 bitcast_add_fusion.route
  24.0 0.0 copy-start
  24.0 1.2 copy-done
  25.2 3.7 %pack.1 = bf16[64,144,128]{2,1,0:T(8,128)(2,1)} custom-call(s32[64]{0:T(128)S(1)} %bitcast_add_fusion.route, bf16[64,64,128]{2,1,0:T(8,128)(2,1)S(1)} %bitcast.18), custom_call_target="tpu_custom_call" | custom-call | bytes 4194304 | tf_op jit(solution)/shard_map/pack/pallas_call | solution.py:83
  28.9 0.0 collective-permute-done
  28.9 28.5 %all_gather.10.near = bf16[192,2048]{1,0:T(8,128)(2,1)S(1)} all-gather(bf16[24,2048]{1,0:T(8,128)(2,1)S(1)} %collective-permute-done), channel_id=1, replica_groups={{0,1,2,3,4,5,6,7},{8,9,10,11,12,13,14,15},{16,17,18,19,20,21,22,23},{24..., dimensions={0}, use_global_device_ids=true | all-gather | bytes 884736 | tf_op jit(solution)/shard_map/all_gather | solution.py:193
  57.4 0.0 copy-start.2
  57.4 3.7 %all-gather.3.cloned.1.call-done = bf16[256,2048]{1,0:T(8,128)(2,1)} async-done(((bf16[32,2048]{1,0:T(8,128)(2,1)}), bf16[256,2048]{1,0:T(8,128)(2,1)}) %all-gather.3.cloned.1.call-update) | async-done | bytes 1048592 | tf_op jit(solution)/shard_map/all_gather | solution.py:188
  61.1 2.1 slice.24
  63.2 16.4 %all-to-all-start = ((bf16[64,144,128]{2,1,0:T(8,128)(2,1)}), bf16[64,144,128]{2,1,0:T(8,128)(2,1)S(1)}, u32[]{:S(2)}, u32[]{:S(2)}) async-start(bf16[64,144,128]{2,1,0:T(8,128)(2,1)} %pack.1), calls=%async_computation | async-start | bytes 4718592 | tf_op jit(solution)/shard_map/all_to_all | solution.py:195
  79.7 0.0 all-gather.5.cloned.1.call-start
  79.7 0.7 all-gather.5.cloned.1.call-update
  80.4 2.7 %collective-permute-start.2 = (bf16[192,2048]{1,0:T(8,128)(2,1)S(1)}, bf16[192,2048]{1,0:T(8,128)(2,1)S(1)}, u32[]{:S(2)}, u32[]{:S(2)}) collective-permute-start(bf16[192,2048]{1,0:T(8,128)(2,1)S(1)} %all_gather.10.near), channel_id=1, source_target_pairs={{0,48},{1,49},{2,50},{3,51},{4,52},{5,53},{6,54},{7,55},{8,56},{9,... | collective-permute-start | bytes 2359304 | tf_op jit(solution)/shard_map/ppermute | solution.py:199
  83.1 0.0 copy-done.2
  83.1 4.4 %collective-permute-start.1 = (bf16[192,2048]{1,0:T(8,128)(2,1)S(1)}, bf16[192,2048]{1,0:T(8,128)(2,1)S(1)}, u32[]{:S(2)}, u32[]{:S(2)}) collective-permute-start(bf16[192,2048]{1,0:T(8,128)(2,1)S(1)} %all_gather.10.near), channel_id=1, source_target_pairs={{0,16},{1,17},{2,18},{3,19},{4,20},{5,21},{6,22},{7,23},{8,24},{9,... | collective-permute-start | bytes 2359304 | tf_op jit(solution)/shard_map/ppermute | solution.py:198
  87.5 45.9 %collective-permute-done.2.right = bf16[192,2048]{1,0:T(8,128)(2,1)S(1)} collective-permute-done((bf16[192,2048]{1,0:T(8,128)(2,1)S(1)}, bf16[192,2048]{1,0:T(8,128)(2,1)S(1)}, u32[]{:S(2)}, u32[]{:S(2)}) %collective-permute-start.2) | collective-permute-done | bytes 786464 | tf_op jit(solution)/shard_map/ppermute | solution.py:199
  133.4 0.0 copy-start.3
  133.4 1.9 collective-permute-start.4
  135.3 0.0 collective-permute-done.1.left
  135.4 0.0 copy-start.4
  135.4 5.1 %collective-permute-start.3 = (bf16[96,2048]{1,0:T(8,128)(2,1)S(1)}, bf16[96,2048]{1,0:T(8,128)(2,1)S(1)}, u32[]{:S(2)}, u32[]{:S(2)}) collective-permute-start(bf16[96,2048]{1,0:T(8,128)(2,1)S(1)} %slice.26), channel_id=1, source_target_pairs={{0,16},{1,17},{2,18},{3,19},{4,20},{5,21},{6,22},{7,23},{8,24},{9,... | collective-permute-start | bytes 1179656 | tf_op jit(solution)/shard_map/ppermute | solution.py:201
  140.5 0.0 copy-done.3
  140.6 0.0 copy-done.4
  140.6 0.7 pad_add_fusion.where
  141.3 0.0 all-to-all-done.arrived
  141.3 0.0 copy-start.1
  141.3 0.7 slice_convert_fusion
  142.0 10.8 %collective-permute-done.4.far1 = bf16[96,2048]{1,0:T(8,128)(2,1)} collective-permute-done((bf16[96,2048]{1,0:T(8,128)(2,1)S(1)}, bf16[96,2048]{1,0:T(8,128)(2,1)}, u32[]{:S(2)}, u32[]{:S(2)}) %collective-permute-start.4) | collective-permute-done | bytes 393248 | tf_op jit(solution)/shard_map/ppermute | solution.py:202
  152.8 1.4 collective-permute-done.3.far0
  154.2 0.0 copy-start.5
  154.2 2.7 %all-gather.5.cloned.1.call-done.own = bf16[768,2048]{1,0:T(8,128)(2,1)} async-done(((bf16[192,2048]{1,0:T(8,128)(2,1)}), bf16[768,2048]{1,0:T(8,128)(2,1)}) %all-gather.5.cloned.1.call-update) | async-done | bytes 3145744 | tf_op jit(solution)/shard_map/all_gather | solution.py:197
  156.9 0.0 copy-done.1
  156.9 0.0 copy-done.5
  156.9 12.9 %contract.1 = (f32[768,512]{1,0:T(8,128)}, f32[768,512]{1,0:T(8,128)}) custom-call(s32[4]{0:T(128)} %pad_add_fusion.where, s32[64,2]{1,0:T(8,128)} %bitcast.24, bf16[768,2048]{1,0:T(8,128)(2,1)} %all-gather.5.cloned.1.call-done.own, bf16[192,2048]{1,0:T(8,128)(2,1)} %copy-done.2, bf16[192,2048]{1,0:T(8,128)(2,1)} %copy-done.4, bf16[192,2048]{1,0:T(8,128)(2,1)} %copy-done.3, ...), custom_call_target="tpu_custom_call" | custom-call | flops 3221225472 | bytes 12582912 | tf_op jit(solution)/shard_map/contract/pallas_call | solution.py:161
  169.8 1.9 collective-permute-start.5
  171.7 3.6 %collective-permute-done.5 = f32[768,512]{1,0:T(8,128)S(1)} collective-permute-done((f32[768,512]{1,0:T(8,128)}, f32[768,512]{1,0:T(8,128)S(1)}, u32[]{:S(2)}, u32[]{:S(2)}) %collective-permute-start.5) | collective-permute-done | bytes 1572896 | tf_op jit(solution)/shard_map/ppermute | solution.py:206
  175.3 1.8 add.28
  177.0 36.4 %all_to_all.10 = f32[3,256,512]{2,1,0:T(8,128)S(1)} all-to-all(f32[3,256,512]{2,1,0:T(8,128)S(1)} %bitcast.19), channel_id=1, replica_groups={{0,128,256},{64,192,320},{384,512,640},{448,576,704},{1,129,257},{65,19..., dimensions={0} | all-to-all | bytes 3145728 | tf_op jit(solution)/shard_map/all_to_all | solution.py:207
  213.4 0.1 slice_reduce_fusion
  213.6 6.6 %collective-permute-start.6 = (f32[128,512]{1,0:T(8,128)S(1)}, f32[128,512]{1,0:T(8,128)S(1)}, u32[]{:S(2)}, u32[]{:S(2)}) collective-permute-start(f32[128,512]{1,0:T(8,128)S(1)} %get-tuple-element.15), channel_id=1, source_target_pairs={{0,384},{64,448},{128,512},{192,576},{256,640},{320,704},{384,0},{... | collective-permute-start | bytes 786440 | tf_op jit(solution)/shard_map/ppermute | solution.py:211
  220.2 16.0 %collective-permute-done.6 = f32[128,512]{1,0:T(8,128)S(1)} collective-permute-done((f32[128,512]{1,0:T(8,128)S(1)}, f32[128,512]{1,0:T(8,128)S(1)}, u32[]{:S(2)}, u32[]{:S(2)}) %collective-permute-start.6) | collective-permute-done | bytes 262176 | tf_op jit(solution)/shard_map/ppermute | solution.py:211
  236.2 0.7 add_convert_fusion
  (2 shorter events, 0.1 us)
Async XLA Ops:
  6.5 54.6 %all-gather.3.cloned.1.call-start = ((), (), s32[]{:S(2)}) async-start(), calls=%async_computation.2 | async-start | bytes 1179648 | tf_op jit(solution)/shard_map/all_gather | solution.py:188
  8.1 20.8 %collective-permute-start = (bf16[24,2048]{1,0:T(8,128)(2,1)}, bf16[24,2048]{1,0:T(8,128)(2,1)S(1)}, u32[]{:S(2)}, u32[]{:S(2)}) collective-permute-start(bf16[24,2048]{1,0:T(8,128)(2,1)} %bitcast.23), channel_id=1, source_target_pairs={{0,8},{1,9},{2,10},{3,11},{4,12},{5,13},{6,14},{7,15},{8,0},{9,1},... | collective-permute-start | bytes 294920 | tf_op jit(solution)/shard_map/ppermute | solution.py:190
  24.0 1.2 copy-start
  57.4 25.7 %copy-start.2 = (bf16[192,2048]{1,0:T(8,128)(2,1)}, bf16[192,2048]{1,0:T(8,128)(2,1)S(1)}, u32[]{:S(2)}) copy-start(bf16[192,2048]{1,0:T(8,128)(2,1)S(1)} %all_gather.10.near) | copy-start | bytes 2359300
  63.2 78.1 %all-to-all-start = ((bf16[64,144,128]{2,1,0:T(8,128)(2,1)}), bf16[64,144,128]{2,1,0:T(8,128)(2,1)S(1)}, u32[]{:S(2)}, u32[]{:S(2)}) async-start(bf16[64,144,128]{2,1,0:T(8,128)(2,1)} %pack.1), calls=%async_computation | async-start | bytes 4718592 | tf_op jit(solution)/shard_map/all_to_all | solution.py:195
  79.7 77.2 %all-gather.5.cloned.1.call-start = ((), (), s32[]{:S(2)}) async-start(), calls=%async_computation.3 | async-start | bytes 3932160 | tf_op jit(solution)/shard_map/all_gather | solution.py:197
  80.4 53.0 %collective-permute-start.2 = (bf16[192,2048]{1,0:T(8,128)(2,1)S(1)}, bf16[192,2048]{1,0:T(8,128)(2,1)S(1)}, u32[]{:S(2)}, u32[]{:S(2)}) collective-permute-start(bf16[192,2048]{1,0:T(8,128)(2,1)S(1)} %all_gather.10.near), channel_id=1, source_target_pairs={{0,48},{1,49},{2,50},{3,51},{4,52},{5,53},{6,54},{7,55},{8,56},{9,... | collective-permute-start | bytes 2359304 | tf_op jit(solution)/shard_map/ppermute | solution.py:199
  83.1 52.3 %collective-permute-start.1 = (bf16[192,2048]{1,0:T(8,128)(2,1)S(1)}, bf16[192,2048]{1,0:T(8,128)(2,1)S(1)}, u32[]{:S(2)}, u32[]{:S(2)}) collective-permute-start(bf16[192,2048]{1,0:T(8,128)(2,1)S(1)} %all_gather.10.near), channel_id=1, source_target_pairs={{0,16},{1,17},{2,18},{3,19},{4,20},{5,21},{6,22},{7,23},{8,24},{9,... | collective-permute-start | bytes 2359304 | tf_op jit(solution)/shard_map/ppermute | solution.py:198
  133.4 7.2 %copy-start.3 = (bf16[192,2048]{1,0:T(8,128)(2,1)}, bf16[192,2048]{1,0:T(8,128)(2,1)S(1)}, u32[]{:S(2)}) copy-start(bf16[192,2048]{1,0:T(8,128)(2,1)S(1)} %collective-permute-done.2.right) | copy-start | bytes 2359300
  133.4 19.4 %collective-permute-start.4 = (bf16[96,2048]{1,0:T(8,128)(2,1)S(1)}, bf16[96,2048]{1,0:T(8,128)(2,1)}, u32[]{:S(2)}, u32[]{:S(2)}) collective-permute-start(bf16[96,2048]{1,0:T(8,128)(2,1)S(1)} %slice.27), channel_id=1, source_target_pairs={{0,48},{1,49},{2,50},{3,51},{4,52},{5,53},{6,54},{7,55},{8,56},{9,... | collective-permute-start | bytes 1179656 | tf_op jit(solution)/shard_map/ppermute | solution.py:202
  135.4 5.2 %copy-start.4 = (bf16[192,2048]{1,0:T(8,128)(2,1)}, bf16[192,2048]{1,0:T(8,128)(2,1)S(1)}, u32[]{:S(2)}) copy-start(bf16[192,2048]{1,0:T(8,128)(2,1)S(1)} %collective-permute-done.1.left) | copy-start | bytes 2359300
  135.4 18.8 %collective-permute-start.3 = (bf16[96,2048]{1,0:T(8,128)(2,1)S(1)}, bf16[96,2048]{1,0:T(8,128)(2,1)S(1)}, u32[]{:S(2)}, u32[]{:S(2)}) collective-permute-start(bf16[96,2048]{1,0:T(8,128)(2,1)S(1)} %slice.26), channel_id=1, source_target_pairs={{0,16},{1,17},{2,18},{3,19},{4,20},{5,21},{6,22},{7,23},{8,24},{9,... | collective-permute-start | bytes 1179656 | tf_op jit(solution)/shard_map/ppermute | solution.py:201
  141.3 15.6 %copy-start.1 = (bf16[64,144,128]{2,1,0:T(8,128)(2,1)}, bf16[64,144,128]{2,1,0:T(8,128)(2,1)S(1)}, u32[]{:S(2)}) copy-start(bf16[64,144,128]{2,1,0:T(8,128)(2,1)S(1)} %all-to-all-done.arrived) | copy-start | bytes 7077892
  154.2 2.7 %copy-start.5 = (bf16[96,2048]{1,0:T(8,128)(2,1)}, bf16[96,2048]{1,0:T(8,128)(2,1)S(1)}, u32[]{:S(2)}) copy-start(bf16[96,2048]{1,0:T(8,128)(2,1)S(1)} %collective-permute-done.3.far0) | copy-start | bytes 1179652
  169.8 5.5 %collective-permute-start.5 = (f32[768,512]{1,0:T(8,128)}, f32[768,512]{1,0:T(8,128)S(1)}, u32[]{:S(2)}, u32[]{:S(2)}) collective-permute-start(f32[768,512]{1,0:T(8,128)} %get-tuple-element.14), channel_id=1, source_target_pairs={{0,64},{64,0},{128,192},{192,128},{256,320},{320,256},{384,448},{4... | collective-permute-start | bytes 4718600 | tf_op jit(solution)/shard_map/ppermute | solution.py:206
  213.6 22.7 %collective-permute-start.6 = (f32[128,512]{1,0:T(8,128)S(1)}, f32[128,512]{1,0:T(8,128)S(1)}, u32[]{:S(2)}, u32[]{:S(2)}) collective-permute-start(f32[128,512]{1,0:T(8,128)S(1)} %get-tuple-element.15), channel_id=1, source_target_pairs={{0,384},{64,448},{128,512},{192,576},{256,640},{320,704},{384,0},{... | collective-permute-start | bytes 786440 | tf_op jit(solution)/shard_map/ppermute | solution.py:211
Sparse Core Ops, SparseCore 0:
  9.7 51.3 all-gather.2
  82.9 73.9 all-gather.4

commit v6 on v5

v6 whole, which is shorter than its diff:
```python
import functools

import jax
import jax.numpy as jnp
from jax import lax
from jax.experimental import pallas as pl
from jax.experimental.pallas import tpu as pltpu
from jax.sharding import PartitionSpec as P

CB = 4
CAP = 2
NX, NZH, NY = 4, 2, 8
NZL, NCORE = 6, 2
NEAR = NZL // 2
N_COL = NX * NZH * NY
LABEL_ROWS = 16
CELLS = 128
GROUP = 8
HALF = 64
WIDE = 32


def device(zl, core, x, zh, y):
    return (((zl * NCORE + core) * NX + x) * NZH + zh) * NY + y


def column(x, zh, y):
    return (x * NZH + zh) * NY + y


Y_GROUPS = [[column(x, zh, y) for y in range(NY)] for x in range(NX) for zh in range(NZH)]
NEAR_GROUPS = [
    [zl * NCORE + core for zl in range(half * NEAR, (half + 1) * NEAR)]
    for half in range(NZL // NEAR)
    for core in range(NCORE)
]
SIDE_SWAP = [(3 * m + a, 3 * m + 2 - a) for m in range(NZL * NCORE // 3) for a in (0, 2)]
FAR_SWAP = [
    (zl * NCORE + core, (zl + NEAR) % NZL * NCORE + core) for zl in range(NZL) for core in range(NCORE)
]
PLANE_SWAP = [
    (column(x, zh, y), column(x, 1 - zh, y)) for x in range(NX) for zh in range(NZH) for y in range(NY)
]
CORE_SWAP = [(zl * NCORE + core, zl * NCORE + 1 - core) for zl in range(NZL) for core in range(NCORE)]


def x_shift(by):
    return [
        (column(x, zh, y), column((x + by) % NX, zh, y))
        for x in range(NX)
        for zh in range(NZH)
        for y in range(NY)
    ]


def pack_kernel(route, tiles, out, count):
    held, rows, cols = tiles.shape
    label_at = CAP * rows

    @pl.loop(0, N_COL)
    def _(c):
        count[c] = 0
        out[c, pl.ds(label_at, LABEL_ROWS), :] = jnp.zeros((LABEL_ROWS, cols), out.dtype)

    lane = lax.broadcasted_iota(jnp.int32, (LABEL_ROWS, cols), 1)

    @pl.loop(0, held)
    def _(t):
        c = route[t] // CELLS
        slot = count[c]
        count[c] = slot + 1
        out[c, pl.ds(pl.multiple_of(slot * rows, rows), rows), :] = tiles[t]
        label = (route[t] % CELLS + 1).astype(jnp.float32)
        old = out[c, pl.ds(label_at, LABEL_ROWS), :].astype(jnp.float32)
        out[c, pl.ds(label_at, LABEL_ROWS), :] = jnp.where(lane == slot, label, old).astype(out.dtype)


SMEM = pl.BlockSpec(memory_space=pltpu.SMEM)
VMEM = pl.BlockSpec(memory_space=pltpu.VMEM)
ANY = pl.BlockSpec(memory_space=pl.ANY)


def pack(tiles, route):
    held, rows, cols = tiles.shape
    return pl.pallas_call(
        pack_kernel,
        out_shape=jax.ShapeDtypeStruct((N_COL, CAP * rows + LABEL_ROWS, cols), tiles.dtype),
        in_specs=[SMEM, VMEM],
        out_specs=VMEM,
        scratch_shapes=[pltpu.SMEM((N_COL,), jnp.int32)],
        compiler_params=pltpu.CompilerParams(vmem_limit_bytes=24 << 20),
        cost_estimate=pl.CostEstimate(flops=0, bytes_accessed=4 << 20, transcendentals=0),
        name="pack",
    )(route, tiles)


def assigned_row(u):
    q = u % 6
    return u // 6 * 3 + jnp.where(q == 1, 2, jnp.where(q == 5, 0, q // 2))


def contract_kernel(first, where, *refs):
    if first:
        labels, near, left, right, far0, far1, arrived, keep, send, dense, a, total, loads, stores = refs
    else:
        near, left, right, far0, far1, dense, keep, send, a, total, loads, stores = refs
    x, plane, zl, core = where[0], where[1], where[2], where[3]
    side = plane if first else 1 - plane
    step = near.shape[0]
    per = step // NY
    groups = HALF // GROUP

    parts = [(0, near), (step, left), (2 * step, right), (3 * step, far0), (3 * step + far0.shape[0], far1)]
    copies = [
        pltpu.make_async_copy(ref, a.at[pl.ds(at, ref.shape[0])], loads.at[n]) for n, (at, ref) in enumerate(parts)
    ]
    for copy in copies:
        copy.start()

    if first:
        rows = (arrived.shape[1] - LABEL_ROWS) // CAP
        cols = arrived.shape[2]

        @pl.loop(0, dense.shape[0] // rows)
        def _(m):
            dense[pl.ds(pl.multiple_of(m * rows, rows), rows), :] = jnp.zeros((rows, dense.shape[1]), dense.dtype)

        @pl.loop(0, N_COL)
        def _(j):
            for slot in range(CAP):
                label = labels[j, slot]

                @pl.when(label > 0)
                def _():
                    cell = label - 1
                    row = pl.multiple_of((cell // CB) * rows, rows)
                    col = pl.multiple_of(cell % CB * cols, cols)
                    dense[pl.ds(row, rows), pl.ds(col, cols)] = arrived[j, pl.ds(slot * rows, rows), :]

    def store(c, block):
        for i in range(per // GROUP):
            g = c * (per // GROUP) + i
            to = assigned_row(g // groups)
            away = jnp.where(to % NCORE == core, 0, 1)
            to = to // NCORE
            slot = to % NEAR * 2 + jnp.where(to // NEAR == zl // NEAR, 0, 1)
            row = pl.multiple_of((slot * groups + g % groups) * GROUP, GROUP)
            total[away, pl.ds(row, GROUP), :] = block[i * GROUP : (i + 1) * GROUP]

    def multiply(block, columns):
        product = jnp.dot(block, dense[...], preferred_element_type=jnp.float32)
        for n, xx in enumerate(columns):
            for y in range(NY):
                row = n * step + y * per
                store((xx * NZH + side) * NY + y, product[row : row + per])

    for copy in copies:
        copy.wait()
    multiply(a[: 2 * step, :], (x, (x + NX - 1) % NX))
    multiply(a[2 * step :, :], ((x + 1) % NX, (x + 2) % NX))
    out = [pltpu.make_async_copy(total.at[k], ref, stores.at[k]) for k, ref in enumerate((keep, send))]
    for copy in out:
        copy.start()
    for copy in out:
        copy.wait()


def contract(where, parts, dense=None, labels=None, arrived=None):
    first = dense is None
    step, mu_rows = parts[0].shape
    occ = step * NX
    width = CB * arrived.shape[2] if first else dense.shape[1]
    shape = jax.ShapeDtypeStruct((occ // NCORE, width), jnp.float32)
    placed = jax.ShapeDtypeStruct((mu_rows, width), parts[0].dtype)
    return pl.pallas_call(
        functools.partial(contract_kernel, first),
        out_shape=(shape, shape, placed) if first else (shape, shape),
        in_specs=[SMEM] * (2 if first else 1) + [ANY] * 5 + [VMEM],
        out_specs=(ANY, ANY, VMEM) if first else (ANY, ANY),
        scratch_shapes=[
            pltpu.VMEM((occ, mu_rows), parts[0].dtype),
            pltpu.VMEM((NCORE, *shape.shape), jnp.float32),
            pltpu.SemaphoreType.DMA((5,)),
            pltpu.SemaphoreType.DMA((NCORE,)),
        ],
        compiler_params=pltpu.CompilerParams(vmem_limit_bytes=56 << 20),
        cost_estimate=pl.CostEstimate(flops=2 * occ * mu_rows * width, bytes_accessed=8 << 20, transcendentals=0),
        name="contract",
    )(where, *([labels] if first else []), *parts, arrived if first else dense)


def along_y(rows):
    per, mu_rows = rows.shape
    padded = jnp.pad(rows, ((0, WIDE - per), (0, 0)))
    gathered = lax.all_gather(padded, "col", axis=0, tiled=True, axis_index_groups=Y_GROUPS)
    return gathered.reshape(NY, WIDE, mu_rows)[:, :per].reshape(NY * per, mu_rows)


def along_x(near):
    left = lax.ppermute(near, "col", x_shift(1))
    right = lax.ppermute(near, "col", x_shift(-1))
    cut = near.shape[0] // 2
    far0 = lax.ppermute(left[:cut], "col", x_shift(1))
    far1 = lax.ppermute(right[cut:], "col", x_shift(-1))
    return near, left, right, far0, far1


def swap_cores(keep, send):
    return keep + lax.ppermute(send, "row", CORE_SWAP)


def reduce(share):
    share = lax.all_to_all(
        share.reshape(NEAR, 2 * HALF, -1), "row", split_axis=0, concat_axis=0, tiled=True, axis_index_groups=NEAR_GROUPS
    )
    away = jnp.sum(share[:, HALF:], axis=0)
    result = jnp.sum(share[:, :HALF], axis=0) + lax.ppermute(away, "row", FAR_SWAP)
    return result.astype(jnp.bfloat16)


def per_device(tiles, dest_col, mu_block, col_block, coeff):
    held, rows, cols = tiles.shape[2:]
    here, row = lax.axis_index("col"), lax.axis_index("row")
    plane = here // NY % NZH
    where = jnp.stack([here // (NZH * NY), plane, row // NCORE, row % NCORE]).astype(jnp.int32)

    mine = coeff.T
    theirs = lax.ppermute(mine, "col", PLANE_SWAP)
    own = lax.all_gather(mine, "col", axis=0, tiled=True, axis_index_groups=Y_GROUPS)
    route = dest_col.reshape(held) * CELLS + mu_block.reshape(held) * CB + col_block.reshape(held)
    outgoing = pack(tiles.reshape(held, rows, cols), route)
    outgoing, own, theirs = lax.optimization_barrier((outgoing, own, theirs))
    arrived = lax.all_to_all(outgoing, "col", split_axis=0, concat_axis=0, tiled=True)
    labels = arrived[:, CAP * rows, :CAP].astype(jnp.int32)

    keep, send, dense = contract(where, along_x(own), labels=labels, arrived=arrived)
    share = swap_cores(keep, send)
    own_sum = reduce(share)
    parts = along_x(along_y(theirs))
    dense, _ = lax.optimization_barrier((dense, share))
    their_sum = reduce(swap_cores(*contract(where, parts, dense=dense)))

    side0 = jnp.where(plane == 0, own_sum, their_sum)
    side1 = jnp.where(plane == 0, their_sum, own_sum)
    moved = lax.ppermute(jnp.where(row % 3 == 0, side1, side0), "row", SIDE_SWAP)
    top = jnp.where(row % 3 == 2, side1, side0)
    return jnp.concatenate([top, jnp.where(row % 3 == 1, side1, moved)], axis=0)


def solution(mesh):
    in_specs = (
        P("row", "col", None, None, None),
        P("row", "col", None, None),
        P("row", "col", None),
        P("row", "col", None),
        P("row", "col"),
    )
    return jax.shard_map(per_device, mesh=mesh, in_specs=in_specs, out_specs=P("row", "col"), check_vma=False)
```

time: 246 us -> 271 us (1.10)
  starting transfers between devices: 54.3 us -> 115 us
  blocking collectives: 64.9 us -> 28.1 us
  waiting for transfers between devices: 84.8 us -> 79.3 us
  Pallas kernels: 16.6 us -> 21.7 us
    all_to_all x0 -> x2, starting transfers between devices: none -> 42.8 us  [reduce(): lax.all_to_all(share.reshape(NEAR, 2 * HALF, -1), 'row', split_axis=0, co...]
    all_to_all x1 -> x0, blocking collectives: 36.4 us -> none  [per_device(): lax.all_to_all(share.reshape(NEAR, 2 * OUT_ROWS, -1), 'row', split_axis=0...]
    ppermute x6 -> x13, starting transfers between devices: 22.7 us -> 48.3 us  [the longest x2 17.9 us: reduce(): lax.ppermute(away, 'row', FAR_SWAP)]
    ppermute x6 -> x13, waiting for transfers between devices: 77.7 us -> 53.7 us  [the longest x2 24.3 us: along_x(): left = lax.ppermute(near, 'col', x_shift(1))]
    all_to_all x1, waiting for transfers between devices: 0.01 us -> 17.1 us  [per_device(): lax.all_to_all(outgoing, 'col', split_axis=0, concat_axis=0, tiled=True)]
    all_to_all x0 -> x2, waiting for transfers between devices: none -> 8.43 us  [reduce(): lax.all_to_all(share.reshape(NEAR, 2 * HALF, -1), 'row', split_axis=0, co...]
    all_to_all x1, starting transfers between devices: 16.4 us -> 9.06 us  [per_device(): lax.all_to_all(outgoing, 'col', split_axis=0, concat_axis=0, tiled=True)]
    all_gather x2 -> x1, waiting for transfers between devices: 6.38 us -> 0.02 us  [along_y(): lax.all_gather(padded, 'col', axis=0, tiled=True, axis_index_groups=Y_GRO...]
  transfers between devices with their start and end apart: 10 -> 18, of which waited for: 7 -> 9; matrix products, arithmetic and copies ran while one was open for 1% -> 3% of each run, Pallas kernels for 2% -> 8%
where the time goes in v6:
time: 271 us; the launch traced here: 270 us
  starting transfers between devices  115 us (42%)
  waiting for transfers between devices  79.3 us (29%)
  blocking collectives  28.1 us (10%)
  Pallas kernels  21.7 us (8%)
  between operations  13.8 us (5%)
  other arithmetic  7.28 us (3%)
  local copies, waits for them, and re-layouts  4.78 us (2%)
    all_to_all x2, starting transfers between devices, reduce(): lax.all_to_all(share.reshape(NEAR, 2 * HALF, -1), 'row', split_axis=0, co...  42.8 us
    all_gather x1, blocking collectives, per_device(): lax.all_gather(mine, 'col', axis=0, tiled=True, axis_index_groups=Y_GROUPS)  28.1 us
    ppermute x2, waiting for transfers between devices, along_x(): left = lax.ppermute(near, 'col', x_shift(1))  24.3 us
    pallas_call x2, Pallas kernels, contract(): pl.pallas_call(functools.partial(contract_kernel, first), out_shape=(shap...  18 us
    ppermute x2, starting transfers between devices, reduce(): lax.ppermute(away, 'row', FAR_SWAP)  17.9 us
    all_to_all x1, waiting for transfers between devices, per_device(): lax.all_to_all(outgoing, 'col', split_axis=0, concat_axis=0, tiled=True)  17.1 us
    ppermute x1, starting transfers between devices, per_device(): theirs = lax.ppermute(mine, 'col', PLANE_SWAP)  15.1 us
    ppermute x2, waiting for transfers between devices, reduce(): lax.ppermute(away, 'row', FAR_SWAP)  9.16 us
  transfers between devices with their start and end apart: 18, of which 9 were waited for; matrix products, arithmetic and copies ran while one was open for 3% of the time, Pallas kernels for 8%

profile of v6, /device:TPU:6, one launch (start us, length us, event | category | flops | bytes accessed | tf_op | source)
XLA Modules:
  0.0 270.3 jit_solution(15015459151575035961)
XLA Ops:
  6.5 15.1 %collective-permute-start = (bf16[24,2048]{1,0:T(8,128)(2,1)}, bf16[24,2048]{1,0:T(8,128)(2,1)S(1)}, u32[]{:S(2)}, u32[]{:S(2)}) collective-permute-start(bf16[24,2048]{1,0:T(8,128)(2,1)} %bitcast.24), channel_id=1, source_target_pairs={{0,8},{1,9},{2,10},{3,11},{4,12},{5,13},{6,14},{7,15},{8,0},{9,1},... | collective-permute-start | bytes 294920 | tf_op jit(solution)/shard_map/ppermute | solution.py:228
  21.7 28.1 %all_gather.6.refs_1_ = bf16[192,2048]{1,0:T(8,128)(2,1)S(1)} all-gather(bf16[24,2048]{1,0:T(8,128)(2,1)} %bitcast.25), channel_id=1, replica_groups={{0,1,2,3,4,5,6,7},{8,9,10,11,12,13,14,15},{16,17,18,19,20,21,22,23},{24..., dimensions={0}, use_global_device_ids=true | all-gather | bytes 884736 | tf_op jit(solution)/shard_map/all_gather | solution.py:229
  49.8 0.8 bitcast_add_fusion.route
  50.5 1.2 copy-done
  51.8 3.7 %pack.1 = bf16[64,144,128]{2,1,0:T(8,128)(2,1)} custom-call(s32[64]{0:T(128)S(1)} %bitcast_add_fusion.route, bf16[64,64,128]{2,1,0:T(8,128)(2,1)S(1)} %bitcast.19), custom_call_target="tpu_custom_call" | custom-call | bytes 4194304 | tf_op jit(solution)/shard_map/pack/pallas_call | solution.py:85
  55.4 0.0 collective-permute-done
  55.5 9.1 %all-to-all-start = ((bf16[64,144,128]{2,1,0:T(8,128)(2,1)}), bf16[64,144,128]{2,1,0:T(8,128)(2,1)S(1)}, u32[]{:S(2)}, u32[]{:S(2)}) async-start(bf16[64,144,128]{2,1,0:T(8,128)(2,1)} %pack.1), calls=%async_computation | async-start | bytes 4718592 | tf_op jit(solution)/shard_map/all_to_all | solution.py:233
  64.5 0.0 all-gather.2.cloned.1.call-start
  64.6 0.7 pad.4
  65.2 0.0 all-gather.2.cloned.1.call-update
  65.3 2.2 collective-permute-start.5
  67.4 0.0 copy-done.2
  67.4 3.7 %collective-permute-start.6 = (bf16[192,2048]{1,0:T(8,128)(2,1)S(1)}, bf16[192,2048]{1,0:T(8,128)(2,1)S(1)}, u32[]{:S(2)}, u32[]{:S(2)}) collective-permute-start(bf16[192,2048]{1,0:T(8,128)(2,1)S(1)} %all_gather.6.refs_1_), channel_id=1, source_target_pairs={{0,48},{1,49},{2,50},{3,51},{4,52},{5,53},{6,54},{7,55},{8,56},{9,... | collective-permute-start | bytes 2359304 | tf_op jit(solution)/shard_map/ppermute | solution.py:201
  71.1 24.3 %collective-permute-done.5.refs_2_ = bf16[192,2048]{1,0:T(8,128)(2,1)S(1)} collective-permute-done((bf16[192,2048]{1,0:T(8,128)(2,1)S(1)}, bf16[192,2048]{1,0:T(8,128)(2,1)S(1)}, u32[]{:S(2)}, u32[]{:S(2)}) %collective-permute-start.5) | collective-permute-done | bytes 786464 | tf_op jit(solution)/shard_map/ppermute | solution.py:200
  95.5 3.7 %collective-permute-start.7 = (bf16[96,2048]{1,0:T(8,128)(2,1)S(1)}, bf16[96,2048]{1,0:T(8,128)(2,1)}, u32[]{:S(2)}, u32[]{:S(2)}) collective-permute-start(bf16[96,2048]{1,0:T(8,128)(2,1)S(1)} %slice.44), channel_id=1, source_target_pairs={{0,16},{1,17},{2,18},{3,19},{4,20},{5,21},{6,22},{7,23},{8,24},{9,... | collective-permute-start | bytes 1179656 | tf_op jit(solution)/shard_map/ppermute | solution.py:203
  99.2 1.9 collective-permute-done.6.refs_3_
  101.2 2.3 collective-permute-start.8
  103.4 0.0 copy-done.4
  103.4 0.0 copy-done.5
  103.5 0.6 pad_add_fusion.where
  104.1 17.1 %all-to-all-done.refs_6_ = bf16[64,144,128]{2,1,0:T(8,128)(2,1)S(1)} async-done(((bf16[64,144,128]{2,1,0:T(8,128)(2,1)}), bf16[64,144,128]{2,1,0:T(8,128)(2,1)S(1)}, u32[]{:S(2)}, u32[]{:S(2)}) %all-to-all-start) | async-done | bytes 2359328 | tf_op jit(solution)/shard_map/all_to_all | solution.py:233
  121.2 0.7 slice_convert_fusion
  121.9 0.0 collective-permute-done.7.refs_4_
  121.9 0.0 collective-permute-done.8.refs_5_
  121.9 0.7 copy-done.1
  122.7 0.1 copy-done.8
  122.8 10.0 %contract.2 = (f32[384,512]{1,0:T(8,128)}, f32[384,512]{1,0:T(8,128)}, bf16[2048,512]{1,0:T(8,128)(2,1)}) custom-call(s32[4]{0:T(128)} %pad_add_fusion.where, s32[64,2]{1,0:T(8,128)} %bitcast.26, bf16[192,2048]{1,0:T(8,128)(2,1)} %copy-done.2, bf16[192,2048]{1,0:T(8,128)(2,1)} %copy-done.4, bf16[192,2048]{1,0:T(8,128)(2,1)} %copy-done.5, ...), custom_call_target="tpu_custom_call" | custom-call | flops 1610612736 | bytes 8388608 | tf_op jit(solution)/shard_map/contract/pallas_call | solution.py:175
  132.7 1.9 collective-permute-start.9
  134.7 0.0 all-gather.2.cloned.1.call-done
  134.7 1.2 slice.40
  135.9 0.0 copy-start.3
  135.9 3.6 %collective-permute-start.1 = (bf16[192,2048]{1,0:T(8,128)(2,1)S(1)}, bf16[192,2048]{1,0:T(8,128)(2,1)S(1)}, u32[]{:S(2)}, u32[]{:S(2)}) collective-permute-start(bf16[192,2048]{1,0:T(8,128)(2,1)S(1)} %bitcast.20), channel_id=1, source_target_pairs={{0,16},{1,17},{2,18},{3,19},{4,20},{5,21},{6,22},{7,23},{8,24},{9,... | collective-permute-start | bytes 2359304 | tf_op jit(solution)/shard_map/ppermute | solution.py:200
  139.4 2.3 collective-permute-start.2
  141.7 0.0 collective-permute-done.9
  141.8 2.2 add.40
  143.9 28.9 %all-to-all-start.2 = ((f32[3,128,512]{2,1,0:T(8,128)}), f32[3,128,512]{2,1,0:T(8,128)S(1)}, u32[]{:S(2)}, u32[]{:S(2)}) async-start(f32[3,128,512]{2,1,0:T(8,128)} %bitcast.13), calls=%async_computation.2 | async-start | bytes 1572864 | tf_op jit(solution)/shard_map/all_to_all | solution.py:213
  172.9 0.0 collective-permute-done.1.refs_1_
  172.9 0.0 copy-done.3
  172.9 5.1 %collective-permute-start.3 = (bf16[96,2048]{1,0:T(8,128)(2,1)S(1)}, bf16[96,2048]{1,0:T(8,128)(2,1)S(1)}, u32[]{:S(2)}, u32[]{:S(2)}) collective-permute-start(bf16[96,2048]{1,0:T(8,128)(2,1)S(1)} %slice.41), channel_id=1, source_target_pairs={{0,16},{1,17},{2,18},{3,19},{4,20},{5,21},{6,22},{7,23},{8,24},{9,... | collective-permute-start | bytes 1179656 | tf_op jit(solution)/shard_map/ppermute | solution.py:203
  178.0 0.0 collective-permute-done.2.refs_2_
  178.1 0.0 copy-start.7
  178.1 1.9 collective-permute-start.4
  180.0 6.2 %collective-permute-done.3.refs_3_ = bf16[96,2048]{1,0:T(8,128)(2,1)S(1)} collective-permute-done((bf16[96,2048]{1,0:T(8,128)(2,1)S(1)}, bf16[96,2048]{1,0:T(8,128)(2,1)S(1)}, u32[]{:S(2)}, u32[]{:S(2)}) %collective-permute-start.3) | collective-permute-done | bytes 393248 | tf_op jit(solution)/shard_map/ppermute | solution.py:203
  186.2 5.4 %collective-permute-done.4.refs_4_ = bf16[96,2048]{1,0:T(8,128)(2,1)S(1)} collective-permute-done((bf16[96,2048]{1,0:T(8,128)(2,1)S(1)}, bf16[96,2048]{1,0:T(8,128)(2,1)S(1)}, u32[]{:S(2)}, u32[]{:S(2)}) %collective-permute-start.4) | collective-permute-done | bytes 393248 | tf_op jit(solution)/shard_map/ppermute | solution.py:204
  191.6 0.0 copy-done.6
  191.6 0.0 copy-done.7
  191.6 0.0 copy-done.9
  191.6 0.7 copy-done.10
  192.4 8.0 %contract.3 = (f32[384,512]{1,0:T(8,128)}, f32[384,512]{1,0:T(8,128)}) custom-call(s32[4]{0:T(128)} %pad_add_fusion.where, bf16[192,2048]{1,0:T(8,128)(2,1)} %bitcast.22, bf16[192,2048]{1,0:T(8,128)(2,1)} %copy-done.6, bf16[192,2048]{1,0:T(8,128)(2,1)} %copy-done.7, bf16[96,2048]{1,0:T(8,128)(2,1)} %copy-done.9, bf16[96,2048]{1,0:T(8,128)(2,1)} %copy-done.10, ...), custom_call_target="tpu_custom_call" | custom-call | flops 1610612736 | bytes 8388608 | tf_op jit(solution)/shard_map/contract/pallas_call | solution.py:175
  200.4 1.9 collective-permute-start.10
  202.3 2.5 collective-permute-done.10
  204.8 2.2 add.41
  207.0 0.0 all-to-all-done.2
  207.0 13.9 %all-to-all-start.1 = ((f32[3,128,512]{2,1,0:T(8,128)}), f32[3,128,512]{2,1,0:T(8,128)S(1)}, u32[]{:S(2)}, u32[]{:S(2)}) async-start(f32[3,128,512]{2,1,0:T(8,128)} %bitcast.12), calls=%async_computation.1 | async-start | bytes 1572864 | tf_op jit(solution)/shard_map/all_to_all | solution.py:213
  220.8 0.1 slice_reduce_fusion
  220.9 9.0 %collective-permute-start.12 = (f32[64,512]{1,0:T(8,128)S(1)}, f32[64,512]{1,0:T(8,128)S(1)}, u32[]{:S(2)}, u32[]{:S(2)}) collective-permute-start(f32[64,512]{1,0:T(8,128)S(1)} %get-tuple-element.23), channel_id=1, source_target_pairs={{0,384},{64,448},{128,512},{192,576},{256,640},{320,704},{384,0},{... | collective-permute-start | bytes 393224 | tf_op jit(solution)/shard_map/ppermute | solution.py:217
  229.9 8.4 %all-to-all-done.1 = f32[3,128,512]{2,1,0:T(8,128)S(1)} async-done(((f32[3,128,512]{2,1,0:T(8,128)}), f32[3,128,512]{2,1,0:T(8,128)S(1)}, u32[]{:S(2)}, u32[]{:S(2)}) %all-to-all-start.1) | async-done | bytes 786464 | tf_op jit(solution)/shard_map/all_to_all | solution.py:213
  238.3 0.1 slice_reduce_fusion.2
  238.4 8.9 %collective-permute-start.11 = (f32[64,512]{1,0:T(8,128)S(1)}, f32[64,512]{1,0:T(8,128)S(1)}, u32[]{:S(2)}, u32[]{:S(2)}) collective-permute-start(f32[64,512]{1,0:T(8,128)S(1)} %get-tuple-element.25), channel_id=1, source_target_pairs={{0,384},{64,448},{128,512},{192,576},{256,640},{320,704},{384,0},{... | collective-permute-start | bytes 393224 | tf_op jit(solution)/shard_map/ppermute | solution.py:217
  247.3 0.0 collective-permute-done.12
  247.3 9.2 %collective-permute-done.11 = f32[64,512]{1,0:T(8,128)S(1)} collective-permute-done((f32[64,512]{1,0:T(8,128)S(1)}, f32[64,512]{1,0:T(8,128)S(1)}, u32[]{:S(2)}, u32[]{:S(2)}) %collective-permute-start.11) | collective-permute-done | bytes 131104 | tf_op jit(solution)/shard_map/ppermute | solution.py:217
  256.6 1.9 collective-permute-start.13
  258.5 4.2 %collective-permute-done.13 = bf16[64,512]{1,0:T(8,128)(2,1)S(1)} collective-permute-done((bf16[64,512]{1,0:T(8,128)(2,1)S(1)}, bf16[64,512]{1,0:T(8,128)(2,1)S(1)}, u32[]{:S(2)}, u32[]{:S(2)}) %collective-permute-start.13) | collective-permute-done | bytes 65568 | tf_op jit(solution)/shard_map/ppermute | solution.py:245
  262.7 0.7 pad_maximum_fusion
  (16 shorter events, 0.2 us)
Async XLA Ops:
  6.5 48.9 %collective-permute-start = (bf16[24,2048]{1,0:T(8,128)(2,1)}, bf16[24,2048]{1,0:T(8,128)(2,1)S(1)}, u32[]{:S(2)}, u32[]{:S(2)}) collective-permute-start(bf16[24,2048]{1,0:T(8,128)(2,1)} %bitcast.24), channel_id=1, source_target_pairs={{0,8},{1,9},{2,10},{3,11},{4,12},{5,13},{6,14},{7,15},{8,0},{9,1},... | collective-permute-start | bytes 294920 | tf_op jit(solution)/shard_map/ppermute | solution.py:228
  49.8 17.7 %copy-start.2 = (bf16[192,2048]{1,0:T(8,128)(2,1)}, bf16[192,2048]{1,0:T(8,128)(2,1)S(1)}, u32[]{:S(2)}) copy-start(bf16[192,2048]{1,0:T(8,128)(2,1)S(1)} %all_gather.6.refs_1_) | copy-start | bytes 2359300
  50.5 1.2 copy-start
  55.5 65.8 %all-to-all-start = ((bf16[64,144,128]{2,1,0:T(8,128)(2,1)}), bf16[64,144,128]{2,1,0:T(8,128)(2,1)S(1)}, u32[]{:S(2)}, u32[]{:S(2)}) async-start(bf16[64,144,128]{2,1,0:T(8,128)(2,1)} %pack.1), calls=%async_computation | async-start | bytes 4718592 | tf_op jit(solution)/shard_map/all_to_all | solution.py:233
  64.5 70.2 %all-gather.2.cloned.1.call-start = ((), (), s32[]{:S(2)}) async-start(), calls=%async_computation.3 | async-start | bytes 1179648 | tf_op jit(solution)/shard_map/all_gather | solution.py:195
  65.3 30.2 %collective-permute-start.5 = (bf16[192,2048]{1,0:T(8,128)(2,1)S(1)}, bf16[192,2048]{1,0:T(8,128)(2,1)S(1)}, u32[]{:S(2)}, u32[]{:S(2)}) collective-permute-start(bf16[192,2048]{1,0:T(8,128)(2,1)S(1)} %all_gather.6.refs_1_), channel_id=1, source_target_pairs={{0,16},{1,17},{2,18},{3,19},{4,20},{5,21},{6,22},{7,23},{8,24},{9,... | collective-permute-start | bytes 2359304 | tf_op jit(solution)/shard_map/ppermute | solution.py:200
  67.4 33.7 %collective-permute-start.6 = (bf16[192,2048]{1,0:T(8,128)(2,1)S(1)}, bf16[192,2048]{1,0:T(8,128)(2,1)S(1)}, u32[]{:S(2)}, u32[]{:S(2)}) collective-permute-start(bf16[192,2048]{1,0:T(8,128)(2,1)S(1)} %all_gather.6.refs_1_), channel_id=1, source_target_pairs={{0,48},{1,49},{2,50},{3,51},{4,52},{5,53},{6,54},{7,55},{8,56},{9,... | collective-permute-start | bytes 2359304 | tf_op jit(solution)/shard_map/ppermute | solution.py:201
  95.5 8.0 %copy-start.4 = (bf16[192,2048]{1,0:T(8,128)(2,1)}, bf16[192,2048]{1,0:T(8,128)(2,1)S(1)}, u32[]{:S(2)}) copy-start(bf16[192,2048]{1,0:T(8,128)(2,1)S(1)} %collective-permute-done.5.refs_2_) | copy-start | bytes 2359300
  95.5 26.4 %collective-permute-start.7 = (bf16[96,2048]{1,0:T(8,128)(2,1)S(1)}, bf16[96,2048]{1,0:T(8,128)(2,1)}, u32[]{:S(2)}, u32[]{:S(2)}) collective-permute-start(bf16[96,2048]{1,0:T(8,128)(2,1)S(1)} %slice.44), channel_id=1, source_target_pairs={{0,16},{1,17},{2,18},{3,19},{4,20},{5,21},{6,22},{7,23},{8,24},{9,... | collective-permute-start | bytes 1179656 | tf_op jit(solution)/shard_map/ppermute | solution.py:203
  101.1 2.3 copy-start.5
  101.2 20.8 %collective-permute-start.8 = (bf16[96,2048]{1,0:T(8,128)(2,1)S(1)}, bf16[96,2048]{1,0:T(8,128)(2,1)S(1)}, u32[]{:S(2)}, u32[]{:S(2)}) collective-permute-start(bf16[96,2048]{1,0:T(8,128)(2,1)S(1)} %slice.45), channel_id=1, source_target_pairs={{0,48},{1,49},{2,50},{3,51},{4,52},{5,53},{6,54},{7,55},{8,56},{9,... | collective-permute-start | bytes 1179656 | tf_op jit(solution)/shard_map/ppermute | solution.py:204
  121.2 1.5 copy-start.1
  121.9 0.8 copy-start.8
  132.7 9.0 %collective-permute-start.9 = (f32[384,512]{1,0:T(8,128)}, f32[384,512]{1,0:T(8,128)S(1)}, u32[]{:S(2)}, u32[]{:S(2)}) collective-permute-start(f32[384,512]{1,0:T(8,128)} %get-tuple-element.19), channel_id=1, source_target_pairs={{0,64},{64,0},{128,192},{192,128},{256,320},{320,256},{384,448},{4... | collective-permute-start | bytes 2359304 | tf_op jit(solution)/shard_map/ppermute | solution.py:209
  135.9 37.0 %copy-start.3 = (bf16[8,24,2048]{2,1,0:T(8,128)(2,1)}, bf16[8,24,2048]{2,1,0:T(8,128)(2,1)S(1)}, u32[]{:S(2)}) copy-start(bf16[8,24,2048]{2,1,0:T(8,128)(2,1)S(1)} %slice.40) | copy-start | bytes 2359300
  135.9 37.0 %collective-permute-start.1 = (bf16[192,2048]{1,0:T(8,128)(2,1)S(1)}, bf16[192,2048]{1,0:T(8,128)(2,1)S(1)}, u32[]{:S(2)}, u32[]{:S(2)}) collective-permute-start(bf16[192,2048]{1,0:T(8,128)(2,1)S(1)} %bitcast.20), channel_id=1, source_target_pairs={{0,16},{1,17},{2,18},{3,19},{4,20},{5,21},{6,22},{7,23},{8,24},{9,... | collective-permute-start | bytes 2359304 | tf_op jit(solution)/shard_map/ppermute | solution.py:200
  139.4 38.6 %collective-permute-start.2 = (bf16[192,2048]{1,0:T(8,128)(2,1)S(1)}, bf16[192,2048]{1,0:T(8,128)(2,1)S(1)}, u32[]{:S(2)}, u32[]{:S(2)}) collective-permute-start(bf16[192,2048]{1,0:T(8,128)(2,1)S(1)} %bitcast.21), channel_id=1, source_target_pairs={{0,48},{1,49},{2,50},{3,51},{4,52},{5,53},{6,54},{7,55},{8,56},{9,... | collective-permute-start | bytes 2359304 | tf_op jit(solution)/shard_map/ppermute | solution.py:201
  143.9 63.1 %all-to-all-start.2 = ((f32[3,128,512]{2,1,0:T(8,128)}), f32[3,128,512]{2,1,0:T(8,128)S(1)}, u32[]{:S(2)}, u32[]{:S(2)}) async-start(f32[3,128,512]{2,1,0:T(8,128)} %bitcast.13), calls=%async_computation.2 | async-start | bytes 1572864 | tf_op jit(solution)/shard_map/all_to_all | solution.py:213
  172.9 18.7 %copy-start.6 = (bf16[192,2048]{1,0:T(8,128)(2,1)}, bf16[192,2048]{1,0:T(8,128)(2,1)S(1)}, u32[]{:S(2)}) copy-start(bf16[192,2048]{1,0:T(8,128)(2,1)S(1)} %collective-permute-done.1.refs_1_) | copy-start | bytes 2359300
  172.9 13.3 %collective-permute-start.3 = (bf16[96,2048]{1,0:T(8,128)(2,1)S(1)}, bf16[96,2048]{1,0:T(8,128)(2,1)S(1)}, u32[]{:S(2)}, u32[]{:S(2)}) collective-permute-start(bf16[96,2048]{1,0:T(8,128)(2,1)S(1)} %slice.41), channel_id=1, source_target_pairs={{0,16},{1,17},{2,18},{3,19},{4,20},{5,21},{6,22},{7,23},{8,24},{9,... | collective-permute-start | bytes 1179656 | tf_op jit(solution)/shard_map/ppermute | solution.py:203
  178.1 13.6 %copy-start.7 = (bf16[192,2048]{1,0:T(8,128)(2,1)}, bf16[192,2048]{1,0:T(8,128)(2,1)S(1)}, u32[]{:S(2)}) copy-start(bf16[192,2048]{1,0:T(8,128)(2,1)S(1)} %collective-permute-done.2.refs_2_) | copy-start | bytes 2359300
  178.1 13.5 %collective-permute-start.4 = (bf16[96,2048]{1,0:T(8,128)(2,1)S(1)}, bf16[96,2048]{1,0:T(8,128)(2,1)S(1)}, u32[]{:S(2)}, u32[]{:S(2)}) collective-permute-start(bf16[96,2048]{1,0:T(8,128)(2,1)S(1)} %slice.42), channel_id=1, source_target_pairs={{0,48},{1,49},{2,50},{3,51},{4,52},{5,53},{6,54},{7,55},{8,56},{9,... | collective-permute-start | bytes 1179656 | tf_op jit(solution)/shard_map/ppermute | solution.py:204
  186.2 5.4 %copy-start.9 = (bf16[96,2048]{1,0:T(8,128)(2,1)}, bf16[96,2048]{1,0:T(8,128)(2,1)S(1)}, u32[]{:S(2)}) copy-start(bf16[96,2048]{1,0:T(8,128)(2,1)S(1)} %collective-permute-done.3.refs_3_) | copy-start | bytes 1179652
  191.6 0.8 copy-start.10
  200.4 4.4 %collective-permute-start.10 = (f32[384,512]{1,0:T(8,128)}, f32[384,512]{1,0:T(8,128)S(1)}, u32[]{:S(2)}, u32[]{:S(2)}) collective-permute-start(f32[384,512]{1,0:T(8,128)} %get-tuple-element.22), channel_id=1, source_target_pairs={{0,64},{64,0},{128,192},{192,128},{256,320},{320,256},{384,448},{4... | collective-permute-start | bytes 2359304 | tf_op jit(solution)/shard_map/ppermute | solution.py:209
  207.0 31.3 %all-to-all-start.1 = ((f32[3,128,512]{2,1,0:T(8,128)}), f32[3,128,512]{2,1,0:T(8,128)S(1)}, u32[]{:S(2)}, u32[]{:S(2)}) async-start(f32[3,128,512]{2,1,0:T(8,128)} %bitcast.12), calls=%async_computation.1 | async-start | bytes 1572864 | tf_op jit(solution)/shard_map/all_to_all | solution.py:213
  220.9 26.4 %collective-permute-start.12 = (f32[64,512]{1,0:T(8,128)S(1)}, f32[64,512]{1,0:T(8,128)S(1)}, u32[]{:S(2)}, u32[]{:S(2)}) collective-permute-start(f32[64,512]{1,0:T(8,128)S(1)} %get-tuple-element.23), channel_id=1, source_target_pairs={{0,384},{64,448},{128,512},{192,576},{256,640},{320,704},{384,0},{... | collective-permute-start | bytes 393224 | tf_op jit(solution)/shard_map/ppermute | solution.py:217
  238.4 18.1 %collective-permute-start.11 = (f32[64,512]{1,0:T(8,128)S(1)}, f32[64,512]{1,0:T(8,128)S(1)}, u32[]{:S(2)}, u32[]{:S(2)}) collective-permute-start(f32[64,512]{1,0:T(8,128)S(1)} %get-tuple-element.25), channel_id=1, source_target_pairs={{0,384},{64,448},{128,512},{192,576},{256,640},{320,704},{384,0},{... | collective-permute-start | bytes 393224 | tf_op jit(solution)/shard_map/ppermute | solution.py:217
  256.6 6.2 %collective-permute-start.13 = (bf16[64,512]{1,0:T(8,128)(2,1)S(1)}, bf16[64,512]{1,0:T(8,128)(2,1)S(1)}, u32[]{:S(2)}, u32[]{:S(2)}) collective-permute-start(bf16[64,512]{1,0:T(8,128)(2,1)S(1)} %broadcast_select_fusion), channel_id=1, source_target_pairs={{0,128},{128,0},{192,320},{320,192},{384,512},{512,384},{576,704},... | collective-permute-start | bytes 196616 | tf_op jit(solution)/shard_map/ppermute | solution.py:245
Sparse Core Ops, SparseCore 0:
  67.7 58.8 all-gather.1

commit v7 on v5

--- a/solution.py
+++ b/solution.py
@@ -26,13 +26,7 @@
     return (x * NZH + zh) * NY + y
 
 
-X_GROUPS = [[column(x, zh, y) for x in range(NX)] for zh in range(NZH) for y in range(NY)]
 Y_GROUPS = [[column(x, zh, y) for y in range(NY)] for x in range(NX) for zh in range(NZH)]
-NEAR_GROUPS = [
-    [zl * NCORE + core for zl in range(half * NEAR, (half + 1) * NEAR)]
-    for half in range(NZL // NEAR)
-    for core in range(NCORE)
-]
 FAR_SWAP = [
     (zl * NCORE + core, (zl + NEAR) % NZL * NCORE + core) for zl in range(NZL) for core in range(NCORE)
 ]
@@ -40,6 +34,14 @@
     (column(x, zh, y), column(x, 1 - zh, y)) for x in range(NX) for zh in range(NZH) for y in range(NY)
 ]
 CORE_SWAP = [(zl * NCORE + core, zl * NCORE + 1 - core) for zl in range(NZL) for core in range(NCORE)]
+
+
+def near_shift(by):
+    return [
+        (zl * NCORE + core, (zl // NEAR * NEAR + (zl + by) % NEAR) * NCORE + core)
+        for zl in range(NZL)
+        for core in range(NCORE)
+    ]
 
 
 def x_shift(by):
@@ -92,17 +94,17 @@
     )(route, tiles)
 
 
-def contract_kernel(where, labels, own, near, left, right, far0, far1, arrived, keep, send, dense, a, b, total, loads, stores):
+def contract_kernel(where, labels, *refs):
+    parts, (arrived, keep, send, dense, a, total, loads, stores) = refs[:-8], refs[-8:]
     x, plane, zl, core = where[0], where[1], where[2], where[3]
-    step = near.shape[0]
+    step = parts[0].shape[0]
     per = step // NY
     groups = OUT_ROWS // GROUP
 
-    parts = [(0, near), (step, left), (2 * step, right), (3 * step, far0), (3 * step + far0.shape[0], far1)]
-    copies = [
-        pltpu.make_async_copy(ref, b.at[pl.ds(at, ref.shape[0])], loads.at[n]) for n, (at, ref) in enumerate(parts)
-    ]
-    copies.append(pltpu.make_async_copy(own, a, loads.at[len(parts)]))
+    copies, at = [], 0
+    for n, ref in enumerate(parts):
+        copies.append(pltpu.make_async_copy(ref, a.at[pl.ds(at, ref.shape[0])], loads.at[n]))
+        at += ref.shape[0]
     for copy in copies:
         copy.start()
 
@@ -130,23 +132,23 @@
             g = c * (per // GROUP) + i
             away = jnp.where(g // groups % NCORE == core, 0, 1)
             to = g // (groups * NCORE)
-            slot = to % NEAR * 2 + jnp.where(to // NEAR == zl // NEAR, 0, 1)
+            slot = (to + NEAR - zl % NEAR) % NEAR * 2 + jnp.where(to // NEAR == zl // NEAR, 0, 1)
             row = pl.multiple_of((slot * groups + g % groups) * GROUP, GROUP)
             total[away, pl.ds(row, GROUP), :] = block[i * GROUP : (i + 1) * GROUP]
 
-    def multiply(block, columns, side):
+    def multiply(block, shifts, side):
         product = jnp.dot(block, dense[...], preferred_element_type=jnp.float32)
-        for n, xx in enumerate(columns):
+        for n, by in enumerate(shifts):
             for y in range(NY):
                 row = n * step + y * per
-                store((xx * NZH + side) * NY + y, product[row : row + per])
+                store(((x + by) % NX * NZH + side) * NY + y, product[row : row + per])
 
     for copy in copies:
         copy.wait()
-    for n in range(0, NX, 2):
-        multiply(a[n * step : (n + 2) * step, :], (n, n + 1), plane)
-    multiply(b[: 2 * step, :], (x, (x + NX - 1) % NX), 1 - plane)
-    multiply(b[2 * step :, :], ((x + 1) % NX, (x + 2) % NX), 1 - plane)
+    for n, side in enumerate((plane, 1 - plane)):
+        for m, shifts in enumerate(((0, NX - 1), (1, 2))):
+            at = (n * NX + m * 2) * step
+            multiply(a[at : at + 2 * step, :], shifts, side)
     out = [pltpu.make_async_copy(total.at[k], ref, stores.at[k]) for k, ref in enumerate((keep, send))]
     for copy in out:
         copy.start()
@@ -154,27 +156,36 @@
         copy.wait()
 
 
-def contract(where, labels, own, near, left, right, far0, far1, arrived):
-    occ, mu_rows = own.shape[0] * NZH, own.shape[1]
+def contract(where, labels, parts, arrived):
+    step, mu_rows = parts[0].shape
+    occ = step * NX * NZH
     width = CB * arrived.shape[2]
     shape = jax.ShapeDtypeStruct((occ // NCORE, width), jnp.float32)
     return pl.pallas_call(
         contract_kernel,
         out_shape=(shape, shape),
-        in_specs=[SMEM] * 2 + [ANY] * 6 + [VMEM],
+        in_specs=[SMEM] * 2 + [ANY] * len(parts) + [VMEM],
         out_specs=(ANY, ANY),
         scratch_shapes=[
-            pltpu.VMEM((mu_rows, width), own.dtype),
-            pltpu.VMEM(own.shape, own.dtype),
-            pltpu.VMEM(own.shape, own.dtype),
+            pltpu.VMEM((mu_rows, width), parts[0].dtype),
+            pltpu.VMEM((occ, mu_rows), parts[0].dtype),
             pltpu.VMEM((NCORE, *shape.shape), jnp.float32),
-            pltpu.SemaphoreType.DMA((6,)),
+            pltpu.SemaphoreType.DMA((len(parts),)),
             pltpu.SemaphoreType.DMA((NCORE,)),
         ],
         compiler_params=pltpu.CompilerParams(vmem_limit_bytes=56 << 20),
         cost_estimate=pl.CostEstimate(flops=2 * occ * mu_rows * width, bytes_accessed=12 << 20, transcendentals=0),
         name="contract",
-    )(where, labels, own, near, left, right, far0, far1, arrived)
+    )(where, labels, *parts, arrived)
+
+
+def beside(near):
+    return lax.ppermute(near, "col", x_shift(1)), lax.ppermute(near, "col", x_shift(-1))
+
+
+def across(left, right):
+    cut = left.shape[0] // 2
+    return lax.ppermute(left[:cut], "col", x_shift(1)), lax.ppermute(right[cut:], "col", x_shift(-1))
 
 
 def per_device(tiles, dest_col, mu_block, col_block, coeff):
@@ -184,31 +195,28 @@
     where = jnp.stack([here // (NZH * NY), here // NY % NZH, row // NCORE, row % NCORE]).astype(jnp.int32)
 
     mine = coeff.T
-    padded = jnp.pad(mine, ((0, WIDE - per), (0, 0)))
-    own = lax.all_gather(padded, "col", axis=0, tiled=True, axis_index_groups=Y_GROUPS)
-    own = own.reshape(NY, WIDE, mu_rows)[:, :per].reshape(NY * per, mu_rows)
-    theirs = lax.ppermute(mine, "col", PLANE_SWAP)
+    padded = jnp.pad(lax.ppermute(mine, "col", PLANE_SWAP), ((0, WIDE - per), (0, 0)))
+    theirs = lax.all_gather(padded, "col", axis=0, tiled=True, axis_index_groups=Y_GROUPS)
+    theirs = theirs.reshape(NY, WIDE, mu_rows)[:, :per].reshape(NY * per, mu_rows)
+    own = lax.all_gather(mine, "col", axis=0, tiled=True, axis_index_groups=Y_GROUPS)
+    left, right = beside(own)
     route = dest_col.reshape(held) * CELLS + mu_block.reshape(held) * CB + col_block.reshape(held)
     outgoing = pack(tiles.reshape(held, rows, cols), route)
-    near = lax.all_gather(theirs, "col", axis=0, tiled=True, axis_index_groups=Y_GROUPS)
-    outgoing, own, near = lax.optimization_barrier((outgoing, own, near))
+    outgoing, theirs, left, right = lax.optimization_barrier((outgoing, theirs, left, right))
     arrived = lax.all_to_all(outgoing, "col", split_axis=0, concat_axis=0, tiled=True)
 
-    own = lax.all_gather(own, "col", axis=0, tiled=True, axis_index_groups=X_GROUPS)
-    left = lax.ppermute(near, "col", x_shift(1))
-    right = lax.ppermute(near, "col", x_shift(-1))
-    cut = near.shape[0] // 2
-    far0 = lax.ppermute(left[:cut], "col", x_shift(1))
-    far1 = lax.ppermute(right[cut:], "col", x_shift(-1))
+    parts = [own, left, right, *across(left, right)]
+    left, right = beside(theirs)
+    parts += [theirs, left, right, *across(left, right)]
 
     labels = arrived[:, CAP * rows, :CAP].astype(jnp.int32)
-    keep, send = contract(where, labels, own, near, left, right, far0, far1, arrived)
+    keep, send = contract(where, labels, parts, arrived)
     share = keep + lax.ppermute(send, "row", CORE_SWAP)
-    share = lax.all_to_all(
-        share.reshape(NEAR, 2 * OUT_ROWS, -1), "row", split_axis=0, concat_axis=0, tiled=True, axis_index_groups=NEAR_GROUPS
-    )
-    away = jnp.sum(share[:, OUT_ROWS:], axis=0)
-    result = jnp.sum(share[:, :OUT_ROWS], axis=0) + lax.ppermute(away, "row", FAR_SWAP)
+    share = share.reshape(NEAR, 2 * OUT_ROWS, -1)
+    here, *others = [share[0]] + [lax.ppermute(share[by], "row", near_shift(by)) for by in range(1, NEAR)]
+    away = sum((part[OUT_ROWS:] for part in others), here[OUT_ROWS:])
+    result = sum((part[:OUT_ROWS] for part in others), here[:OUT_ROWS])
+    result = result + lax.ppermute(away, "row", FAR_SWAP)
     return result.astype(jnp.bfloat16)
 
 

time: 246 us -> 262 us (1.065); the launches traced: 244 us -> 257 us
  starting transfers between devices: 54.3 us -> 97.1 us
  blocking collectives: 64.9 us -> 28 us
  waiting for transfers between devices: 84.8 us -> 88.4 us
  local copies, waits for them, and re-layouts: 4.95 us -> 8.51 us
    ppermute x6 -> x12, starting transfers between devices: 35.9 us -> 78.4 us  [the longest x2 28.6 us: per_device(): lax.ppermute(share[by], 'row', near_shift(by))]
    all_to_all x1 -> x0, blocking collectives: 36.4 us -> none  [per_device(): lax.all_to_all(share.reshape(NEAR, 2 * OUT_ROWS, -1), 'row', split_axis=0...]
    all_to_all x1, waiting for transfers between devices: 0.01 us -> 7.77 us  [per_device(): lax.all_to_all(outgoing, 'col', split_axis=0, concat_axis=0, tiled=True)]
    ppermute x6 -> x12, waiting for transfers between devices: 74.1 us -> 67.1 us  [the longest x2 25.1 us: beside(): lax.ppermute(near, 'col', x_shift(-1))]
    all_gather x1, waiting for transfers between devices: 3.7 us -> 9.86 us  [per_device(): lax.all_gather(padded, 'col', axis=0, tiled=True, axis_index_groups=Y_GRO...]
    slice x3 -> x6, local copies, waits for them, and re-layouts: 2.15 us -> 5.84 us  [the longest x2 2.61 us: across(): right[cut:]]
    all_gather x1 -> x0, waiting for transfers between devices: 2.68 us -> none  [per_device(): lax.all_gather(own, 'col', axis=0, tiled=True, axis_index_groups=X_GROUPS)]
  transfers between devices with their start and end apart: 10 -> 15, of which waited for: 7 -> 9; matrix products, arithmetic and copies ran while one was open for 1% -> 3% of each run, Pallas kernels for 2% -> 1%
where the time goes in v7:
time: 262 us; the launch traced here: 257 us
  starting transfers between devices  97.1 us (37%)
  waiting for transfers between devices  88.4 us (34%)
  blocking collectives  28 us (11%)
  Pallas kernels  16.4 us (6%)
  between operations  13.7 us (5%)
  local copies, waits for them, and re-layouts  8.51 us (3%)
  other arithmetic  4.6 us (2%)
    ppermute x2, starting transfers between devices, per_device(): lax.ppermute(share[by], 'row', near_shift(by))  28.6 us
    all_gather x1, blocking collectives, per_device(): lax.all_gather(mine, 'col', axis=0, tiled=True, axis_index_groups=Y_GROUPS)  28 us
    ppermute x2, waiting for transfers between devices, beside(): lax.ppermute(near, 'col', x_shift(-1))  25.1 us
    ppermute x2, waiting for transfers between devices, per_device(): lax.ppermute(share[by], 'row', near_shift(by))  20.8 us
    ppermute x1, waiting for transfers between devices, per_device(): result = result + lax.ppermute(away, 'row', FAR_SWAP)  17.4 us
    all_to_all x1, starting transfers between devices, per_device(): lax.all_to_all(outgoing, 'col', split_axis=0, concat_axis=0, tiled=True)  16.8 us
    ppermute x1, starting transfers between devices, per_device(): lax.ppermute(mine, 'col', PLANE_SWAP)  15.3 us
    pallas_call x1, Pallas kernels, contract(): pl.pallas_call(contract_kernel, out_shape=(shape, shape), in_specs=[SMEM]...  12.7 us
  transfers between devices with their start and end apart: 15, of which 9 were waited for; matrix products, arithmetic and copies ran while one was open for 3% of the time, Pallas kernels for 1%

profile of v7, /device:TPU:6, one launch (start us, length us, event | category | flops | bytes accessed | tf_op | source)
XLA Modules:
  0.0 256.7 jit_solution(13262445059825915723)
XLA Ops:
  6.5 0.0 copy-start
  6.5 0.0 all-gather.2.cloned.1.call-start
  6.5 15.3 %collective-permute-start = (bf16[24,2048]{1,0:T(8,128)(2,1)}, bf16[24,2048]{1,0:T(8,128)(2,1)S(1)}, u32[]{:S(2)}, u32[]{:S(2)}) collective-permute-start(bf16[24,2048]{1,0:T(8,128)(2,1)} %bitcast.22), channel_id=1, source_target_pairs={{0,8},{1,9},{2,10},{3,11},{4,12},{5,13},{6,14},{7,15},{8,0},{9,1},... | collective-permute-start | bytes 294920 | tf_op jit(solution)/shard_map/ppermute | solution.py:198
  21.8 3.2 %collective-permute-done = bf16[24,2048]{1,0:T(8,128)(2,1)S(1)} collective-permute-done((bf16[24,2048]{1,0:T(8,128)(2,1)}, bf16[24,2048]{1,0:T(8,128)(2,1)S(1)}, u32[]{:S(2)}, u32[]{:S(2)}) %collective-permute-start) | collective-permute-done | bytes 98336 | tf_op jit(solution)/shard_map/ppermute | solution.py:198
  25.0 0.7 pad.4
  25.7 0.0 all-gather.2.cloned.1.call-update
  25.7 28.0 %all_gather.7.refs_0_ = bf16[192,2048]{1,0:T(8,128)(2,1)S(1)} all-gather(bf16[24,2048]{1,0:T(8,128)(2,1)} %bitcast.23), channel_id=1, replica_groups={{0,1,2,3,4,5,6,7},{8,9,10,11,12,13,14,15},{16,17,18,19,20,21,22,23},{24..., dimensions={0}, use_global_device_ids=true | all-gather | bytes 884736 | tf_op jit(solution)/shard_map/all_gather | solution.py:201
  53.7 0.0 copy-start.2
  53.7 2.7 %collective-permute-start.2 = (bf16[192,2048]{1,0:T(8,128)(2,1)S(1)}, bf16[192,2048]{1,0:T(8,128)(2,1)S(1)}, u32[]{:S(2)}, u32[]{:S(2)}) collective-permute-start(bf16[192,2048]{1,0:T(8,128)(2,1)S(1)} %all_gather.7.refs_0_), channel_id=1, source_target_pairs={{0,48},{1,49},{2,50},{3,51},{4,52},{5,53},{6,54},{7,55},{8,56},{9,... | collective-permute-start | bytes 2359304 | tf_op jit(solution)/shard_map/ppermute | solution.py:183
  56.5 4.3 %collective-permute-start.1 = (bf16[192,2048]{1,0:T(8,128)(2,1)S(1)}, bf16[192,2048]{1,0:T(8,128)(2,1)S(1)}, u32[]{:S(2)}, u32[]{:S(2)}) collective-permute-start(bf16[192,2048]{1,0:T(8,128)(2,1)S(1)} %all_gather.7.refs_0_), channel_id=1, source_target_pairs={{0,16},{1,17},{2,18},{3,19},{4,20},{5,21},{6,22},{7,23},{8,24},{9,... | collective-permute-start | bytes 2359304 | tf_op jit(solution)/shard_map/ppermute | solution.py:183
  60.8 0.7 bitcast_add_fusion.route
  61.5 0.0 copy-done
  61.5 3.7 %pack.1 = bf16[64,144,128]{2,1,0:T(8,128)(2,1)} custom-call(s32[64]{0:T(128)S(1)} %bitcast_add_fusion.route, bf16[64,64,128]{2,1,0:T(8,128)(2,1)S(1)} %bitcast.17), custom_call_target="tpu_custom_call" | custom-call | bytes 4194304 | tf_op jit(solution)/shard_map/pack/pallas_call | solution.py:85
  65.2 0.0 copy-done.2
  65.2 9.9 %all-gather.2.cloned.1.call-done = bf16[256,2048]{1,0:T(8,128)(2,1)} async-done(((bf16[32,2048]{1,0:T(8,128)(2,1)}), bf16[256,2048]{1,0:T(8,128)(2,1)}) %all-gather.2.cloned.1.call-update) | async-done | bytes 1048592 | tf_op jit(solution)/shard_map/all_gather | solution.py:199
  75.0 2.1 slice.63
  77.1 0.0 collective-permute-done.2.refs_2_
  77.2 0.0 copy-start.4
  77.2 0.0 collective-permute-done.1.refs_1_
  77.2 0.0 copy-start.5
  77.2 0.9 copy-done.5
  78.1 0.0 copy-start.3
  78.1 0.3 copy-done.4
  78.4 16.8 %all-to-all-start = ((bf16[64,144,128]{2,1,0:T(8,128)(2,1)}), bf16[64,144,128]{2,1,0:T(8,128)(2,1)S(1)}, u32[]{:S(2)}, u32[]{:S(2)}) async-start(bf16[64,144,128]{2,1,0:T(8,128)(2,1)} %pack.1), calls=%async_computation | async-start | bytes 4718592 | tf_op jit(solution)/shard_map/all_to_all | solution.py:206
  95.2 0.0 copy-done.3
  95.2 2.7 %collective-permute-start.6 = (bf16[192,2048]{1,0:T(8,128)(2,1)S(1)}, bf16[192,2048]{1,0:T(8,128)(2,1)S(1)}, u32[]{:S(2)}, u32[]{:S(2)}) collective-permute-start(bf16[192,2048]{1,0:T(8,128)(2,1)S(1)} %bitcast.19), channel_id=1, source_target_pairs={{0,48},{1,49},{2,50},{3,51},{4,52},{5,53},{6,54},{7,55},{8,56},{9,... | collective-permute-start | bytes 2359304 | tf_op jit(solution)/shard_map/ppermute | solution.py:183
  97.9 4.4 %collective-permute-start.5 = (bf16[192,2048]{1,0:T(8,128)(2,1)S(1)}, bf16[192,2048]{1,0:T(8,128)(2,1)S(1)}, u32[]{:S(2)}, u32[]{:S(2)}) collective-permute-start(bf16[192,2048]{1,0:T(8,128)(2,1)S(1)} %bitcast.20), channel_id=1, source_target_pairs={{0,16},{1,17},{2,18},{3,19},{4,20},{5,21},{6,22},{7,23},{8,24},{9,... | collective-permute-start | bytes 2359304 | tf_op jit(solution)/shard_map/ppermute | solution.py:183
  102.3 1.0 slice.51
  103.3 1.8 slice.52
  105.1 1.9 collective-permute-start.4
  107.0 5.1 %collective-permute-start.3 = (bf16[96,2048]{1,0:T(8,128)(2,1)S(1)}, bf16[96,2048]{1,0:T(8,128)(2,1)}, u32[]{:S(2)}, u32[]{:S(2)}) collective-permute-start(bf16[96,2048]{1,0:T(8,128)(2,1)S(1)} %slice.51), channel_id=1, source_target_pairs={{0,16},{1,17},{2,18},{3,19},{4,20},{5,21},{6,22},{7,23},{8,24},{9,... | collective-permute-start | bytes 1179656 | tf_op jit(solution)/shard_map/ppermute | solution.py:188
  112.2 25.1 %collective-permute-done.6.refs_7_ = bf16[192,2048]{1,0:T(8,128)(2,1)S(1)} collective-permute-done((bf16[192,2048]{1,0:T(8,128)(2,1)S(1)}, bf16[192,2048]{1,0:T(8,128)(2,1)S(1)}, u32[]{:S(2)}, u32[]{:S(2)}) %collective-permute-start.6) | collective-permute-done | bytes 786464 | tf_op jit(solution)/shard_map/ppermute | solution.py:183
  137.2 0.0 copy-start.6
  137.2 0.8 slice.66
  138.0 1.9 collective-permute-start.8
  140.0 0.0 collective-permute-done.5.refs_6_
  140.0 0.0 copy-start.7
  140.0 5.1 %collective-permute-start.7 = (bf16[96,2048]{1,0:T(8,128)(2,1)S(1)}, bf16[96,2048]{1,0:T(8,128)(2,1)S(1)}, u32[]{:S(2)}, u32[]{:S(2)}) collective-permute-start(bf16[96,2048]{1,0:T(8,128)(2,1)S(1)} %slice.65), channel_id=1, source_target_pairs={{0,16},{1,17},{2,18},{3,19},{4,20},{5,21},{6,22},{7,23},{8,24},{9,... | collective-permute-start | bytes 1179656 | tf_op jit(solution)/shard_map/ppermute | solution.py:188
  145.2 0.0 copy-done.6
  145.2 0.0 copy-done.7
  145.2 0.6 pad_add_fusion.where
  145.9 7.8 %all-to-all-done.refs_10_ = bf16[64,144,128]{2,1,0:T(8,128)(2,1)S(1)} async-done(((bf16[64,144,128]{2,1,0:T(8,128)(2,1)}), bf16[64,144,128]{2,1,0:T(8,128)(2,1)S(1)}, u32[]{:S(2)}, u32[]{:S(2)}) %all-to-all-start) | async-done | bytes 2359328 | tf_op jit(solution)/shard_map/all_to_all | solution.py:206
  153.6 0.0 copy-start.1
  153.7 0.7 slice_convert_fusion
  154.4 0.0 collective-permute-done.4.refs_4_
  154.4 0.0 collective-permute-done.3.refs_3_
  154.4 0.0 collective-permute-done.8.refs_9_
  154.4 0.8 collective-permute-done.7.refs_8_
  155.1 0.0 copy-start.8
  155.1 0.0 copy-done.1
  155.1 0.7 copy-done.8
  155.9 12.7 %contract.1 = (f32[768,512]{1,0:T(8,128)}, f32[768,512]{1,0:T(8,128)}) custom-call(s32[4]{0:T(128)} %pad_add_fusion.where, s32[64,2]{1,0:T(8,128)} %bitcast.24, bf16[192,2048]{1,0:T(8,128)(2,1)} %copy-done.2, bf16[192,2048]{1,0:T(8,128)(2,1)} %copy-done.5, bf16[192,2048]{1,0:T(8,128)(2,1)} %copy-done.4, bf16[96,2048]{1,0:T(8,128)(2,1)} %collective-permute-done.3.refs_3_, ...), custom_call_target="tpu_custom_call" | custom-call | flops 3221225472 | bytes 12582912 | tf_op jit(solution)/shard_map/contract/pallas_call | solution.py:164
  168.6 1.9 collective-permute-start.9
  170.6 3.6 %collective-permute-done.9 = f32[768,512]{1,0:T(8,128)S(1)} collective-permute-done((f32[768,512]{1,0:T(8,128)}, f32[768,512]{1,0:T(8,128)S(1)}, u32[]{:S(2)}, u32[]{:S(2)}) %collective-permute-start.9) | collective-permute-done | bytes 1572896 | tf_op jit(solution)/shard_map/ppermute | solution.py:214
  174.2 1.8 add.40
  175.9 0.1 fusion.2
  176.0 26.7 %collective-permute-start.10 = (f32[256,512]{1,0:T(8,128)S(1)}, f32[256,512]{1,0:T(8,128)S(1)}, u32[]{:S(2)}, u32[]{:S(2)}) collective-permute-start(f32[256,512]{1,0:T(8,128)S(1)} %get-tuple-element.17), channel_id=1, source_target_pairs={{0,128},{64,192},{128,256},{192,320},{256,0},{320,64},{384,512},{4... | collective-permute-start | bytes 1572872 | tf_op jit(solution)/shard_map/ppermute | solution.py:216
  202.7 1.9 collective-permute-start.11
  204.6 10.3 %collective-permute-done.10 = f32[256,512]{1,0:T(8,128)S(1)} collective-permute-done((f32[256,512]{1,0:T(8,128)S(1)}, f32[256,512]{1,0:T(8,128)S(1)}, u32[]{:S(2)}, u32[]{:S(2)}) %collective-permute-start.10) | collective-permute-done | bytes 524320 | tf_op jit(solution)/shard_map/ppermute | solution.py:216
  215.0 10.4 %collective-permute-done.11 = f32[256,512]{1,0:T(8,128)S(1)} collective-permute-done((f32[256,512]{1,0:T(8,128)S(1)}, f32[256,512]{1,0:T(8,128)S(1)}, u32[]{:S(2)}, u32[]{:S(2)}) %collective-permute-start.11) | collective-permute-done | bytes 524320 | tf_op jit(solution)/shard_map/ppermute | solution.py:216
  225.4 0.1 slice_add_fusion
  225.5 6.3 %collective-permute-start.12 = (f32[128,512]{1,0:T(8,128)S(1)}, f32[128,512]{1,0:T(8,128)S(1)}, u32[]{:S(2)}, u32[]{:S(2)}) collective-permute-start(f32[128,512]{1,0:T(8,128)S(1)} %slice_add_fusion), channel_id=1, source_target_pairs={{0,384},{64,448},{128,512},{192,576},{256,640},{320,704},{384,0},{... | collective-permute-start | bytes 786440 | tf_op jit(solution)/shard_map/ppermute | solution.py:219
  231.8 17.4 %collective-permute-done.12 = f32[128,512]{1,0:T(8,128)S(1)} collective-permute-done((f32[128,512]{1,0:T(8,128)S(1)}, f32[128,512]{1,0:T(8,128)S(1)}, u32[]{:S(2)}, u32[]{:S(2)}) %collective-permute-start.12) | collective-permute-done | bytes 262176 | tf_op jit(solution)/shard_map/ppermute | solution.py:219
  249.1 0.7 fusion.1
  (1 shorter events, 0.0 us)
Async XLA Ops:
  6.5 55.0 %copy-start = (bf16[1,1,64,64,128]{4,3,2,1,0:T(8,128)(2,1)S(1)}, bf16[1,1,64,64,128]{4,3,2,1,0:T(8,128)(2,1)}, u32[]{:S(2)}) copy-start(bf16[1,1,64,64,128]{4,3,2,1,0:T(8,128)(2,1)} %param.5) | copy-start | bytes 3145732
  6.5 68.5 %all-gather.2.cloned.1.call-start = ((), (), s32[]{:S(2)}) async-start(), calls=%async_computation.1 | async-start | bytes 1179648 | tf_op jit(solution)/shard_map/all_gather | solution.py:199
  6.5 18.5 %collective-permute-start = (bf16[24,2048]{1,0:T(8,128)(2,1)}, bf16[24,2048]{1,0:T(8,128)(2,1)S(1)}, u32[]{:S(2)}, u32[]{:S(2)}) collective-permute-start(bf16[24,2048]{1,0:T(8,128)(2,1)} %bitcast.22), channel_id=1, source_target_pairs={{0,8},{1,9},{2,10},{3,11},{4,12},{5,13},{6,14},{7,15},{8,0},{9,1},... | collective-permute-start | bytes 294920 | tf_op jit(solution)/shard_map/ppermute | solution.py:198
  53.7 11.5 %copy-start.2 = (bf16[192,2048]{1,0:T(8,128)(2,1)}, bf16[192,2048]{1,0:T(8,128)(2,1)S(1)}, u32[]{:S(2)}) copy-start(bf16[192,2048]{1,0:T(8,128)(2,1)S(1)} %all_gather.7.refs_0_) | copy-start | bytes 2359300
  53.7 23.4 %collective-permute-start.2 = (bf16[192,2048]{1,0:T(8,128)(2,1)S(1)}, bf16[192,2048]{1,0:T(8,128)(2,1)S(1)}, u32[]{:S(2)}, u32[]{:S(2)}) collective-permute-start(bf16[192,2048]{1,0:T(8,128)(2,1)S(1)} %all_gather.7.refs_0_), channel_id=1, source_target_pairs={{0,48},{1,49},{2,50},{3,51},{4,52},{5,53},{6,54},{7,55},{8,56},{9,... | collective-permute-start | bytes 2359304 | tf_op jit(solution)/shard_map/ppermute | solution.py:183
  56.5 20.7 %collective-permute-start.1 = (bf16[192,2048]{1,0:T(8,128)(2,1)S(1)}, bf16[192,2048]{1,0:T(8,128)(2,1)S(1)}, u32[]{:S(2)}, u32[]{:S(2)}) collective-permute-start(bf16[192,2048]{1,0:T(8,128)(2,1)S(1)} %all_gather.7.refs_0_), channel_id=1, source_target_pairs={{0,16},{1,17},{2,18},{3,19},{4,20},{5,21},{6,22},{7,23},{8,24},{9,... | collective-permute-start | bytes 2359304 | tf_op jit(solution)/shard_map/ppermute | solution.py:183
  77.2 1.3 copy-start.4
  77.2 0.9 copy-start.5
  78.1 17.1 %copy-start.3 = (bf16[8,24,2048]{2,1,0:T(8,128)(2,1)S(1)}, bf16[8,24,2048]{2,1,0:T(8,128)(2,1)}, u32[]{:S(2)}) copy-start(bf16[8,24,2048]{2,1,0:T(8,128)(2,1)} %slice.63) | copy-start | bytes 2359300
  78.4 75.2 %all-to-all-start = ((bf16[64,144,128]{2,1,0:T(8,128)(2,1)}), bf16[64,144,128]{2,1,0:T(8,128)(2,1)S(1)}, u32[]{:S(2)}, u32[]{:S(2)}) async-start(bf16[64,144,128]{2,1,0:T(8,128)(2,1)} %pack.1), calls=%async_computation | async-start | bytes 4718592 | tf_op jit(solution)/shard_map/all_to_all | solution.py:206
  95.2 42.0 %collective-permute-start.6 = (bf16[192,2048]{1,0:T(8,128)(2,1)S(1)}, bf16[192,2048]{1,0:T(8,128)(2,1)S(1)}, u32[]{:S(2)}, u32[]{:S(2)}) collective-permute-start(bf16[192,2048]{1,0:T(8,128)(2,1)S(1)} %bitcast.19), channel_id=1, source_target_pairs={{0,48},{1,49},{2,50},{3,51},{4,52},{5,53},{6,54},{7,55},{8,56},{9,... | collective-permute-start | bytes 2359304 | tf_op jit(solution)/shard_map/ppermute | solution.py:183
  97.9 42.1 %collective-permute-start.5 = (bf16[192,2048]{1,0:T(8,128)(2,1)S(1)}, bf16[192,2048]{1,0:T(8,128)(2,1)S(1)}, u32[]{:S(2)}, u32[]{:S(2)}) collective-permute-start(bf16[192,2048]{1,0:T(8,128)(2,1)S(1)} %bitcast.20), channel_id=1, source_target_pairs={{0,16},{1,17},{2,18},{3,19},{4,20},{5,21},{6,22},{7,23},{8,24},{9,... | collective-permute-start | bytes 2359304 | tf_op jit(solution)/shard_map/ppermute | solution.py:183
  105.1 49.3 %collective-permute-start.4 = (bf16[96,2048]{1,0:T(8,128)(2,1)}, bf16[96,2048]{1,0:T(8,128)(2,1)}, u32[]{:S(2)}, u32[]{:S(2)}) collective-permute-start(bf16[96,2048]{1,0:T(8,128)(2,1)} %slice.52), channel_id=1, source_target_pairs={{0,48},{1,49},{2,50},{3,51},{4,52},{5,53},{6,54},{7,55},{8,56},{9,... | collective-permute-start | bytes 1179656 | tf_op jit(solution)/shard_map/ppermute | solution.py:188
  107.0 47.4 %collective-permute-start.3 = (bf16[96,2048]{1,0:T(8,128)(2,1)S(1)}, bf16[96,2048]{1,0:T(8,128)(2,1)}, u32[]{:S(2)}, u32[]{:S(2)}) collective-permute-start(bf16[96,2048]{1,0:T(8,128)(2,1)S(1)} %slice.51), channel_id=1, source_target_pairs={{0,16},{1,17},{2,18},{3,19},{4,20},{5,21},{6,22},{7,23},{8,24},{9,... | collective-permute-start | bytes 1179656 | tf_op jit(solution)/shard_map/ppermute | solution.py:188
  137.2 7.9 %copy-start.6 = (bf16[192,2048]{1,0:T(8,128)(2,1)}, bf16[192,2048]{1,0:T(8,128)(2,1)S(1)}, u32[]{:S(2)}) copy-start(bf16[192,2048]{1,0:T(8,128)(2,1)S(1)} %collective-permute-done.6.refs_7_) | copy-start | bytes 2359300
  138.0 16.3 %collective-permute-start.8 = (bf16[96,2048]{1,0:T(8,128)(2,1)}, bf16[96,2048]{1,0:T(8,128)(2,1)}, u32[]{:S(2)}, u32[]{:S(2)}) collective-permute-start(bf16[96,2048]{1,0:T(8,128)(2,1)} %slice.66), channel_id=1, source_target_pairs={{0,48},{1,49},{2,50},{3,51},{4,52},{5,53},{6,54},{7,55},{8,56},{9,... | collective-permute-start | bytes 1179656 | tf_op jit(solution)/shard_map/ppermute | solution.py:188
  140.0 5.2 %copy-start.7 = (bf16[192,2048]{1,0:T(8,128)(2,1)}, bf16[192,2048]{1,0:T(8,128)(2,1)S(1)}, u32[]{:S(2)}) copy-start(bf16[192,2048]{1,0:T(8,128)(2,1)S(1)} %collective-permute-done.5.refs_6_) | copy-start | bytes 2359300
  140.0 15.1 %collective-permute-start.7 = (bf16[96,2048]{1,0:T(8,128)(2,1)S(1)}, bf16[96,2048]{1,0:T(8,128)(2,1)S(1)}, u32[]{:S(2)}, u32[]{:S(2)}) collective-permute-start(bf16[96,2048]{1,0:T(8,128)(2,1)S(1)} %slice.65), channel_id=1, source_target_pairs={{0,16},{1,17},{2,18},{3,19},{4,20},{5,21},{6,22},{7,23},{8,24},{9,... | collective-permute-start | bytes 1179656 | tf_op jit(solution)/shard_map/ppermute | solution.py:188
  153.6 1.5 copy-start.1
  155.1 0.8 copy-start.8
  168.6 5.5 %collective-permute-start.9 = (f32[768,512]{1,0:T(8,128)}, f32[768,512]{1,0:T(8,128)S(1)}, u32[]{:S(2)}, u32[]{:S(2)}) collective-permute-start(f32[768,512]{1,0:T(8,128)} %get-tuple-element.16), channel_id=1, source_target_pairs={{0,64},{64,0},{128,192},{192,128},{256,320},{320,256},{384,448},{4... | collective-permute-start | bytes 4718600 | tf_op jit(solution)/shard_map/ppermute | solution.py:214
  176.0 39.0 %collective-permute-start.10 = (f32[256,512]{1,0:T(8,128)S(1)}, f32[256,512]{1,0:T(8,128)S(1)}, u32[]{:S(2)}, u32[]{:S(2)}) collective-permute-start(f32[256,512]{1,0:T(8,128)S(1)} %get-tuple-element.17), channel_id=1, source_target_pairs={{0,128},{64,192},{128,256},{192,320},{256,0},{320,64},{384,512},{4... | collective-permute-start | bytes 1572872 | tf_op jit(solution)/shard_map/ppermute | solution.py:216
  202.7 22.7 %collective-permute-start.11 = (f32[256,512]{1,0:T(8,128)S(1)}, f32[256,512]{1,0:T(8,128)S(1)}, u32[]{:S(2)}, u32[]{:S(2)}) collective-permute-start(f32[256,512]{1,0:T(8,128)S(1)} %get-tuple-element.18), channel_id=1, source_target_pairs={{0,256},{64,320},{128,0},{192,64},{256,128},{320,192},{384,640},{4... | collective-permute-start | bytes 1572872 | tf_op jit(solution)/shard_map/ppermute | solution.py:216
  225.5 23.7 %collective-permute-start.12 = (f32[128,512]{1,0:T(8,128)S(1)}, f32[128,512]{1,0:T(8,128)S(1)}, u32[]{:S(2)}, u32[]{:S(2)}) collective-permute-start(f32[128,512]{1,0:T(8,128)S(1)} %slice_add_fusion), channel_id=1, source_target_pairs={{0,384},{64,448},{128,512},{192,576},{256,640},{320,704},{384,0},{... | collective-permute-start | bytes 786440 | tf_op jit(solution)/shard_map/ppermute | solution.py:219
Sparse Core Ops, SparseCore 0:
  25.8 49.1 all-gather.1

commit v8 on v7

--- a/solution.py
+++ b/solution.py
@@ -27,6 +27,11 @@
 
 
 Y_GROUPS = [[column(x, zh, y) for y in range(NY)] for x in range(NX) for zh in range(NZH)]
+NEAR_GROUPS = [
+    [zl * NCORE + core for zl in range(half * NEAR, (half + 1) * NEAR)]
+    for half in range(NZL // NEAR)
+    for core in range(NCORE)
+]
 FAR_SWAP = [
     (zl * NCORE + core, (zl + NEAR) % NZL * NCORE + core) for zl in range(NZL) for core in range(NCORE)
 ]
@@ -34,14 +39,6 @@
     (column(x, zh, y), column(x, 1 - zh, y)) for x in range(NX) for zh in range(NZH) for y in range(NY)
 ]
 CORE_SWAP = [(zl * NCORE + core, zl * NCORE + 1 - core) for zl in range(NZL) for core in range(NCORE)]
-
-
-def near_shift(by):
-    return [
-        (zl * NCORE + core, (zl // NEAR * NEAR + (zl + by) % NEAR) * NCORE + core)
-        for zl in range(NZL)
-        for core in range(NCORE)
-    ]
 
 
 def x_shift(by):
@@ -132,7 +129,7 @@
             g = c * (per // GROUP) + i
             away = jnp.where(g // groups % NCORE == core, 0, 1)
             to = g // (groups * NCORE)
-            slot = (to + NEAR - zl % NEAR) % NEAR * 2 + jnp.where(to // NEAR == zl // NEAR, 0, 1)
+            slot = to % NEAR * 2 + jnp.where(to // NEAR == zl // NEAR, 0, 1)
             row = pl.multiple_of((slot * groups + g % groups) * GROUP, GROUP)
             total[away, pl.ds(row, GROUP), :] = block[i * GROUP : (i + 1) * GROUP]
 
@@ -195,28 +192,29 @@
     where = jnp.stack([here // (NZH * NY), here // NY % NZH, row // NCORE, row % NCORE]).astype(jnp.int32)
 
     mine = coeff.T
-    padded = jnp.pad(lax.ppermute(mine, "col", PLANE_SWAP), ((0, WIDE - per), (0, 0)))
+    theirs = lax.ppermute(mine, "col", PLANE_SWAP)
+    route = dest_col.reshape(held) * CELLS + mu_block.reshape(held) * CB + col_block.reshape(held)
+    outgoing = pack(tiles.reshape(held, rows, cols), route)
+    outgoing, mine, theirs = lax.optimization_barrier((outgoing, mine, theirs))
+    arrived = lax.all_to_all(outgoing, "col", split_axis=0, concat_axis=0, tiled=True)
+
+    padded = jnp.pad(theirs, ((0, WIDE - per), (0, 0)))
     theirs = lax.all_gather(padded, "col", axis=0, tiled=True, axis_index_groups=Y_GROUPS)
     theirs = theirs.reshape(NY, WIDE, mu_rows)[:, :per].reshape(NY * per, mu_rows)
     own = lax.all_gather(mine, "col", axis=0, tiled=True, axis_index_groups=Y_GROUPS)
-    left, right = beside(own)
-    route = dest_col.reshape(held) * CELLS + mu_block.reshape(held) * CB + col_block.reshape(held)
-    outgoing = pack(tiles.reshape(held, rows, cols), route)
-    outgoing, theirs, left, right = lax.optimization_barrier((outgoing, theirs, left, right))
-    arrived = lax.all_to_all(outgoing, "col", split_axis=0, concat_axis=0, tiled=True)
-
-    parts = [own, left, right, *across(left, right)]
-    left, right = beside(theirs)
-    parts += [theirs, left, right, *across(left, right)]
+    parts = []
+    for near in (own, theirs):
+        left, right = beside(near)
+        parts += [near, left, right, *across(left, right)]
 
     labels = arrived[:, CAP * rows, :CAP].astype(jnp.int32)
     keep, send = contract(where, labels, parts, arrived)
     share = keep + lax.ppermute(send, "row", CORE_SWAP)
-    share = share.reshape(NEAR, 2 * OUT_ROWS, -1)
-    here, *others = [share[0]] + [lax.ppermute(share[by], "row", near_shift(by)) for by in range(1, NEAR)]
-    away = sum((part[OUT_ROWS:] for part in others), here[OUT_ROWS:])
-    result = sum((part[:OUT_ROWS] for part in others), here[:OUT_ROWS])
-    result = result + lax.ppermute(away, "row", FAR_SWAP)
+    share = lax.all_to_all(
+        share.reshape(NEAR, 2 * OUT_ROWS, -1), "row", split_axis=0, concat_axis=0, tiled=True, axis_index_groups=NEAR_GROUPS
+    )
+    away = jnp.sum(share[:, OUT_ROWS:], axis=0)
+    result = jnp.sum(share[:, :OUT_ROWS], axis=0) + lax.ppermute(away, "row", FAR_SWAP)
     return result.astype(jnp.bfloat16)
 
 

time: 262 us -> 258 us (0.985)
  blocking collectives: 28 us -> 108 us
  waiting for transfers between devices: 88.4 us -> 37 us
  starting transfers between devices: 97.1 us -> 69.1 us
    all_gather x1, blocking collectives: 28 us -> 79.6 us  [per_device(): lax.all_gather(mine, 'col', axis=0, tiled=True, axis_index_groups=Y_GROUPS)]
    ppermute x4 -> x2, starting transfers between devices: 50.2 us -> 19.6 us  [the longest x1 15.1 us: per_device(): theirs = lax.ppermute(mine, 'col', PLANE_SWAP)]
    all_to_all x0 -> x1, blocking collectives: none -> 28.4 us  [per_device(): lax.all_to_all(share.reshape(NEAR, 2 * OUT_ROWS, -1), 'row', split_axis=0...]
    ppermute x4 -> x2, waiting for transfers between devices: 41.3 us -> 17.6 us  [the longest x1 17.6 us: per_device(): lax.ppermute(away, 'row', FAR_SWAP)]
    ppermute x2, waiting for transfers between devices: 25.1 us -> 11.9 us  [beside(): lax.ppermute(near, 'col', x_shift(-1))]
    all_gather x1, waiting for transfers between devices: 9.86 us -> 0.02 us  [per_device(): lax.all_gather(padded, 'col', axis=0, tiled=True, axis_index_groups=Y_GRO...]
    all_to_all x1, waiting for transfers between devices: 7.77 us -> 0.01 us  [per_device(): lax.all_to_all(outgoing, 'col', split_axis=0, concat_axis=0, tiled=True)]
  transfers between devices with their start and end apart: 15 -> 13, of which waited for: 9 -> 6; matrix products, arithmetic and copies ran while one was open for 3% -> 3% of each run, Pallas kernels for 1% -> 1%
where the time goes in v8:
time: 258 us; the launch traced here: 254 us
  blocking collectives  108 us (42%)
  starting transfers between devices  69.1 us (27%)
  waiting for transfers between devices  37 us (14%)
  Pallas kernels  16 us (6%)
  between operations  13.7 us (5%)
  local copies, waits for them, and re-layouts  5.98 us (2%)
  other arithmetic  4.58 us (2%)
    all_gather x1, blocking collectives, per_device(): lax.all_gather(mine, 'col', axis=0, tiled=True, axis_index_groups=Y_GROUPS)  79.6 us
    all_to_all x1, blocking collectives, per_device(): lax.all_to_all(share.reshape(NEAR, 2 * OUT_ROWS, -1), 'row', split_axis=0...  28.4 us
    all_to_all x1, starting transfers between devices, per_device(): lax.all_to_all(outgoing, 'col', split_axis=0, concat_axis=0, tiled=True)  19.3 us
    ppermute x1, waiting for transfers between devices, per_device(): lax.ppermute(away, 'row', FAR_SWAP)  17.6 us
    ppermute x1, starting transfers between devices, per_device(): theirs = lax.ppermute(mine, 'col', PLANE_SWAP)  15.1 us
    pallas_call x1, Pallas kernels, contract(): pl.pallas_call(contract_kernel, out_shape=(shape, shape), in_specs=[SMEM]...  12.3 us
    ppermute x2, waiting for transfers between devices, beside(): lax.ppermute(near, 'col', x_shift(-1))  11.9 us
    ppermute x2, starting transfers between devices, across(): lax.ppermute(left[:cut], 'col', x_shift(1))  10.3 us
  transfers between devices with their start and end apart: 13, of which 6 were waited for; matrix products, arithmetic and copies ran while one was open for 3% of the time, Pallas kernels for 1%

profile of v8, /device:TPU:6, one launch (start us, length us, event | category | flops | bytes accessed | tf_op | source)
XLA Modules:
  0.0 254.3 jit_solution(15986724635575417801)
XLA Ops:
  6.5 15.1 %collective-permute-start = (bf16[24,2048]{1,0:T(8,128)(2,1)}, bf16[24,2048]{1,0:T(8,128)(2,1)S(1)}, u32[]{:S(2)}, u32[]{:S(2)}) collective-permute-start(bf16[24,2048]{1,0:T(8,128)(2,1)} %bitcast.24), channel_id=1, source_target_pairs={{0,8},{1,9},{2,10},{3,11},{4,12},{5,13},{6,14},{7,15},{8,0},{9,1},... | collective-permute-start | bytes 294920 | tf_op jit(solution)/shard_map/ppermute | solution.py:195
  21.7 0.7 bitcast_add_fusion.route
  22.4 0.0 copy-start
  22.4 1.2 copy-done
  23.6 3.7 %pack.1 = bf16[64,144,128]{2,1,0:T(8,128)(2,1)} custom-call(s32[64]{0:T(128)S(1)} %bitcast_add_fusion.route, bf16[64,64,128]{2,1,0:T(8,128)(2,1)S(1)} %bitcast.18), custom_call_target="tpu_custom_call" | custom-call | bytes 4194304 | tf_op jit(solution)/shard_map/pack/pallas_call | solution.py:82
  27.3 0.0 copy-start.6
  27.3 0.0 collective-permute-done
  27.3 19.3 %all-to-all-start = ((bf16[64,144,128]{2,1,0:T(8,128)(2,1)}), bf16[64,144,128]{2,1,0:T(8,128)(2,1)S(1)}, u32[]{:S(2)}, u32[]{:S(2)}) async-start(bf16[64,144,128]{2,1,0:T(8,128)(2,1)} %pack.1), calls=%async_computation | async-start | bytes 4718592 | tf_op jit(solution)/shard_map/all_to_all | solution.py:199
  46.6 0.0 all-gather.2.cloned.1.call-start
  46.6 0.7 pad.4
  47.3 0.0 all-gather.2.cloned.1.call-update
  47.3 0.0 copy-done.6
  47.3 79.6 %all_gather.6.refs_0_ = bf16[192,2048]{1,0:T(8,128)(2,1)S(1)} all-gather(bf16[24,2048]{1,0:T(8,128)(2,1)S(1)} %bitcast.25), channel_id=1, replica_groups={{0,1,2,3,4,5,6,7},{8,9,10,11,12,13,14,15},{16,17,18,19,20,21,22,23},{24..., dimensions={0}, use_global_device_ids=true | all-gather | bytes 884736 | tf_op jit(solution)/shard_map/all_gather | solution.py:204
  126.9 0.0 copy-start.2
  126.9 2.7 %collective-permute-start.2 = (bf16[192,2048]{1,0:T(8,128)(2,1)S(1)}, bf16[192,2048]{1,0:T(8,128)(2,1)}, u32[]{:S(2)}, u32[]{:S(2)}) collective-permute-start(bf16[192,2048]{1,0:T(8,128)(2,1)S(1)} %all_gather.6.refs_0_), channel_id=1, source_target_pairs={{0,48},{1,49},{2,50},{3,51},{4,52},{5,53},{6,54},{7,55},{8,56},{9,... | collective-permute-start | bytes 2359304 | tf_op jit(solution)/shard_map/ppermute | solution.py:180
  129.6 4.4 %collective-permute-start.1 = (bf16[192,2048]{1,0:T(8,128)(2,1)S(1)}, bf16[192,2048]{1,0:T(8,128)(2,1)}, u32[]{:S(2)}, u32[]{:S(2)}) collective-permute-start(bf16[192,2048]{1,0:T(8,128)(2,1)S(1)} %all_gather.6.refs_0_), channel_id=1, source_target_pairs={{0,16},{1,17},{2,18},{3,19},{4,20},{5,21},{6,22},{7,23},{8,24},{9,... | collective-permute-start | bytes 2359304 | tf_op jit(solution)/shard_map/ppermute | solution.py:180
  134.0 0.0 all-gather.2.cloned.1.call-done
  134.0 1.2 slice.35
  135.2 0.0 copy-start.3
  135.2 1.9 collective-permute-start.6
  137.2 5.1 %collective-permute-start.5 = (bf16[192,2048]{1,0:T(8,128)(2,1)S(1)}, bf16[192,2048]{1,0:T(8,128)(2,1)S(1)}, u32[]{:S(2)}, u32[]{:S(2)}) collective-permute-start(bf16[192,2048]{1,0:T(8,128)(2,1)S(1)} %bitcast.21), channel_id=1, source_target_pairs={{0,16},{1,17},{2,18},{3,19},{4,20},{5,21},{6,22},{7,23},{8,24},{9,... | collective-permute-start | bytes 2359304 | tf_op jit(solution)/shard_map/ppermute | solution.py:180
  142.3 8.3 %collective-permute-done.2.refs_2_ = bf16[192,2048]{1,0:T(8,128)(2,1)} collective-permute-done((bf16[192,2048]{1,0:T(8,128)(2,1)S(1)}, bf16[192,2048]{1,0:T(8,128)(2,1)}, u32[]{:S(2)}, u32[]{:S(2)}) %collective-permute-start.2) | collective-permute-done | bytes 786464 | tf_op jit(solution)/shard_map/ppermute | solution.py:180
  150.6 1.0 slice.34
  151.6 1.9 collective-permute-start.4
  153.6 0.0 collective-permute-done.1.refs_1_
  153.6 1.8 slice.33
  155.3 0.0 copy-done.2
  155.3 5.1 %collective-permute-start.3 = (bf16[96,2048]{1,0:T(8,128)(2,1)}, bf16[96,2048]{1,0:T(8,128)(2,1)}, u32[]{:S(2)}, u32[]{:S(2)}) collective-permute-start(bf16[96,2048]{1,0:T(8,128)(2,1)} %slice.33), channel_id=1, source_target_pairs={{0,16},{1,17},{2,18},{3,19},{4,20},{5,21},{6,22},{7,23},{8,24},{9,... | collective-permute-start | bytes 1179656 | tf_op jit(solution)/shard_map/ppermute | solution.py:185
  160.5 3.6 %collective-permute-done.6.refs_7_ = bf16[192,2048]{1,0:T(8,128)(2,1)S(1)} collective-permute-done((bf16[192,2048]{1,0:T(8,128)(2,1)S(1)}, bf16[192,2048]{1,0:T(8,128)(2,1)S(1)}, u32[]{:S(2)}, u32[]{:S(2)}) %collective-permute-start.6) | collective-permute-done | bytes 786464 | tf_op jit(solution)/shard_map/ppermute | solution.py:180
  164.1 0.0 copy-start.4
  164.1 1.9 collective-permute-start.8
  166.0 0.0 collective-permute-done.5.refs_6_
  166.0 0.0 copy-start.5
  166.1 0.0 copy-done.3
  166.1 5.1 %collective-permute-start.7 = (bf16[96,2048]{1,0:T(8,128)(2,1)S(1)}, bf16[96,2048]{1,0:T(8,128)(2,1)}, u32[]{:S(2)}, u32[]{:S(2)}) collective-permute-start(bf16[96,2048]{1,0:T(8,128)(2,1)S(1)} %slice.36), channel_id=1, source_target_pairs={{0,16},{1,17},{2,18},{3,19},{4,20},{5,21},{6,22},{7,23},{8,24},{9,... | collective-permute-start | bytes 1179656 | tf_op jit(solution)/shard_map/ppermute | solution.py:185
  171.2 0.0 copy-done.4
  171.3 0.0 copy-done.5
  171.3 0.6 pad_add_fusion.where
  171.9 0.0 all-to-all-done.refs_10_
  171.9 0.0 copy-start.1
  171.9 0.7 slice_convert_fusion
  172.6 0.0 collective-permute-done.4.refs_4_
  172.6 0.0 collective-permute-done.3.refs_3_
  172.6 2.5 collective-permute-done.8.refs_9_
  175.1 1.4 collective-permute-done.7.refs_8_
  176.5 0.0 copy-done.1
  176.5 12.3 %contract.1 = (f32[768,512]{1,0:T(8,128)}, f32[768,512]{1,0:T(8,128)}) custom-call(s32[4]{0:T(128)} %pad_add_fusion.where, s32[64,2]{1,0:T(8,128)} %bitcast.26, bf16[192,2048]{1,0:T(8,128)(2,1)} %copy-done.2, bf16[192,2048]{1,0:T(8,128)(2,1)} %collective-permute-done.1.refs_1_, bf16[192,2048]{1,0:T(8,128)(2,1)} %collective-permute-done.2.refs_2_, ...), custom_call_target="tpu_custom_call" | custom-call | flops 3221225472 | bytes 12582912 | tf_op jit(solution)/shard_map/contract/pallas_call | solution.py:161
  188.8 1.9 collective-permute-start.9
  190.8 3.6 %collective-permute-done.9 = f32[768,512]{1,0:T(8,128)S(1)} collective-permute-done((f32[768,512]{1,0:T(8,128)}, f32[768,512]{1,0:T(8,128)S(1)}, u32[]{:S(2)}, u32[]{:S(2)}) %collective-permute-start.9) | collective-permute-done | bytes 1572896 | tf_op jit(solution)/shard_map/ppermute | solution.py:212
  194.3 1.8 add.28
  196.1 28.4 %all_to_all.10 = f32[3,256,512]{2,1,0:T(8,128)S(1)} all-to-all(f32[3,256,512]{2,1,0:T(8,128)S(1)} %bitcast.19), channel_id=1, replica_groups={{0,128,256},{64,192,320},{384,512,640},{448,576,704},{1,129,257},{65,19..., dimensions={0} | all-to-all | bytes 3145728 | tf_op jit(solution)/shard_map/all_to_all | solution.py:213
  224.5 0.1 slice_reduce_fusion
  224.7 4.5 %collective-permute-start.10 = (f32[128,512]{1,0:T(8,128)S(1)}, f32[128,512]{1,0:T(8,128)S(1)}, u32[]{:S(2)}, u32[]{:S(2)}) collective-permute-start(f32[128,512]{1,0:T(8,128)S(1)} %get-tuple-element.15), channel_id=1, source_target_pairs={{0,384},{64,448},{128,512},{192,576},{256,640},{320,704},{384,0},{... | collective-permute-start | bytes 786440 | tf_op jit(solution)/shard_map/ppermute | solution.py:217
  229.2 17.6 %collective-permute-done.10 = f32[128,512]{1,0:T(8,128)S(1)} collective-permute-done((f32[128,512]{1,0:T(8,128)S(1)}, f32[128,512]{1,0:T(8,128)S(1)}, u32[]{:S(2)}, u32[]{:S(2)}) %collective-permute-start.10) | collective-permute-done | bytes 262176 | tf_op jit(solution)/shard_map/ppermute | solution.py:217
  246.8 0.7 add_convert_fusion
  (2 shorter events, 0.1 us)
Async XLA Ops:
  6.5 20.7 %collective-permute-start = (bf16[24,2048]{1,0:T(8,128)(2,1)}, bf16[24,2048]{1,0:T(8,128)(2,1)S(1)}, u32[]{:S(2)}, u32[]{:S(2)}) collective-permute-start(bf16[24,2048]{1,0:T(8,128)(2,1)} %bitcast.24), channel_id=1, source_target_pairs={{0,8},{1,9},{2,10},{3,11},{4,12},{5,13},{6,14},{7,15},{8,0},{9,1},... | collective-permute-start | bytes 294920 | tf_op jit(solution)/shard_map/ppermute | solution.py:195
  22.4 1.2 copy-start
  27.3 20.1 %copy-start.6 = (bf16[2048,24]{0,1:T(8,128)(2,1)S(1)}, bf16[2048,24]{0,1:T(8,128)(2,1)}, u32[]{:S(2)}) copy-start(bf16[2048,24]{0,1:T(8,128)(2,1)} %param.9) | copy-start | bytes 294916
  27.3 144.6 %all-to-all-start = ((bf16[64,144,128]{2,1,0:T(8,128)(2,1)}), bf16[64,144,128]{2,1,0:T(8,128)(2,1)S(1)}, u32[]{:S(2)}, u32[]{:S(2)}) async-start(bf16[64,144,128]{2,1,0:T(8,128)(2,1)} %pack.1), calls=%async_computation | async-start | bytes 4718592 | tf_op jit(solution)/shard_map/all_to_all | solution.py:199
  46.6 87.4 %all-gather.2.cloned.1.call-start = ((), (), s32[]{:S(2)}) async-start(), calls=%async_computation.2 | async-start | bytes 1179648 | tf_op jit(solution)/shard_map/all_gather | solution.py:202
  126.9 28.4 %copy-start.2 = (bf16[192,2048]{1,0:T(8,128)(2,1)}, bf16[192,2048]{1,0:T(8,128)(2,1)S(1)}, u32[]{:S(2)}) copy-start(bf16[192,2048]{1,0:T(8,128)(2,1)S(1)} %all_gather.6.refs_0_) | copy-start | bytes 2359300
  126.9 23.7 %collective-permute-start.2 = (bf16[192,2048]{1,0:T(8,128)(2,1)S(1)}, bf16[192,2048]{1,0:T(8,128)(2,1)}, u32[]{:S(2)}, u32[]{:S(2)}) collective-permute-start(bf16[192,2048]{1,0:T(8,128)(2,1)S(1)} %all_gather.6.refs_0_), channel_id=1, source_target_pairs={{0,48},{1,49},{2,50},{3,51},{4,52},{5,53},{6,54},{7,55},{8,56},{9,... | collective-permute-start | bytes 2359304 | tf_op jit(solution)/shard_map/ppermute | solution.py:180
  129.6 24.0 %collective-permute-start.1 = (bf16[192,2048]{1,0:T(8,128)(2,1)S(1)}, bf16[192,2048]{1,0:T(8,128)(2,1)}, u32[]{:S(2)}, u32[]{:S(2)}) collective-permute-start(bf16[192,2048]{1,0:T(8,128)(2,1)S(1)} %all_gather.6.refs_0_), channel_id=1, source_target_pairs={{0,16},{1,17},{2,18},{3,19},{4,20},{5,21},{6,22},{7,23},{8,24},{9,... | collective-permute-start | bytes 2359304 | tf_op jit(solution)/shard_map/ppermute | solution.py:180
  135.2 30.9 %copy-start.3 = (bf16[8,24,2048]{2,1,0:T(8,128)(2,1)}, bf16[8,24,2048]{2,1,0:T(8,128)(2,1)S(1)}, u32[]{:S(2)}) copy-start(bf16[8,24,2048]{2,1,0:T(8,128)(2,1)S(1)} %slice.35) | copy-start | bytes 2359300
  135.2 28.8 %collective-permute-start.6 = (bf16[192,2048]{1,0:T(8,128)(2,1)S(1)}, bf16[192,2048]{1,0:T(8,128)(2,1)S(1)}, u32[]{:S(2)}, u32[]{:S(2)}) collective-permute-start(bf16[192,2048]{1,0:T(8,128)(2,1)S(1)} %bitcast.20), channel_id=1, source_target_pairs={{0,48},{1,49},{2,50},{3,51},{4,52},{5,53},{6,54},{7,55},{8,56},{9,... | collective-permute-start | bytes 2359304 | tf_op jit(solution)/shard_map/ppermute | solution.py:180
  137.2 28.9 %collective-permute-start.5 = (bf16[192,2048]{1,0:T(8,128)(2,1)S(1)}, bf16[192,2048]{1,0:T(8,128)(2,1)S(1)}, u32[]{:S(2)}, u32[]{:S(2)}) collective-permute-start(bf16[192,2048]{1,0:T(8,128)(2,1)S(1)} %bitcast.21), channel_id=1, source_target_pairs={{0,16},{1,17},{2,18},{3,19},{4,20},{5,21},{6,22},{7,23},{8,24},{9,... | collective-permute-start | bytes 2359304 | tf_op jit(solution)/shard_map/ppermute | solution.py:180
  151.6 21.0 %collective-permute-start.4 = (bf16[96,2048]{1,0:T(8,128)(2,1)S(1)}, bf16[96,2048]{1,0:T(8,128)(2,1)}, u32[]{:S(2)}, u32[]{:S(2)}) collective-permute-start(bf16[96,2048]{1,0:T(8,128)(2,1)S(1)} %slice.34), channel_id=1, source_target_pairs={{0,48},{1,49},{2,50},{3,51},{4,52},{5,53},{6,54},{7,55},{8,56},{9,... | collective-permute-start | bytes 1179656 | tf_op jit(solution)/shard_map/ppermute | solution.py:185
  155.3 17.3 %collective-permute-start.3 = (bf16[96,2048]{1,0:T(8,128)(2,1)}, bf16[96,2048]{1,0:T(8,128)(2,1)}, u32[]{:S(2)}, u32[]{:S(2)}) collective-permute-start(bf16[96,2048]{1,0:T(8,128)(2,1)} %slice.33), channel_id=1, source_target_pairs={{0,16},{1,17},{2,18},{3,19},{4,20},{5,21},{6,22},{7,23},{8,24},{9,... | collective-permute-start | bytes 1179656 | tf_op jit(solution)/shard_map/ppermute | solution.py:185
  164.1 7.2 %copy-start.4 = (bf16[192,2048]{1,0:T(8,128)(2,1)}, bf16[192,2048]{1,0:T(8,128)(2,1)S(1)}, u32[]{:S(2)}) copy-start(bf16[192,2048]{1,0:T(8,128)(2,1)S(1)} %collective-permute-done.6.refs_7_) | copy-start | bytes 2359300
  164.1 11.0 %collective-permute-start.8 = (bf16[96,2048]{1,0:T(8,128)(2,1)S(1)}, bf16[96,2048]{1,0:T(8,128)(2,1)}, u32[]{:S(2)}, u32[]{:S(2)}) collective-permute-start(bf16[96,2048]{1,0:T(8,128)(2,1)S(1)} %slice.37), channel_id=1, source_target_pairs={{0,48},{1,49},{2,50},{3,51},{4,52},{5,53},{6,54},{7,55},{8,56},{9,... | collective-permute-start | bytes 1179656 | tf_op jit(solution)/shard_map/ppermute | solution.py:185
  166.0 5.2 %copy-start.5 = (bf16[192,2048]{1,0:T(8,128)(2,1)}, bf16[192,2048]{1,0:T(8,128)(2,1)S(1)}, u32[]{:S(2)}) copy-start(bf16[192,2048]{1,0:T(8,128)(2,1)S(1)} %collective-permute-done.5.refs_6_) | copy-start | bytes 2359300
  166.1 10.4 %collective-permute-start.7 = (bf16[96,2048]{1,0:T(8,128)(2,1)S(1)}, bf16[96,2048]{1,0:T(8,128)(2,1)}, u32[]{:S(2)}, u32[]{:S(2)}) collective-permute-start(bf16[96,2048]{1,0:T(8,128)(2,1)S(1)} %slice.36), channel_id=1, source_target_pairs={{0,16},{1,17},{2,18},{3,19},{4,20},{5,21},{6,22},{7,23},{8,24},{9,... | collective-permute-start | bytes 1179656 | tf_op jit(solution)/shard_map/ppermute | solution.py:185
  171.9 4.6 %copy-start.1 = (bf16[64,144,128]{2,1,0:T(8,128)(2,1)}, bf16[64,144,128]{2,1,0:T(8,128)(2,1)S(1)}, u32[]{:S(2)}) copy-start(bf16[64,144,128]{2,1,0:T(8,128)(2,1)S(1)} %all-to-all-done.refs_10_) | copy-start | bytes 7077892
  188.8 5.5 %collective-permute-start.9 = (f32[768,512]{1,0:T(8,128)}, f32[768,512]{1,0:T(8,128)S(1)}, u32[]{:S(2)}, u32[]{:S(2)}) collective-permute-start(f32[768,512]{1,0:T(8,128)} %get-tuple-element.14), channel_id=1, source_target_pairs={{0,64},{64,0},{128,192},{192,128},{256,320},{320,256},{384,448},{4... | collective-permute-start | bytes 4718600 | tf_op jit(solution)/shard_map/ppermute | solution.py:212
  224.7 22.1 %collective-permute-start.10 = (f32[128,512]{1,0:T(8,128)S(1)}, f32[128,512]{1,0:T(8,128)S(1)}, u32[]{:S(2)}, u32[]{:S(2)}) collective-permute-start(f32[128,512]{1,0:T(8,128)S(1)} %get-tuple-element.15), channel_id=1, source_target_pairs={{0,384},{64,448},{128,512},{192,576},{256,640},{320,704},{384,0},{... | collective-permute-start | bytes 786440 | tf_op jit(solution)/shard_map/ppermute | solution.py:217
Sparse Core Ops, SparseCore 0:
  49.8 60.6 all-gather.1

commit v9 on v3

--- a/solution.py
+++ b/solution.py
@@ -11,10 +11,12 @@
 NZL, NCORE = 6, 2
 NEAR = NZL // 2
 N_COL = NX * NZH * NY
-LABEL_ROWS = 16
+LABEL_ROWS = 8
+TILE_ROWS = 16
 CELLS = 128
 GROUP = 8
 OUT_ROWS = 128
+WIDE = 32
 
 
 def device(zl, core, x, zh, y):
@@ -25,6 +27,7 @@
     return (x * NZH + zh) * NY + y
 
 
+X_GROUPS = [[column(x, zh, y) for x in range(NX)] for zh in range(NZH) for y in range(NY)]
 Y_GROUPS = [[column(x, zh, y) for y in range(NY)] for x in range(NX) for zh in range(NZH)]
 NEAR_GROUPS = [
     [zl * NCORE + core for zl in range(half * NEAR, (half + 1) * NEAR)]
@@ -49,16 +52,15 @@
     ]
 
 
-def pack_kernel(route, tiles, out, count):
+def pack_kernel(route, tiles, out, labels, count):
     held, rows, cols = tiles.shape
-    label_at = CAP * rows
 
     @pl.loop(0, N_COL)
     def _(c):
         count[c] = 0
-        out[c, pl.ds(label_at, LABEL_ROWS), :] = jnp.zeros((LABEL_ROWS, cols), out.dtype)
-
-    lane = lax.broadcasted_iota(jnp.int32, (LABEL_ROWS, cols), 1)
+        labels[c] = jnp.zeros((TILE_ROWS, cols), labels.dtype)
+
+    lane = lax.broadcasted_iota(jnp.int32, (TILE_ROWS, cols), 1)
 
     @pl.loop(0, held)
     def _(t):
@@ -67,8 +69,7 @@
         count[c] = slot + 1
         out[c, pl.ds(pl.multiple_of(slot * rows, rows), rows), :] = tiles[t]
         label = (route[t] % CELLS + 1).astype(jnp.float32)
-        old = out[c, pl.ds(label_at, LABEL_ROWS), :].astype(jnp.float32)
-        out[c, pl.ds(label_at, LABEL_ROWS), :] = jnp.where(lane == slot, label, old).astype(out.dtype)
+        labels[c] = jnp.where(lane == slot, label, labels[c].astype(jnp.float32)).astype(labels.dtype)
 
 
 SMEM = pl.BlockSpec(memory_space=pltpu.SMEM)
@@ -78,16 +79,20 @@
 
 def pack(tiles, route):
     held, rows, cols = tiles.shape
-    return pl.pallas_call(
+    out, labels = pl.pallas_call(
         pack_kernel,
-        out_shape=jax.ShapeDtypeStruct((N_COL, CAP * rows + LABEL_ROWS, cols), tiles.dtype),
+        out_shape=(
+            jax.ShapeDtypeStruct((N_COL, CAP * rows + LABEL_ROWS, cols), tiles.dtype),
+            jax.ShapeDtypeStruct((N_COL, TILE_ROWS, cols), tiles.dtype),
+        ),
         in_specs=[SMEM, VMEM],
-        out_specs=VMEM,
+        out_specs=(VMEM, VMEM),
         scratch_shapes=[pltpu.SMEM((N_COL,), jnp.int32)],
         compiler_params=pltpu.CompilerParams(vmem_limit_bytes=24 << 20),
         cost_estimate=pl.CostEstimate(flops=0, bytes_accessed=4 << 20, transcendentals=0),
         name="pack",
     )(route, tiles)
+    return out.at[:, CAP * rows :].set(labels[:, :LABEL_ROWS])
 
 
 def place_kernel(labels, arrived, dense):
@@ -129,10 +134,10 @@
     per = step // NY
     groups = OUT_ROWS // GROUP
 
-    parts = [(0, near, 0), (1, left, 0), (2, right, 0), (3, far0, 0), (3, far1, far0.shape[0])]
-    copies = []
-    for n, (slot, ref, at) in enumerate(parts):
-        copies.append(pltpu.make_async_copy(ref, b.at[pl.ds(slot * step + at, ref.shape[0])], loads.at[n]))
+    parts = [(0, near), (step, left), (2 * step, right), (3 * step, far0), (3 * step + far0.shape[0], far1)]
+    copies = [
+        pltpu.make_async_copy(ref, b.at[pl.ds(at, ref.shape[0])], loads.at[n]) for n, (at, ref) in enumerate(parts)
+    ]
     copies.append(pltpu.make_async_copy(own, a, loads.at[len(parts)]))
     for copy in copies:
         copy.start()
@@ -146,25 +151,22 @@
             row = pl.multiple_of((slot * groups + g % groups) * GROUP, GROUP)
             total[away, pl.ds(row, GROUP), :] = block[i * GROUP : (i + 1) * GROUP]
 
-    def multiply(rows, columns):
-        product = jnp.dot(rows, dense[...], preferred_element_type=jnp.float32)
-        for n, c in enumerate(columns):
-            store(c, product[n * per : (n + 1) * per])
-
-    def at_column(by, side, y):
-        return ((x + by) % NX * NZH + side) * NY + y
+    def multiply(block, columns, side):
+        product = jnp.dot(block, dense[...], preferred_element_type=jnp.float32)
+        for n, xx in enumerate(columns):
+            for y in range(NY):
+                row = n * step + y * per
+                store((xx * NZH + side) * NY + y, product[row : row + per])
 
     for copy in copies[:3]:
         copy.wait()
-    multiply(b[: 2 * step, :], [at_column(by, 1 - plane, y) for by in (0, NX - 1) for y in range(NY)])
+    multiply(b[: 2 * step, :], (x, (x + NX - 1) % NX), 1 - plane)
     for copy in copies[3:5]:
         copy.wait()
-    multiply(b[2 * step :, :], [at_column(by, 1 - plane, y) for by in (1, 2) for y in range(NY)])
+    multiply(b[2 * step :, :], ((x + 1) % NX, (x + 2) % NX), 1 - plane)
     copies[5].wait()
-    half = max(NY // 2, 1)
-    for y0 in range(0, NY, half):
-        rows = a[y0 * NX * per : (y0 + half) * NX * per, :]
-        multiply(rows, [at_column(by, plane, y0 + y) for y in range(half) for by in (0, NX - 1, 1, 2)])
+    for n in range(0, NX, 2):
+        multiply(a[n * step : (n + 2) * step, :], (n, n + 1), plane)
     out = [pltpu.make_async_copy(total.at[k], ref, stores.at[k]) for k, ref in enumerate((keep, send))]
     for copy in out:
         copy.start()
@@ -173,8 +175,8 @@
 
 
 def contract(where, own, near, left, right, far0, far1, dense):
-    occ = own.shape[0] * NZH
-    shape = jax.ShapeDtypeStruct((occ // NCORE, dense.shape[1]), jnp.float32)
+    occ, (mu_rows, width) = own.shape[0] * NZH, dense.shape
+    shape = jax.ShapeDtypeStruct((occ // NCORE, width), jnp.float32)
     return pl.pallas_call(
         contract_kernel,
         out_shape=(shape, shape),
@@ -188,9 +190,7 @@
             pltpu.SemaphoreType.DMA((NCORE,)),
         ],
         compiler_params=pltpu.CompilerParams(vmem_limit_bytes=56 << 20),
-        cost_estimate=pl.CostEstimate(
-            flops=2 * occ * dense.shape[0] * dense.shape[1], bytes_accessed=12 << 20, transcendentals=0
-        ),
+        cost_estimate=pl.CostEstimate(flops=2 * occ * mu_rows * width, bytes_accessed=12 << 20, transcendentals=0),
         name="contract",
     )(where, own, near, left, right, far0, far1, dense)
 
@@ -202,15 +202,17 @@
     where = jnp.stack([here // (NZH * NY), here // NY % NZH, row // NCORE, row % NCORE]).astype(jnp.int32)
 
     mine = coeff.T
+    padded = jnp.pad(mine, ((0, WIDE - per), (0, 0)))
+    own = lax.all_gather(padded, "col", axis=0, tiled=True, axis_index_groups=Y_GROUPS)
     theirs = lax.ppermute(mine, "col", PLANE_SWAP)
-    own = jnp.concatenate([mine] + [lax.ppermute(mine, "col", x_shift(by)) for by in (1, -1, 2)], axis=0)
     route = dest_col.reshape(held) * CELLS + mu_block.reshape(held) * CB + col_block.reshape(held)
     outgoing = pack(tiles.reshape(held, rows, cols), route)
-    outgoing, theirs, own = lax.optimization_barrier((outgoing, theirs, own))
+    near = lax.all_gather(theirs, "col", axis=0, tiled=True, axis_index_groups=Y_GROUPS)
+    outgoing, own, near = lax.optimization_barrier((outgoing, own, near))
     arrived = lax.all_to_all(outgoing, "col", split_axis=0, concat_axis=0, tiled=True)
 
-    own = lax.all_gather(own, "col", axis=0, tiled=True, axis_index_groups=Y_GROUPS)
-    near = lax.all_gather(theirs, "col", axis=0, tiled=True, axis_index_groups=Y_GROUPS)
+    own = own.reshape(NY, WIDE, mu_rows)[:, :per].reshape(NY * per, mu_rows)
+    own = lax.all_gather(own, "col", axis=0, tiled=True, axis_index_groups=X_GROUPS)
     left = lax.ppermute(near, "col", x_shift(1))
     right = lax.ppermute(near, "col", x_shift(-1))
     cut = near.shape[0] // 2

time: 254 us -> 242 us (0.953)
  blocking collectives: 113 us -> 66 us
  waiting for transfers between devices: 36.5 us -> 77 us
  starting transfers between devices: 61.3 us -> 53.7 us
  local copies, waits for them, and re-layouts: 5.08 us -> 8.42 us
    all_gather x1, blocking collectives: 84.6 us -> 29 us  [per_device(): lax.all_gather(theirs, 'col', axis=0, tiled=True, axis_index_groups=Y_GRO...]
    ppermute x1, waiting for transfers between devices: 11.8 us -> 45.3 us  [per_device(): right = lax.ppermute(near, 'col', x_shift(-1))]
    ppermute x3 -> x0, starting transfers between devices: 16.1 us -> none  [per_device(): lax.ppermute(mine, 'col', x_shift(by))]
    all_to_all x1, blocking collectives: 28.4 us -> 37 us  [per_device(): lax.all_to_all(share.reshape(NEAR, 2 * OUT_ROWS, -1), 'row', split_axis=0...]
    ppermute x1, waiting for transfers between devices: 0.01 us -> 6.92 us  [per_device(): far1 = lax.ppermute(right[cut:], 'col', x_shift(-1))]
    ppermute x1, starting transfers between devices: 9.42 us -> 15.1 us  [per_device(): theirs = lax.ppermute(mine, 'col', PLANE_SWAP)]
    ppermute x1, starting transfers between devices: 1.92 us -> 6.54 us  [per_device(): lax.ppermute(away, 'row', FAR_SWAP)]
    all_gather x1 -> x2, waiting for transfers between devices: 0.01 us -> 4.39 us  [the longest x1 3.2 us: per_device(): lax.all_gather(padded, 'col', axis=0, tiled=True, axis_index_groups=Y_GRO...]
  transfers between devices with their start and end apart: 12 -> 10, of which waited for: 4 -> 7; matrix products, arithmetic and copies ran while one was open for 1% -> 2% of each run, Pallas kernels for 2% -> 2%
where the time goes in v9:
time: 242 us; the launch traced here: 240 us
  waiting for transfers between devices  77 us (32%)
  blocking collectives  66 us (27%)
  starting transfers between devices  53.7 us (22%)
  Pallas kernels  17.2 us (7%)
  between operations  13.6 us (6%)
  local copies, waits for them, and re-layouts  8.42 us (3%)
  other arithmetic  3.91 us (2%)
    ppermute x1, waiting for transfers between devices, per_device(): right = lax.ppermute(near, 'col', x_shift(-1))  45.3 us
    all_to_all x1, blocking collectives, per_device(): lax.all_to_all(share.reshape(NEAR, 2 * OUT_ROWS, -1), 'row', split_axis=0...  37 us
    all_gather x1, blocking collectives, per_device(): lax.all_gather(theirs, 'col', axis=0, tiled=True, axis_index_groups=Y_GRO...  29 us
    ppermute x1, waiting for transfers between devices, per_device(): lax.ppermute(away, 'row', FAR_SWAP)  16 us
    all_to_all x1, starting transfers between devices, per_device(): lax.all_to_all(outgoing, 'col', split_axis=0, concat_axis=0, tiled=True)  16 us
    ppermute x1, starting transfers between devices, per_device(): theirs = lax.ppermute(mine, 'col', PLANE_SWAP)  15.1 us
    pallas_call x1, Pallas kernels, contract(): pl.pallas_call(contract_kernel, out_shape=(shape, shape), in_specs=[SMEM]...  11.8 us
    ppermute x1, waiting for transfers between devices, per_device(): far1 = lax.ppermute(right[cut:], 'col', x_shift(-1))  6.92 us
  transfers between devices with their start and end apart: 10, of which 7 were waited for; matrix products, arithmetic and copies ran while one was open for 2% of the time, Pallas kernels for 2%

profile of v9, /device:TPU:6, one launch (start us, length us, event | category | flops | bytes accessed | tf_op | source)
XLA Modules:
  0.0 239.8 jit_solution(9211199315163853216)
XLA Ops:
  6.5 0.0 all-gather.3.cloned.1.call-start
  6.5 1.6 pad.6
  8.1 0.0 all-gather.3.cloned.1.call-update
  8.1 15.1 %collective-permute-start = (bf16[24,2048]{1,0:T(8,128)(2,1)}, bf16[24,2048]{1,0:T(8,128)(2,1)S(1)}, u32[]{:S(2)}, u32[]{:S(2)}) collective-permute-start(bf16[24,2048]{1,0:T(8,128)(2,1)} %bitcast.24), channel_id=1, source_target_pairs={{0,8},{1,9},{2,10},{3,11},{4,12},{5,13},{6,14},{7,15},{8,0},{9,1},... | collective-permute-start | bytes 294920 | tf_op jit(solution)/shard_map/ppermute | solution.py:207
  23.3 0.7 bitcast_add_fusion.route
  24.0 0.0 copy-start.2
  24.0 1.2 copy-done.2
  25.2 2.1 pack.1
  27.3 0.0 copy-start
  27.3 1.4 copy-done
  28.7 0.7 slice_dynamic-update-slice_fusion
  29.4 0.0 collective-permute-done
  29.4 29.0 %all_gather.10.near = bf16[192,2048]{1,0:T(8,128)(2,1)S(1)} all-gather(bf16[24,2048]{1,0:T(8,128)(2,1)S(1)} %collective-permute-done), channel_id=1, replica_groups={{0,1,2,3,4,5,6,7},{8,9,10,11,12,13,14,15},{16,17,18,19,20,21,22,23},{24..., dimensions={0}, use_global_device_ids=true | all-gather | bytes 884736 | tf_op jit(solution)/shard_map/all_gather | solution.py:210
  58.4 0.0 copy-start.3
  58.4 3.2 %all-gather.3.cloned.1.call-done = bf16[256,2048]{1,0:T(8,128)(2,1)} async-done(((bf16[32,2048]{1,0:T(8,128)(2,1)}), bf16[256,2048]{1,0:T(8,128)(2,1)}) %all-gather.3.cloned.1.call-update) | async-done | bytes 1048592 | tf_op jit(solution)/shard_map/all_gather | solution.py:206
  61.6 16.0 %all-to-all-start = ((bf16[64,136,128]{2,1,0:T(8,128)(2,1)}), bf16[64,136,128]{2,1,0:T(8,128)(2,1)S(1)}, u32[]{:S(2)}, u32[]{:S(2)}) async-start(bf16[64,136,128]{2,1,0:T(8,128)(2,1)} %slice_dynamic-update-slice_fusion), calls=%async_computation | async-start | bytes 4456448 | tf_op jit(solution)/shard_map/all_to_all | solution.py:212
  77.6 0.0 all-gather.5.cloned.1.call-start
  77.6 2.1 slice.50
  79.7 0.0 all-gather.5.cloned.1.call-update
  79.7 2.7 %collective-permute-start.2 = (bf16[192,2048]{1,0:T(8,128)(2,1)S(1)}, bf16[192,2048]{1,0:T(8,128)(2,1)S(1)}, u32[]{:S(2)}, u32[]{:S(2)}) collective-permute-start(bf16[192,2048]{1,0:T(8,128)(2,1)S(1)} %all_gather.10.near), channel_id=1, source_target_pairs={{0,48},{1,49},{2,50},{3,51},{4,52},{5,53},{6,54},{7,55},{8,56},{9,... | collective-permute-start | bytes 2359304 | tf_op jit(solution)/shard_map/ppermute | solution.py:217
  82.4 0.0 copy-done.3
  82.4 4.4 %collective-permute-start.1 = (bf16[192,2048]{1,0:T(8,128)(2,1)S(1)}, bf16[192,2048]{1,0:T(8,128)(2,1)S(1)}, u32[]{:S(2)}, u32[]{:S(2)}) collective-permute-start(bf16[192,2048]{1,0:T(8,128)(2,1)S(1)} %all_gather.10.near), channel_id=1, source_target_pairs={{0,16},{1,17},{2,18},{3,19},{4,20},{5,21},{6,22},{7,23},{8,24},{9,... | collective-permute-start | bytes 2359304 | tf_op jit(solution)/shard_map/ppermute | solution.py:216
  86.8 45.3 %collective-permute-done.2.right = bf16[192,2048]{1,0:T(8,128)(2,1)S(1)} collective-permute-done((bf16[192,2048]{1,0:T(8,128)(2,1)S(1)}, bf16[192,2048]{1,0:T(8,128)(2,1)S(1)}, u32[]{:S(2)}, u32[]{:S(2)}) %collective-permute-start.2) | collective-permute-done | bytes 786464 | tf_op jit(solution)/shard_map/ppermute | solution.py:217
  132.2 0.0 copy-start.4
  132.2 1.9 collective-permute-start.4
  134.1 0.0 collective-permute-done.1.left
  134.1 0.0 copy-start.5
  134.2 5.1 %collective-permute-start.3 = (bf16[96,2048]{1,0:T(8,128)(2,1)S(1)}, bf16[96,2048]{1,0:T(8,128)(2,1)S(1)}, u32[]{:S(2)}, u32[]{:S(2)}) collective-permute-start(bf16[96,2048]{1,0:T(8,128)(2,1)S(1)} %slice.51), channel_id=1, source_target_pairs={{0,16},{1,17},{2,18},{3,19},{4,20},{5,21},{6,22},{7,23},{8,24},{9,... | collective-permute-start | bytes 1179656 | tf_op jit(solution)/shard_map/ppermute | solution.py:219
  139.3 0.0 copy-done.4
  139.3 0.0 copy-done.5
  139.4 0.6 pad_add_fusion.where
  140.0 0.0 all-to-all-done.arrived
  140.0 3.3 %place.1.dense = bf16[2048,512]{1,0:T(8,128)(2,1)S(1)} custom-call(s32[64,2]{1,0:T(8,128)S(1)} %bitcast.19, bf16[64,136,128]{2,1,0:T(8,128)(2,1)S(1)} %all-to-all-done.arrived), custom_call_target="tpu_custom_call" | custom-call | bytes 4194304 | tf_op jit(solution)/shard_map/place/pallas_call | solution.py:120
  143.4 0.0 copy-start.1
  143.4 1.3 copy-done.1
  144.7 6.9 %collective-permute-done.4.far1 = bf16[96,2048]{1,0:T(8,128)(2,1)} collective-permute-done((bf16[96,2048]{1,0:T(8,128)(2,1)S(1)}, bf16[96,2048]{1,0:T(8,128)(2,1)}, u32[]{:S(2)}, u32[]{:S(2)}) %collective-permute-start.4) | collective-permute-done | bytes 393248 | tf_op jit(solution)/shard_map/ppermute | solution.py:220
  151.6 0.7 collective-permute-done.3.far0
  152.3 0.0 copy-start.6
  152.3 1.2 all-gather.5.cloned.1.call-done.own
  153.5 0.0 copy-done.6
  153.5 11.8 %contract.1 = (f32[768,512]{1,0:T(8,128)}, f32[768,512]{1,0:T(8,128)}) custom-call(s32[4]{0:T(128)} %pad_add_fusion.where, bf16[768,2048]{1,0:T(8,128)(2,1)} %all-gather.5.cloned.1.call-done.own, bf16[192,2048]{1,0:T(8,128)(2,1)} %copy-done.3, bf16[192,2048]{1,0:T(8,128)(2,1)} %copy-done.5, bf16[192,2048]{1,0:T(8,128)(2,1)} %copy-done.4, ...), custom_call_target="tpu_custom_call" | custom-call | flops 3221225472 | bytes 12582912 | tf_op jit(solution)/shard_map/contract/pallas_call | solution.py:180
  165.3 1.9 collective-permute-start.5
  167.2 3.6 %collective-permute-done.5 = f32[768,512]{1,0:T(8,128)S(1)} collective-permute-done((f32[768,512]{1,0:T(8,128)}, f32[768,512]{1,0:T(8,128)S(1)}, u32[]{:S(2)}, u32[]{:S(2)}) %collective-permute-start.5) | collective-permute-done | bytes 1572896 | tf_op jit(solution)/shard_map/ppermute | solution.py:225
  170.8 1.8 add.30
  172.5 37.0 %all_to_all.10 = f32[3,256,512]{2,1,0:T(8,128)S(1)} all-to-all(f32[3,256,512]{2,1,0:T(8,128)S(1)} %bitcast.20), channel_id=1, replica_groups={{0,128,256},{64,192,320},{384,512,640},{448,576,704},{1,129,257},{65,19..., dimensions={0} | all-to-all | bytes 3145728 | tf_op jit(solution)/shard_map/all_to_all | solution.py:226
  209.5 0.1 slice_reduce_fusion
  209.7 6.5 %collective-permute-start.6 = (f32[128,512]{1,0:T(8,128)S(1)}, f32[128,512]{1,0:T(8,128)S(1)}, u32[]{:S(2)}, u32[]{:S(2)}) collective-permute-start(f32[128,512]{1,0:T(8,128)S(1)} %get-tuple-element.31), channel_id=1, source_target_pairs={{0,384},{64,448},{128,512},{192,576},{256,640},{320,704},{384,0},{... | collective-permute-start | bytes 786440 | tf_op jit(solution)/shard_map/ppermute | solution.py:230
  216.2 16.0 %collective-permute-done.6 = f32[128,512]{1,0:T(8,128)S(1)} collective-permute-done((f32[128,512]{1,0:T(8,128)S(1)}, f32[128,512]{1,0:T(8,128)S(1)}, u32[]{:S(2)}, u32[]{:S(2)}) %collective-permute-start.6) | collective-permute-done | bytes 262176 | tf_op jit(solution)/shard_map/ppermute | solution.py:230
  232.3 0.7 add_convert_fusion
  (3 shorter events, 0.1 us)
Async XLA Ops:
  6.5 55.1 %all-gather.3.cloned.1.call-start = ((), (), s32[]{:S(2)}) async-start(), calls=%async_computation.2 | async-start | bytes 1179648 | tf_op jit(solution)/shard_map/all_gather | solution.py:206
  8.1 21.3 %collective-permute-start = (bf16[24,2048]{1,0:T(8,128)(2,1)}, bf16[24,2048]{1,0:T(8,128)(2,1)S(1)}, u32[]{:S(2)}, u32[]{:S(2)}) collective-permute-start(bf16[24,2048]{1,0:T(8,128)(2,1)} %bitcast.24), channel_id=1, source_target_pairs={{0,8},{1,9},{2,10},{3,11},{4,12},{5,13},{6,14},{7,15},{8,0},{9,1},... | collective-permute-start | bytes 294920 | tf_op jit(solution)/shard_map/ppermute | solution.py:207
  24.0 1.2 copy-start.2
  27.3 1.4 copy-start
  58.4 24.0 %copy-start.3 = (bf16[192,2048]{1,0:T(8,128)(2,1)}, bf16[192,2048]{1,0:T(8,128)(2,1)S(1)}, u32[]{:S(2)}) copy-start(bf16[192,2048]{1,0:T(8,128)(2,1)S(1)} %all_gather.10.near) | copy-start | bytes 2359300
  61.6 78.4 %all-to-all-start = ((bf16[64,136,128]{2,1,0:T(8,128)(2,1)}), bf16[64,136,128]{2,1,0:T(8,128)(2,1)S(1)}, u32[]{:S(2)}, u32[]{:S(2)}) async-start(bf16[64,136,128]{2,1,0:T(8,128)(2,1)} %slice_dynamic-update-slice_fusion), calls=%async_computation | async-start | bytes 4456448 | tf_op jit(solution)/shard_map/all_to_all | solution.py:212
  77.6 75.9 %all-gather.5.cloned.1.call-start = ((), (), s32[]{:S(2)}) async-start(), calls=%async_computation.3 | async-start | bytes 3932160 | tf_op jit(solution)/shard_map/all_gather | solution.py:215
  79.7 52.4 %collective-permute-start.2 = (bf16[192,2048]{1,0:T(8,128)(2,1)S(1)}, bf16[192,2048]{1,0:T(8,128)(2,1)S(1)}, u32[]{:S(2)}, u32[]{:S(2)}) collective-permute-start(bf16[192,2048]{1,0:T(8,128)(2,1)S(1)} %all_gather.10.near), channel_id=1, source_target_pairs={{0,48},{1,49},{2,50},{3,51},{4,52},{5,53},{6,54},{7,55},{8,56},{9,... | collective-permute-start | bytes 2359304 | tf_op jit(solution)/shard_map/ppermute | solution.py:217
  82.4 51.7 %collective-permute-start.1 = (bf16[192,2048]{1,0:T(8,128)(2,1)S(1)}, bf16[192,2048]{1,0:T(8,128)(2,1)S(1)}, u32[]{:S(2)}, u32[]{:S(2)}) collective-permute-start(bf16[192,2048]{1,0:T(8,128)(2,1)S(1)} %all_gather.10.near), channel_id=1, source_target_pairs={{0,16},{1,17},{2,18},{3,19},{4,20},{5,21},{6,22},{7,23},{8,24},{9,... | collective-permute-start | bytes 2359304 | tf_op jit(solution)/shard_map/ppermute | solution.py:216
  132.2 7.2 %copy-start.4 = (bf16[192,2048]{1,0:T(8,128)(2,1)}, bf16[192,2048]{1,0:T(8,128)(2,1)S(1)}, u32[]{:S(2)}) copy-start(bf16[192,2048]{1,0:T(8,128)(2,1)S(1)} %collective-permute-done.2.right) | copy-start | bytes 2359300
  132.2 19.4 %collective-permute-start.4 = (bf16[96,2048]{1,0:T(8,128)(2,1)S(1)}, bf16[96,2048]{1,0:T(8,128)(2,1)}, u32[]{:S(2)}, u32[]{:S(2)}) collective-permute-start(bf16[96,2048]{1,0:T(8,128)(2,1)S(1)} %slice.52), channel_id=1, source_target_pairs={{0,48},{1,49},{2,50},{3,51},{4,52},{5,53},{6,54},{7,55},{8,56},{9,... | collective-permute-start | bytes 1179656 | tf_op jit(solution)/shard_map/ppermute | solution.py:220
  134.1 5.2 %copy-start.5 = (bf16[192,2048]{1,0:T(8,128)(2,1)}, bf16[192,2048]{1,0:T(8,128)(2,1)S(1)}, u32[]{:S(2)}) copy-start(bf16[192,2048]{1,0:T(8,128)(2,1)S(1)} %collective-permute-done.1.left) | copy-start | bytes 2359300
  134.2 18.1 %collective-permute-start.3 = (bf16[96,2048]{1,0:T(8,128)(2,1)S(1)}, bf16[96,2048]{1,0:T(8,128)(2,1)S(1)}, u32[]{:S(2)}, u32[]{:S(2)}) collective-permute-start(bf16[96,2048]{1,0:T(8,128)(2,1)S(1)} %slice.51), channel_id=1, source_target_pairs={{0,16},{1,17},{2,18},{3,19},{4,20},{5,21},{6,22},{7,23},{8,24},{9,... | collective-permute-start | bytes 1179656 | tf_op jit(solution)/shard_map/ppermute | solution.py:219
  143.4 1.4 copy-start.1
  152.3 1.2 copy-start.6
  165.3 5.5 %collective-permute-start.5 = (f32[768,512]{1,0:T(8,128)}, f32[768,512]{1,0:T(8,128)S(1)}, u32[]{:S(2)}, u32[]{:S(2)}) collective-permute-start(f32[768,512]{1,0:T(8,128)} %get-tuple-element.30), channel_id=1, source_target_pairs={{0,64},{64,0},{128,192},{192,128},{256,320},{320,256},{384,448},{4... | collective-permute-start | bytes 4718600 | tf_op jit(solution)/shard_map/ppermute | solution.py:225
  209.7 22.6 %collective-permute-start.6 = (f32[128,512]{1,0:T(8,128)S(1)}, f32[128,512]{1,0:T(8,128)S(1)}, u32[]{:S(2)}, u32[]{:S(2)}) collective-permute-start(f32[128,512]{1,0:T(8,128)S(1)} %get-tuple-element.31), channel_id=1, source_target_pairs={{0,384},{64,448},{128,512},{192,576},{256,640},{320,704},{384,0},{... | collective-permute-start | bytes 786440 | tf_op jit(solution)/shard_map/ppermute | solution.py:230
Sparse Core Ops, SparseCore 0:
  9.7 51.8 all-gather.2
  80.8 72.6 all-gather.4

commit v10 on v9

--- a/solution.py
+++ b/solution.py
@@ -10,6 +10,7 @@
 NX, NZH, NY = 4, 2, 8
 NZL, NCORE = 6, 2
 NEAR = NZL // 2
+AXES = ("row", "col")
 N_COL = NX * NZH * NY
 LABEL_ROWS = 8
 TILE_ROWS = 16
@@ -29,6 +30,7 @@
 
 X_GROUPS = [[column(x, zh, y) for x in range(NX)] for zh in range(NZH) for y in range(NY)]
 Y_GROUPS = [[column(x, zh, y) for y in range(NY)] for x in range(NX) for zh in range(NZH)]
+PLANE_GROUPS = [[column(x, zh, y) for x in range(NX) for y in range(NY)] for zh in range(NZH)]
 NEAR_GROUPS = [
     [zl * NCORE + core for zl in range(half * NEAR, (half + 1) * NEAR)]
     for half in range(NZL // NEAR)
@@ -43,6 +45,16 @@
 CORE_SWAP = [(zl * NCORE + core, zl * NCORE + 1 - core) for zl in range(NZL) for core in range(NCORE)]
 
 
+def z_shift(by):
+    return [
+        (device(z % NZL, core, x, z // NZL, y), device(to % NZL, core, x, to // NZL, y))
+        for z, to in ((z, (z + by) % (NZL * NZH)) for z in range(NZL * NZH))
+        for core in range(NCORE)
+        for x in range(NX)
+        for y in range(NY)
+    ]
+
+
 def x_shift(by):
     return [
         (column(x, zh, y), column((x + by) % NX, zh, y))
@@ -52,13 +64,17 @@
     ]
 
 
-def pack_kernel(route, tiles, out, labels, count):
+def pack_kernel(where, route, tiles, stay, cross, stay_labels, cross_labels, count):
     held, rows, cols = tiles.shape
 
     @pl.loop(0, N_COL)
     def _(c):
         count[c] = 0
-        labels[c] = jnp.zeros((TILE_ROWS, cols), labels.dtype)
+
+    @pl.loop(0, NX * NY)
+    def _(j):
+        stay_labels[j] = jnp.zeros((TILE_ROWS, cols), stay_labels.dtype)
+        cross_labels[j] = jnp.zeros((TILE_ROWS, cols), cross_labels.dtype)
 
     lane = lax.broadcasted_iota(jnp.int32, (TILE_ROWS, cols), 1)
 
@@ -67,9 +83,21 @@
         c = route[t] // CELLS
         slot = count[c]
         count[c] = slot + 1
-        out[c, pl.ds(pl.multiple_of(slot * rows, rows), rows), :] = tiles[t]
+        j = c // (NZH * NY) * NY + c % NY
         label = (route[t] % CELLS + 1).astype(jnp.float32)
-        labels[c] = jnp.where(lane == slot, label, labels[c].astype(jnp.float32)).astype(labels.dtype)
+        here = c // NY % NZH == where[1]
+
+        def put(out, labels):
+            out[j, pl.ds(pl.multiple_of(slot * rows, rows), rows), :] = tiles[t]
+            labels[j] = jnp.where(lane == slot, label, labels[j].astype(jnp.float32)).astype(labels.dtype)
+
+        @pl.when(here)
+        def _():
+            put(stay, stay_labels)
+
+        @pl.when(jnp.logical_not(here))
+        def _():
+            put(cross, cross_labels)
 
 
 SMEM = pl.BlockSpec(memory_space=pltpu.SMEM)
@@ -77,55 +105,57 @@
 ANY = pl.BlockSpec(memory_space=pl.ANY)
 
 
-def pack(tiles, route):
+def pack(where, tiles, route):
     held, rows, cols = tiles.shape
-    out, labels = pl.pallas_call(
+    out = jax.ShapeDtypeStruct((NX * NY, CAP * rows + LABEL_ROWS, cols), tiles.dtype)
+    labels = jax.ShapeDtypeStruct((NX * NY, TILE_ROWS, cols), tiles.dtype)
+    *blocks, label0, label1 = pl.pallas_call(
         pack_kernel,
-        out_shape=(
-            jax.ShapeDtypeStruct((N_COL, CAP * rows + LABEL_ROWS, cols), tiles.dtype),
-            jax.ShapeDtypeStruct((N_COL, TILE_ROWS, cols), tiles.dtype),
-        ),
-        in_specs=[SMEM, VMEM],
-        out_specs=(VMEM, VMEM),
+        out_shape=(out, out, labels, labels),
+        in_specs=[SMEM, SMEM, VMEM],
+        out_specs=(VMEM,) * 4,
         scratch_shapes=[pltpu.SMEM((N_COL,), jnp.int32)],
         compiler_params=pltpu.CompilerParams(vmem_limit_bytes=24 << 20),
         cost_estimate=pl.CostEstimate(flops=0, bytes_accessed=4 << 20, transcendentals=0),
         name="pack",
-    )(route, tiles)
-    return out.at[:, CAP * rows :].set(labels[:, :LABEL_ROWS])
-
-
-def place_kernel(labels, arrived, dense):
-    rows = (arrived.shape[1] - LABEL_ROWS) // CAP
-    cols = arrived.shape[2]
+    )(where, route, tiles)
+    return [
+        block.at[:, CAP * rows :].set(label[:, :LABEL_ROWS]) for block, label in zip(blocks, (label0, label1))
+    ]
+
+
+def place_kernel(labels0, labels1, arrived0, arrived1, dense):
+    rows = (arrived0.shape[1] - LABEL_ROWS) // CAP
+    cols = arrived0.shape[2]
 
     @pl.loop(0, dense.shape[0] // rows)
     def _(m):
         dense[pl.ds(pl.multiple_of(m * rows, rows), rows), :] = jnp.zeros((rows, dense.shape[1]), dense.dtype)
 
-    @pl.loop(0, N_COL)
+    @pl.loop(0, NX * NY)
     def _(j):
-        for slot in range(CAP):
-            label = labels[j, slot]
-
-            @pl.when(label > 0)
-            def _():
-                cell = label - 1
-                row = pl.multiple_of((cell // CB) * rows, rows)
-                col = pl.multiple_of(cell % CB * cols, cols)
-                dense[pl.ds(row, rows), pl.ds(col, cols)] = arrived[j, pl.ds(slot * rows, rows), :]
+        for labels, arrived in ((labels0, arrived0), (labels1, arrived1)):
+            for slot in range(CAP):
+                label = labels[j, slot]
+
+                @pl.when(label > 0)
+                def _():
+                    cell = label - 1
+                    row = pl.multiple_of((cell // CB) * rows, rows)
+                    col = pl.multiple_of(cell % CB * cols, cols)
+                    dense[pl.ds(row, rows), pl.ds(col, cols)] = arrived[j, pl.ds(slot * rows, rows), :]
 
 
 def place(labels, arrived, mu_rows):
     return pl.pallas_call(
         place_kernel,
-        out_shape=jax.ShapeDtypeStruct((mu_rows, CB * arrived.shape[2]), arrived.dtype),
-        in_specs=[SMEM, VMEM],
+        out_shape=jax.ShapeDtypeStruct((mu_rows, CB * arrived[0].shape[2]), arrived[0].dtype),
+        in_specs=[SMEM, SMEM, VMEM, VMEM],
         out_specs=VMEM,
         compiler_params=pltpu.CompilerParams(vmem_limit_bytes=24 << 20),
         cost_estimate=pl.CostEstimate(flops=0, bytes_accessed=4 << 20, transcendentals=0),
         name="place",
-    )(labels, arrived)
+    )(*labels, *arrived)
 
 
 def contract_kernel(where, own, near, left, right, far0, far1, dense, keep, send, a, b, total, loads, stores):
@@ -206,20 +236,27 @@
     own = lax.all_gather(padded, "col", axis=0, tiled=True, axis_index_groups=Y_GROUPS)
     theirs = lax.ppermute(mine, "col", PLANE_SWAP)
     route = dest_col.reshape(held) * CELLS + mu_block.reshape(held) * CB + col_block.reshape(held)
-    outgoing = pack(tiles.reshape(held, rows, cols), route)
+    stay, cross = pack(where, tiles.reshape(held, rows, cols), route)
+    cut = cross.shape[0] // 2
+    over = [lax.ppermute(half, AXES, z_shift(by)) for half, by in ((cross[:cut], NEAR), (cross[cut:], -NEAR))]
     near = lax.all_gather(theirs, "col", axis=0, tiled=True, axis_index_groups=Y_GROUPS)
-    outgoing, own, near = lax.optimization_barrier((outgoing, own, near))
-    arrived = lax.all_to_all(outgoing, "col", split_axis=0, concat_axis=0, tiled=True)
+    stay, own, near, over = lax.optimization_barrier((stay, own, near, over))
+    over = [lax.ppermute(half, AXES, z_shift(by)) for half, by in zip(over, (NZL - NEAR, NEAR - NZL))]
+    arrived0 = lax.all_to_all(stay, "col", split_axis=0, concat_axis=0, tiled=True, axis_index_groups=PLANE_GROUPS)
+    left = lax.ppermute(near, "col", x_shift(1))
+    right = lax.ppermute(near, "col", x_shift(-1))
+    cross = jnp.concatenate(over, axis=0)
+    cross, arrived0, left, right = lax.optimization_barrier((cross, arrived0, left, right))
+    arrived1 = lax.all_to_all(cross, "col", split_axis=0, concat_axis=0, tiled=True, axis_index_groups=PLANE_GROUPS)
+    arrived = [arrived0, arrived1]
 
     own = own.reshape(NY, WIDE, mu_rows)[:, :per].reshape(NY * per, mu_rows)
     own = lax.all_gather(own, "col", axis=0, tiled=True, axis_index_groups=X_GROUPS)
-    left = lax.ppermute(near, "col", x_shift(1))
-    right = lax.ppermute(near, "col", x_shift(-1))
     cut = near.shape[0] // 2
     far0 = lax.ppermute(left[:cut], "col", x_shift(1))
     far1 = lax.ppermute(right[cut:], "col", x_shift(-1))
 
-    labels = arrived[:, CAP * rows, :CAP].astype(jnp.int32)
+    labels = [part[:, CAP * rows, :CAP].astype(jnp.int32) for part in arrived]
     dense = place(labels, arrived, mu_rows)
     keep, send = contract(where, own, near, left, right, far0, far1, dense)
     share = keep + lax.ppermute(send, "row", CORE_SWAP)

time: 242 us -> 260 us (1.074)
  starting transfers between devices: 53.7 us -> 76.8 us
  waiting for transfers between devices: 77 us -> 68.1 us
  Pallas kernels: 17.2 us -> 19.8 us
    ppermute x1, waiting for transfers between devices: 45.3 us -> 0.01 us  [per_device(): right = lax.ppermute(near, 'col', x_shift(-1))]
    ppermute x0 -> x4, waiting for transfers between devices: none -> 30.3 us  [per_device(): lax.ppermute(half, AXES, z_shift(by))]
    ppermute x0 -> x4, starting transfers between devices: none -> 23.7 us  [per_device(): lax.ppermute(half, AXES, z_shift(by))]
    all_to_all x1 -> x2, waiting for transfers between devices: 0.01 us -> 16.9 us  [the longest x1 16.9 us: per_device(): lax.all_to_all(cross, 'col', split_axis=0, concat_axis=0, tiled=True, axi...]
    ppermute x1, waiting for transfers between devices: 6.92 us -> 0.01 us  [per_device(): far1 = lax.ppermute(right[cut:], 'col', x_shift(-1))]
    all_gather x1, waiting for transfers between devices: 3.2 us -> 0.02 us  [per_device(): lax.all_gather(padded, 'col', axis=0, tiled=True, axis_index_groups=Y_GRO...]
    pallas_call x1, Pallas kernels: 2.09 us -> 4.95 us  [pack(): pl.pallas_call(pack_kernel, out_shape=(out, out, labels, labels), in_spec...]
    all_to_all x1 -> x2, starting transfers between devices: 16 us -> 17.6 us  [the longest x1 9.54 us: per_device(): lax.all_to_all(cross, 'col', split_axis=0, concat_axis=0, tiled=True, axi...]
  transfers between devices with their start and end apart: 10 -> 15, of which waited for: 7 -> 4; matrix products, arithmetic and copies ran while one was open for 2% -> 2% of each run, Pallas kernels for 2% -> 3%
where the time goes in v10:
time: 260 us; the launch traced here: 257 us
  starting transfers between devices  76.8 us (30%)
  waiting for transfers between devices  68.1 us (26%)
  blocking collectives  63.6 us (24%)
  Pallas kernels  19.8 us (8%)
  between operations  13.7 us (5%)
  local copies, waits for them, and re-layouts  11 us (4%)
  other arithmetic  4.47 us (2%)
    all_to_all x1, blocking collectives, per_device(): lax.all_to_all(share.reshape(NEAR, 2 * OUT_ROWS, -1), 'row', split_axis=0...  34.9 us
    ppermute x4, waiting for transfers between devices, per_device(): lax.ppermute(half, AXES, z_shift(by))  30.3 us
    all_gather x1, blocking collectives, per_device(): lax.all_gather(theirs, 'col', axis=0, tiled=True, axis_index_groups=Y_GRO...  28.7 us
    ppermute x4, starting transfers between devices, per_device(): lax.ppermute(half, AXES, z_shift(by))  23.7 us
    ppermute x1, waiting for transfers between devices, per_device(): lax.ppermute(away, 'row', FAR_SWAP)  17.3 us
    all_to_all x1, waiting for transfers between devices, per_device(): lax.all_to_all(cross, 'col', split_axis=0, concat_axis=0, tiled=True, axi...  16.9 us
    ppermute x1, starting transfers between devices, per_device(): theirs = lax.ppermute(mine, 'col', PLANE_SWAP)  15.1 us
    pallas_call x1, Pallas kernels, contract(): pl.pallas_call(contract_kernel, out_shape=(shape, shape), in_specs=[SMEM]...  11.8 us
  transfers between devices with their start and end apart: 15, of which 4 were waited for; matrix products, arithmetic and copies ran while one was open for 2% of the time, Pallas kernels for 3%

profile of v10, /device:TPU:6, one launch (start us, length us, event | category | flops | bytes accessed | tf_op | source)
XLA Modules:
  0.0 257.4 jit_solution(10187022177320026961)
XLA Ops:
  6.5 0.0 all-gather.3.cloned.1.call-start
  6.5 1.6 pad.8
  8.1 0.0 all-gather.3.cloned.1.call-update
  8.1 0.0 all-gather.5.cloned.1.call-start
  8.2 15.1 %collective-permute-start = (bf16[24,2048]{1,0:T(8,128)(2,1)}, bf16[24,2048]{1,0:T(8,128)(2,1)S(1)}, u32[]{:S(2)}, u32[]{:S(2)}) collective-permute-start(bf16[24,2048]{1,0:T(8,128)(2,1)} %bitcast.26), channel_id=1, source_target_pairs={{0,8},{1,9},{2,10},{3,11},{4,12},{5,13},{6,14},{7,15},{8,0},{9,1},... | collective-permute-start | bytes 294920 | tf_op jit(solution)/shard_map/ppermute | solution.py:237
  23.4 0.1 pad_add_fusion.where
  23.5 0.0 copy-start.2
  23.5 0.7 bitcast_add_fusion.route
  24.1 0.0 copy-start.1
  24.2 1.2 copy-done.1
  25.4 4.9 %pack.1 = (bf16[32,136,128]{2,1,0:T(8,128)(2,1)}, bf16[32,136,128]{2,1,0:T(8,128)(2,1)S(1)}, bf16[32,16,128]{2,1,0:T(8,128)(2,1)S(1)}, bf16[32,16,128]{2,1,0:T(8,128)(2,1)S(1)}) custom-call(s32[4]{0:T(128)S(1)} %pad_add_fusion.where, s32[64]{0:T(128)S(1)} %bitcast_add_fusion.route, bf16[64,64,128]{2,1,0:T(8,128)(2,1)S(1)} %bitcast.19), custom_call_target="tpu_custom_call" | custom-call | bytes 4194304 | tf_op jit(solution)/shard_map/pack/pallas_call | solution.py:112
  30.3 0.1 fusion
  30.4 0.0 copy-done.2
  30.4 1.9 collective-permute-start.2
  32.4 5.7 %collective-permute-start.1 = (bf16[16,136,128]{2,1,0:T(8,128)(2,1)S(1)}, bf16[16,136,128]{2,1,0:T(8,128)(2,1)S(1)}, u32[]{:S(2)}, u32[]{:S(2)}) collective-permute-start(bf16[16,136,128]{2,1,0:T(8,128)(2,1)S(1)} %get-tuple-element.62), channel_id=1, source_target_pairs={{0,384},{1,385},{2,386},{3,387},{4,388},{5,389},{6,390},{7,391},{1... | collective-permute-start | bytes 1671176 | tf_op jit(solution)/shard_map/ppermute | solution.py:241
  38.1 0.7 slice_dynamic-update-slice_fusion.1
  38.8 0.0 collective-permute-done
  38.8 28.7 %all_gather.10.near = bf16[192,2048]{1,0:T(8,128)(2,1)S(1)} all-gather(bf16[24,2048]{1,0:T(8,128)(2,1)S(1)} %collective-permute-done), channel_id=1, replica_groups={{0,1,2,3,4,5,6,7},{8,9,10,11,12,13,14,15},{16,17,18,19,20,21,22,23},{24..., dimensions={0}, use_global_device_ids=true | all-gather | bytes 884736 | tf_op jit(solution)/shard_map/all_gather | solution.py:242
  67.4 0.0 copy-start.3
  67.4 0.0 collective-permute-done.2
  67.4 0.0 collective-permute-done.1
  67.5 0.0 all-gather.3.cloned.1.call-done
  67.5 2.4 slice.90
  69.8 0.0 all-gather.5.cloned.1.call-update
  69.9 8.1 %all-to-all-start = ((bf16[32,136,128]{2,1,0:T(8,128)(2,1)}), bf16[32,136,128]{2,1,0:T(8,128)(2,1)S(1)}, u32[]{:S(2)}, u32[]{:S(2)}) async-start(bf16[32,136,128]{2,1,0:T(8,128)(2,1)} %slice_dynamic-update-slice_fusion.1), calls=%async_computation | async-start | bytes 2228224 | tf_op jit(solution)/shard_map/all_to_all | solution.py:245
  78.0 2.7 %collective-permute-start.6 = (bf16[192,2048]{1,0:T(8,128)(2,1)S(1)}, bf16[192,2048]{1,0:T(8,128)(2,1)S(1)}, u32[]{:S(2)}, u32[]{:S(2)}) collective-permute-start(bf16[192,2048]{1,0:T(8,128)(2,1)S(1)} %all_gather.10.near), channel_id=1, source_target_pairs={{0,48},{1,49},{2,50},{3,51},{4,52},{5,53},{6,54},{7,55},{8,56},{9,... | collective-permute-start | bytes 2359304 | tf_op jit(solution)/shard_map/ppermute | solution.py:247
  80.7 0.0 copy-done.3
  80.7 4.3 %collective-permute-start.5 = (bf16[192,2048]{1,0:T(8,128)(2,1)S(1)}, bf16[192,2048]{1,0:T(8,128)(2,1)}, u32[]{:S(2)}, u32[]{:S(2)}) collective-permute-start(bf16[192,2048]{1,0:T(8,128)(2,1)S(1)} %all_gather.10.near), channel_id=1, source_target_pairs={{0,16},{1,17},{2,18},{3,19},{4,20},{5,21},{6,22},{7,23},{8,24},{9,... | collective-permute-start | bytes 2359304 | tf_op jit(solution)/shard_map/ppermute | solution.py:246
  85.0 14.2 %collective-permute-start.3 = (bf16[16,136,128]{2,1,0:T(8,128)(2,1)S(1)}, bf16[16,136,128]{2,1,0:T(8,128)(2,1)S(1)}, u32[]{:S(2)}, u32[]{:S(2)}) collective-permute-start(bf16[16,136,128]{2,1,0:T(8,128)(2,1)S(1)} %collective-permute-done.1), channel_id=1, source_target_pairs={{0,384},{1,385},{2,386},{3,387},{4,388},{5,389},{6,390},{7,391},{1... | collective-permute-start | bytes 1671176 | tf_op jit(solution)/shard_map/ppermute | solution.py:244
  99.2 1.9 collective-permute-start.4
  101.1 30.2 %collective-permute-done.3 = bf16[16,136,128]{2,1,0:T(8,128)(2,1)S(1)} collective-permute-done((bf16[16,136,128]{2,1,0:T(8,128)(2,1)S(1)}, bf16[16,136,128]{2,1,0:T(8,128)(2,1)S(1)}, u32[]{:S(2)}, u32[]{:S(2)}) %collective-permute-start.3) | collective-permute-done | bytes 557088 | tf_op jit(solution)/shard_map/ppermute | solution.py:244
  131.4 0.0 collective-permute-done.4
  131.4 1.1 pad_maximum_fusion
  132.5 0.0 collective-permute-done.6.right
  132.5 0.0 copy-start.4
  132.5 0.9 copy-done.4
  133.4 0.0 collective-permute-done.5.left
  133.4 0.0 all-to-all-done.arrived0
  133.4 9.5 %all-to-all-start.1 = ((bf16[32,136,128]{2,1,0:T(8,128)(2,1)}), bf16[32,136,128]{2,1,0:T(8,128)(2,1)S(1)}, u32[]{:S(2)}, u32[]{:S(2)}) async-start(bf16[32,136,128]{2,1,0:T(8,128)(2,1)} %pad_maximum_fusion), calls=%async_computation.1 | async-start | bytes 2228224 | tf_op jit(solution)/shard_map/all_to_all | solution.py:250
  142.9 1.0 slice.82
  144.0 1.0 slice.83
  145.0 2.7 %collective-permute-start.8 = (bf16[96,2048]{1,0:T(8,128)(2,1)S(1)}, bf16[96,2048]{1,0:T(8,128)(2,1)S(1)}, u32[]{:S(2)}, u32[]{:S(2)}) collective-permute-start(bf16[96,2048]{1,0:T(8,128)(2,1)S(1)} %slice.83), channel_id=1, source_target_pairs={{0,48},{1,49},{2,50},{3,51},{4,52},{5,53},{6,54},{7,55},{8,56},{9,... | collective-permute-start | bytes 1179656 | tf_op jit(solution)/shard_map/ppermute | solution.py:257
  147.7 4.3 %collective-permute-start.7 = (bf16[96,2048]{1,0:T(8,128)(2,1)S(1)}, bf16[96,2048]{1,0:T(8,128)(2,1)}, u32[]{:S(2)}, u32[]{:S(2)}) collective-permute-start(bf16[96,2048]{1,0:T(8,128)(2,1)S(1)} %slice.82), channel_id=1, source_target_pairs={{0,16},{1,17},{2,18},{3,19},{4,20},{5,21},{6,22},{7,23},{8,24},{9,... | collective-permute-start | bytes 1179656 | tf_op jit(solution)/shard_map/ppermute | solution.py:256
  152.1 16.9 %all-to-all-done.1.arrived1 = bf16[32,136,128]{2,1,0:T(8,128)(2,1)S(1)} async-done(((bf16[32,136,128]{2,1,0:T(8,128)(2,1)}), bf16[32,136,128]{2,1,0:T(8,128)(2,1)S(1)}, u32[]{:S(2)}, u32[]{:S(2)}) %all-to-all-start.1) | async-done | bytes 1114144 | tf_op jit(solution)/shard_map/all_to_all | solution.py:250
  169.0 3.1 %place.1.dense = bf16[2048,512]{1,0:T(8,128)(2,1)S(1)} custom-call(s32[32,2]{1,0:T(8,128)S(1)} %bitcast.20, s32[32,2]{1,0:T(8,128)S(1)} %bitcast.21, bf16[32,136,128]{2,1,0:T(8,128)(2,1)S(1)} %all-to-all-done.arrived0, bf16[32,136,128]{2,1,0:T(8,128)(2,1)S(1)} %all-to-all-done.1.arrived1), custom_call_target="tpu_custom_call" | custom-call | bytes 4194304 | tf_op jit(solution)/shard_map/place/pallas_call | solution.py:150
  172.1 0.0 copy-start
  172.1 1.4 copy-done
  173.5 0.0 collective-permute-done.8.far1
  173.5 0.0 copy-start.5
  173.5 0.0 collective-permute-done.7.far0
  173.5 0.0 all-gather.5.cloned.1.call-done.own
  173.6 0.7 copy-done.5
  174.3 11.8 %contract.1 = (f32[768,512]{1,0:T(8,128)}, f32[768,512]{1,0:T(8,128)}) custom-call(s32[4]{0:T(128)} %copy-done.2, bf16[768,2048]{1,0:T(8,128)(2,1)} %all-gather.5.cloned.1.call-done.own, bf16[192,2048]{1,0:T(8,128)(2,1)} %copy-done.3, bf16[192,2048]{1,0:T(8,128)(2,1)} %collective-permute-done.5.left, bf16[192,2048]{1,0:T(8,128)(2,1)} %copy-done.4, ...), custom_call_target="tpu_custom_call" | custom-call | flops 3221225472 | bytes 12582912 | tf_op jit(solution)/shard_map/contract/pallas_call | solution.py:210
  186.1 1.9 collective-permute-start.9
  188.0 3.6 %collective-permute-done.9 = f32[768,512]{1,0:T(8,128)S(1)} collective-permute-done((f32[768,512]{1,0:T(8,128)}, f32[768,512]{1,0:T(8,128)S(1)}, u32[]{:S(2)}, u32[]{:S(2)}) %collective-permute-start.9) | collective-permute-done | bytes 1572896 | tf_op jit(solution)/shard_map/ppermute | solution.py:262
  191.6 1.8 add.32
  193.3 34.9 %all_to_all.15 = f32[3,256,512]{2,1,0:T(8,128)S(1)} all-to-all(f32[3,256,512]{2,1,0:T(8,128)S(1)} %bitcast.22), channel_id=1, replica_groups={{0,128,256},{64,192,320},{384,512,640},{448,576,704},{1,129,257},{65,19..., dimensions={0} | all-to-all | bytes 3145728 | tf_op jit(solution)/shard_map/all_to_all | solution.py:263
  228.3 0.1 slice_reduce_fusion
  228.4 4.2 %collective-permute-start.10 = (f32[128,512]{1,0:T(8,128)S(1)}, f32[128,512]{1,0:T(8,128)S(1)}, u32[]{:S(2)}, u32[]{:S(2)}) collective-permute-start(f32[128,512]{1,0:T(8,128)S(1)} %get-tuple-element.59), channel_id=1, source_target_pairs={{0,384},{64,448},{128,512},{192,576},{256,640},{320,704},{384,0},{... | collective-permute-start | bytes 786440 | tf_op jit(solution)/shard_map/ppermute | solution.py:267
  232.6 17.3 %collective-permute-done.10 = f32[128,512]{1,0:T(8,128)S(1)} collective-permute-done((f32[128,512]{1,0:T(8,128)S(1)}, f32[128,512]{1,0:T(8,128)S(1)}, u32[]{:S(2)}, u32[]{:S(2)}) %collective-permute-start.10) | collective-permute-done | bytes 262176 | tf_op jit(solution)/shard_map/ppermute | solution.py:267
  249.9 0.7 add_convert_fusion
  (3 shorter events, 0.1 us)
Async XLA Ops:
  6.5 60.9 %all-gather.3.cloned.1.call-start = ((), (), s32[]{:S(2)}) async-start(), calls=%async_computation.3 | async-start | bytes 1179648 | tf_op jit(solution)/shard_map/all_gather | solution.py:236
  8.1 165.4 %all-gather.5.cloned.1.call-start = ((), (), s32[]{:S(2)}) async-start(), calls=%async_computation.4 | async-start | bytes 3932160 | tf_op jit(solution)/shard_map/all_gather | solution.py:254
  8.2 30.6 %collective-permute-start = (bf16[24,2048]{1,0:T(8,128)(2,1)}, bf16[24,2048]{1,0:T(8,128)(2,1)S(1)}, u32[]{:S(2)}, u32[]{:S(2)}) collective-permute-start(bf16[24,2048]{1,0:T(8,128)(2,1)} %bitcast.26), channel_id=1, source_target_pairs={{0,8},{1,9},{2,10},{3,11},{4,12},{5,13},{6,14},{7,15},{8,0},{9,1},... | collective-permute-start | bytes 294920 | tf_op jit(solution)/shard_map/ppermute | solution.py:237
  23.5 7.0 %copy-start.2 = (s32[4]{0:T(128)}, s32[4]{0:T(128)S(1)}, u32[]{:S(2)}) copy-start(s32[4]{0:T(128)S(1)} %pad_add_fusion.where) | copy-start | bytes 52
  24.1 1.2 copy-start.1
  30.4 37.0 %collective-permute-start.2 = (bf16[16,136,128]{2,1,0:T(8,128)(2,1)S(1)}, bf16[16,136,128]{2,1,0:T(8,128)(2,1)S(1)}, u32[]{:S(2)}, u32[]{:S(2)}) collective-permute-start(bf16[16,136,128]{2,1,0:T(8,128)(2,1)S(1)} %get-tuple-element.61), channel_id=1, source_target_pairs={{0,392},{1,393},{2,394},{3,395},{4,396},{5,397},{6,398},{7,399},{1... | collective-permute-start | bytes 1671176 | tf_op jit(solution)/shard_map/ppermute | solution.py:241
  32.4 35.1 %collective-permute-start.1 = (bf16[16,136,128]{2,1,0:T(8,128)(2,1)S(1)}, bf16[16,136,128]{2,1,0:T(8,128)(2,1)S(1)}, u32[]{:S(2)}, u32[]{:S(2)}) collective-permute-start(bf16[16,136,128]{2,1,0:T(8,128)(2,1)S(1)} %get-tuple-element.62), channel_id=1, source_target_pairs={{0,384},{1,385},{2,386},{3,387},{4,388},{5,389},{6,390},{7,391},{1... | collective-permute-start | bytes 1671176 | tf_op jit(solution)/shard_map/ppermute | solution.py:241
  67.4 13.2 %copy-start.3 = (bf16[192,2048]{1,0:T(8,128)(2,1)}, bf16[192,2048]{1,0:T(8,128)(2,1)S(1)}, u32[]{:S(2)}) copy-start(bf16[192,2048]{1,0:T(8,128)(2,1)S(1)} %all_gather.10.near) | copy-start | bytes 2359300
  69.9 63.5 %all-to-all-start = ((bf16[32,136,128]{2,1,0:T(8,128)(2,1)}), bf16[32,136,128]{2,1,0:T(8,128)(2,1)S(1)}, u32[]{:S(2)}, u32[]{:S(2)}) async-start(bf16[32,136,128]{2,1,0:T(8,128)(2,1)} %slice_dynamic-update-slice_fusion.1), calls=%async_computation | async-start | bytes 2228224 | tf_op jit(solution)/shard_map/all_to_all | solution.py:245
  78.0 54.5 %collective-permute-start.6 = (bf16[192,2048]{1,0:T(8,128)(2,1)S(1)}, bf16[192,2048]{1,0:T(8,128)(2,1)S(1)}, u32[]{:S(2)}, u32[]{:S(2)}) collective-permute-start(bf16[192,2048]{1,0:T(8,128)(2,1)S(1)} %all_gather.10.near), channel_id=1, source_target_pairs={{0,48},{1,49},{2,50},{3,51},{4,52},{5,53},{6,54},{7,55},{8,56},{9,... | collective-permute-start | bytes 2359304 | tf_op jit(solution)/shard_map/ppermute | solution.py:247
  80.7 52.7 %collective-permute-start.5 = (bf16[192,2048]{1,0:T(8,128)(2,1)S(1)}, bf16[192,2048]{1,0:T(8,128)(2,1)}, u32[]{:S(2)}, u32[]{:S(2)}) collective-permute-start(bf16[192,2048]{1,0:T(8,128)(2,1)S(1)} %all_gather.10.near), channel_id=1, source_target_pairs={{0,16},{1,17},{2,18},{3,19},{4,20},{5,21},{6,22},{7,23},{8,24},{9,... | collective-permute-start | bytes 2359304 | tf_op jit(solution)/shard_map/ppermute | solution.py:246
  85.0 46.4 %collective-permute-start.3 = (bf16[16,136,128]{2,1,0:T(8,128)(2,1)S(1)}, bf16[16,136,128]{2,1,0:T(8,128)(2,1)S(1)}, u32[]{:S(2)}, u32[]{:S(2)}) collective-permute-start(bf16[16,136,128]{2,1,0:T(8,128)(2,1)S(1)} %collective-permute-done.1), channel_id=1, source_target_pairs={{0,384},{1,385},{2,386},{3,387},{4,388},{5,389},{6,390},{7,391},{1... | collective-permute-start | bytes 1671176 | tf_op jit(solution)/shard_map/ppermute | solution.py:244
  99.2 32.2 %collective-permute-start.4 = (bf16[16,136,128]{2,1,0:T(8,128)(2,1)S(1)}, bf16[16,136,128]{2,1,0:T(8,128)(2,1)S(1)}, u32[]{:S(2)}, u32[]{:S(2)}) collective-permute-start(bf16[16,136,128]{2,1,0:T(8,128)(2,1)S(1)} %collective-permute-done.2), channel_id=1, source_target_pairs={{0,392},{1,393},{2,394},{3,395},{4,396},{5,397},{6,398},{7,399},{1... | collective-permute-start | bytes 1671176 | tf_op jit(solution)/shard_map/ppermute | solution.py:244
  132.5 0.9 copy-start.4
  133.4 35.6 %all-to-all-start.1 = ((bf16[32,136,128]{2,1,0:T(8,128)(2,1)}), bf16[32,136,128]{2,1,0:T(8,128)(2,1)S(1)}, u32[]{:S(2)}, u32[]{:S(2)}) async-start(bf16[32,136,128]{2,1,0:T(8,128)(2,1)} %pad_maximum_fusion), calls=%async_computation.1 | async-start | bytes 2228224 | tf_op jit(solution)/shard_map/all_to_all | solution.py:250
  145.0 28.5 %collective-permute-start.8 = (bf16[96,2048]{1,0:T(8,128)(2,1)S(1)}, bf16[96,2048]{1,0:T(8,128)(2,1)S(1)}, u32[]{:S(2)}, u32[]{:S(2)}) collective-permute-start(bf16[96,2048]{1,0:T(8,128)(2,1)S(1)} %slice.83), channel_id=1, source_target_pairs={{0,48},{1,49},{2,50},{3,51},{4,52},{5,53},{6,54},{7,55},{8,56},{9,... | collective-permute-start | bytes 1179656 | tf_op jit(solution)/shard_map/ppermute | solution.py:257
  147.7 25.8 %collective-permute-start.7 = (bf16[96,2048]{1,0:T(8,128)(2,1)S(1)}, bf16[96,2048]{1,0:T(8,128)(2,1)}, u32[]{:S(2)}, u32[]{:S(2)}) collective-permute-start(bf16[96,2048]{1,0:T(8,128)(2,1)S(1)} %slice.82), channel_id=1, source_target_pairs={{0,16},{1,17},{2,18},{3,19},{4,20},{5,21},{6,22},{7,23},{8,24},{9,... | collective-permute-start | bytes 1179656 | tf_op jit(solution)/shard_map/ppermute | solution.py:256
  172.1 1.4 copy-start
  173.5 0.7 copy-start.5
  186.1 5.5 %collective-permute-start.9 = (f32[768,512]{1,0:T(8,128)}, f32[768,512]{1,0:T(8,128)S(1)}, u32[]{:S(2)}, u32[]{:S(2)}) collective-permute-start(f32[768,512]{1,0:T(8,128)} %get-tuple-element.58), channel_id=1, source_target_pairs={{0,64},{64,0},{128,192},{192,128},{256,320},{320,256},{384,448},{4... | collective-permute-start | bytes 4718600 | tf_op jit(solution)/shard_map/ppermute | solution.py:262
  228.4 21.5 %collective-permute-start.10 = (f32[128,512]{1,0:T(8,128)S(1)}, f32[128,512]{1,0:T(8,128)S(1)}, u32[]{:S(2)}, u32[]{:S(2)}) collective-permute-start(f32[128,512]{1,0:T(8,128)S(1)} %get-tuple-element.59), channel_id=1, source_target_pairs={{0,384},{64,448},{128,512},{192,576},{256,640},{320,704},{384,0},{... | collective-permute-start | bytes 786440 | tf_op jit(solution)/shard_map/ppermute | solution.py:267
Sparse Core Ops, SparseCore 0:
  9.7 50.6 all-gather.2
  70.0 62.1 all-gather.4

commit v11 on v9

--- a/solution.py
+++ b/solution.py
@@ -95,7 +95,7 @@
     return out.at[:, CAP * rows :].set(labels[:, :LABEL_ROWS])
 
 
-def place_kernel(labels, arrived, dense):
+def place_kernel(labels, arrived, out, dense, sem):
     rows = (arrived.shape[1] - LABEL_ROWS) // CAP
     cols = arrived.shape[2]
 
@@ -115,14 +115,20 @@
                 col = pl.multiple_of(cell % CB * cols, cols)
                 dense[pl.ds(row, rows), pl.ds(col, cols)] = arrived[j, pl.ds(slot * rows, rows), :]
 
+    copy = pltpu.make_async_copy(dense, out, sem)
+    copy.start()
+    copy.wait()
+
 
 def place(labels, arrived, mu_rows):
+    shape = jax.ShapeDtypeStruct((mu_rows, CB * arrived.shape[2]), arrived.dtype)
     return pl.pallas_call(
         place_kernel,
-        out_shape=jax.ShapeDtypeStruct((mu_rows, CB * arrived.shape[2]), arrived.dtype),
+        out_shape=shape,
         in_specs=[SMEM, VMEM],
-        out_specs=VMEM,
-        compiler_params=pltpu.CompilerParams(vmem_limit_bytes=24 << 20),
+        out_specs=ANY,
+        scratch_shapes=[pltpu.VMEM(shape.shape, shape.dtype), pltpu.SemaphoreType.DMA(())],
+        compiler_params=pltpu.CompilerParams(vmem_limit_bytes=56 << 20),
         cost_estimate=pl.CostEstimate(flops=0, bytes_accessed=4 << 20, transcendentals=0),
         name="place",
     )(labels, arrived)
@@ -189,7 +195,7 @@
             pltpu.SemaphoreType.DMA((6,)),
             pltpu.SemaphoreType.DMA((NCORE,)),
         ],
-        compiler_params=pltpu.CompilerParams(vmem_limit_bytes=56 << 20),
+        compiler_params=pltpu.CompilerParams(vmem_limit_bytes=52 << 20),
         cost_estimate=pl.CostEstimate(flops=2 * occ * mu_rows * width, bytes_accessed=12 << 20, transcendentals=0),
         name="contract",
     )(where, own, near, left, right, far0, far1, dense)

time: 242 us -> 244 us (level)
  local copies, waits for them, and re-layouts: 8.42 us -> 4.51 us
  Pallas kernels: 17.2 us -> 20.4 us
    unnamed x14 -> x8, local copies, waits for them, and re-layouts: 4.02 us -> 1.24 us
  transfers between devices with their start and end apart: 10 -> 10, of which waited for: 7 -> 7; matrix products, arithmetic and copies ran while one was open for 2% -> 2% of each run, Pallas kernels for 2% -> 4%
where the time goes in v11:
time: 244 us; the launch traced here: 241 us
  waiting for transfers between devices  76.5 us (31%)
  blocking collectives  67.3 us (28%)
  starting transfers between devices  53.8 us (22%)
  Pallas kernels  20.4 us (8%)
  between operations  13.6 us (6%)
  other arithmetic  4.91 us (2%)
  local copies, waits for them, and re-layouts  4.51 us (2%)
    ppermute x1, waiting for transfers between devices, per_device(): right = lax.ppermute(near, 'col', x_shift(-1))  45 us
    all_to_all x1, blocking collectives, per_device(): lax.all_to_all(share.reshape(NEAR, 2 * OUT_ROWS, -1), 'row', split_axis=0...  38.6 us
    all_gather x1, blocking collectives, per_device(): lax.all_gather(theirs, 'col', axis=0, tiled=True, axis_index_groups=Y_GRO...  28.7 us
    all_to_all x1, starting transfers between devices, per_device(): lax.all_to_all(outgoing, 'col', split_axis=0, concat_axis=0, tiled=True)  16.3 us
    ppermute x1, waiting for transfers between devices, per_device(): lax.ppermute(away, 'row', FAR_SWAP)  16 us
    ppermute x1, starting transfers between devices, per_device(): theirs = lax.ppermute(mine, 'col', PLANE_SWAP)  15.1 us
    pallas_call x1, Pallas kernels, contract(): pl.pallas_call(contract_kernel, out_shape=(shape, shape), in_specs=[SMEM]...  11.6 us
    ppermute x1, starting transfers between devices, per_device(): lax.ppermute(away, 'row', FAR_SWAP)  6.24 us
  transfers between devices with their start and end apart: 10, of which 7 were waited for; matrix products, arithmetic and copies ran while one was open for 2% of the time, Pallas kernels for 4%

profile of v11, /device:TPU:6, one launch (start us, length us, event | category | flops | bytes accessed | tf_op | source)
XLA Modules:
  0.0 241.0 jit_solution(13820977343631590229)
XLA Ops:
  6.5 0.0 all-gather.3.cloned.1.call-start
  6.5 1.6 pad.6
  8.1 0.0 all-gather.3.cloned.1.call-update
  8.1 15.1 %collective-permute-start = (bf16[24,2048]{1,0:T(8,128)(2,1)}, bf16[24,2048]{1,0:T(8,128)(2,1)S(1)}, u32[]{:S(2)}, u32[]{:S(2)}) collective-permute-start(bf16[24,2048]{1,0:T(8,128)(2,1)} %bitcast.24), channel_id=1, source_target_pairs={{0,8},{1,9},{2,10},{3,11},{4,12},{5,13},{6,14},{7,15},{8,0},{9,1},... | collective-permute-start | bytes 294920 | tf_op jit(solution)/shard_map/ppermute | solution.py:213
  23.3 0.7 bitcast_add_fusion.route
  24.0 0.0 copy-start
  24.0 1.2 copy-done
  25.2 3.5 %pack.1 = (bf16[64,136,128]{2,1,0:T(8,128)(2,1)}, bf16[64,16,128]{2,1,0:T(8,128)(2,1)S(1)}) custom-call(s32[64]{0:T(128)S(1)} %bitcast_add_fusion.route, bf16[64,64,128]{2,1,0:T(8,128)(2,1)S(1)} %bitcast.18), custom_call_target="tpu_custom_call" | custom-call | bytes 4194304 | tf_op jit(solution)/shard_map/pack/pallas_call | solution.py:82
  28.7 0.7 slice_dynamic-update-slice_fusion
  29.4 0.0 collective-permute-done
  29.4 28.7 %all_gather.10.near = bf16[192,2048]{1,0:T(8,128)(2,1)S(1)} all-gather(bf16[24,2048]{1,0:T(8,128)(2,1)S(1)} %collective-permute-done), channel_id=1, replica_groups={{0,1,2,3,4,5,6,7},{8,9,10,11,12,13,14,15},{16,17,18,19,20,21,22,23},{24..., dimensions={0}, use_global_device_ids=true | all-gather | bytes 884736 | tf_op jit(solution)/shard_map/all_gather | solution.py:216
  58.2 3.4 %all-gather.3.cloned.1.call-done = bf16[256,2048]{1,0:T(8,128)(2,1)} async-done(((bf16[32,2048]{1,0:T(8,128)(2,1)}), bf16[256,2048]{1,0:T(8,128)(2,1)}) %all-gather.3.cloned.1.call-update) | async-done | bytes 1048592 | tf_op jit(solution)/shard_map/all_gather | solution.py:212
  61.6 0.0 copy-start.1
  61.6 16.3 %all-to-all-start = ((bf16[64,136,128]{2,1,0:T(8,128)(2,1)}), bf16[64,136,128]{2,1,0:T(8,128)(2,1)}, u32[]{:S(2)}, u32[]{:S(2)}) async-start(bf16[64,136,128]{2,1,0:T(8,128)(2,1)} %slice_dynamic-update-slice_fusion), calls=%async_computation | async-start | bytes 4456448 | tf_op jit(solution)/shard_map/all_to_all | solution.py:218
  77.9 0.0 all-gather.5.cloned.1.call-start
  77.9 0.0 copy-done.1
  77.9 1.0 slice.50
  78.9 0.0 all-gather.5.cloned.1.call-update
  78.9 2.7 %collective-permute-start.2 = (bf16[192,2048]{1,0:T(8,128)(2,1)S(1)}, bf16[192,2048]{1,0:T(8,128)(2,1)S(1)}, u32[]{:S(2)}, u32[]{:S(2)}) collective-permute-start(bf16[192,2048]{1,0:T(8,128)(2,1)S(1)} %all_gather.10.near), channel_id=1, source_target_pairs={{0,48},{1,49},{2,50},{3,51},{4,52},{5,53},{6,54},{7,55},{8,56},{9,... | collective-permute-start | bytes 2359304 | tf_op jit(solution)/shard_map/ppermute | solution.py:223
  81.6 4.4 %collective-permute-start.1 = (bf16[192,2048]{1,0:T(8,128)(2,1)S(1)}, bf16[192,2048]{1,0:T(8,128)(2,1)S(1)}, u32[]{:S(2)}, u32[]{:S(2)}) collective-permute-start(bf16[192,2048]{1,0:T(8,128)(2,1)S(1)} %all_gather.10.near), channel_id=1, source_target_pairs={{0,16},{1,17},{2,18},{3,19},{4,20},{5,21},{6,22},{7,23},{8,24},{9,... | collective-permute-start | bytes 2359304 | tf_op jit(solution)/shard_map/ppermute | solution.py:222
  86.0 45.0 %collective-permute-done.2.right = bf16[192,2048]{1,0:T(8,128)(2,1)S(1)} collective-permute-done((bf16[192,2048]{1,0:T(8,128)(2,1)S(1)}, bf16[192,2048]{1,0:T(8,128)(2,1)S(1)}, u32[]{:S(2)}, u32[]{:S(2)}) %collective-permute-start.2) | collective-permute-done | bytes 786464 | tf_op jit(solution)/shard_map/ppermute | solution.py:223
  130.9 0.0 copy-start.2
  131.0 1.9 collective-permute-start.4
  132.9 0.0 collective-permute-done.1.left
  132.9 0.0 copy-start.3
  132.9 5.1 %collective-permute-start.3 = (bf16[96,2048]{1,0:T(8,128)(2,1)S(1)}, bf16[96,2048]{1,0:T(8,128)(2,1)S(1)}, u32[]{:S(2)}, u32[]{:S(2)}) collective-permute-start(bf16[96,2048]{1,0:T(8,128)(2,1)S(1)} %slice.51), channel_id=1, source_target_pairs={{0,16},{1,17},{2,18},{3,19},{4,20},{5,21},{6,22},{7,23},{8,24},{9,... | collective-permute-start | bytes 1179656 | tf_op jit(solution)/shard_map/ppermute | solution.py:225
  138.1 0.0 copy-done.3
  138.1 0.1 pad_add_fusion.where
  138.2 0.0 all-to-all-done.arrived
  138.2 1.5 slice_convert_fusion
  139.8 5.3 %place.1.dense = bf16[2048,512]{1,0:T(8,128)(2,1)} custom-call(s32[64,2]{1,0:T(8,128)} %bitcast.22, bf16[64,136,128]{2,1,0:T(8,128)(2,1)} %all-to-all-done.arrived), custom_call_target="tpu_custom_call" | custom-call | bytes 4194304 | tf_op jit(solution)/shard_map/place/pallas_call | solution.py:125
  145.1 0.0 copy-done.2
  145.1 5.2 %collective-permute-done.4.far1 = bf16[96,2048]{1,0:T(8,128)(2,1)S(1)} collective-permute-done((bf16[96,2048]{1,0:T(8,128)(2,1)S(1)}, bf16[96,2048]{1,0:T(8,128)(2,1)S(1)}, u32[]{:S(2)}, u32[]{:S(2)}) %collective-permute-start.4) | collective-permute-done | bytes 393248 | tf_op jit(solution)/shard_map/ppermute | solution.py:226
  150.2 1.5 collective-permute-done.3.far0
  151.8 1.9 all-gather.5.cloned.1.call-done.own
  153.6 11.6 %contract.1 = (f32[768,512]{1,0:T(8,128)}, f32[768,512]{1,0:T(8,128)}) custom-call(s32[4]{0:T(128)S(1)} %pad_add_fusion.where, bf16[768,2048]{1,0:T(8,128)(2,1)} %all-gather.5.cloned.1.call-done.own, bf16[192,2048]{1,0:T(8,128)(2,1)S(1)} %all_gather.10.near, bf16[192,2048]{1,0:T(8,128)(2,1)} %copy-done.3, bf16[192,2048]{1,0:T(8,128)(2,1)} %copy-done.2, ...), custom_call_target="tpu_custom_call" | custom-call | flops 3221225472 | bytes 12582912 | tf_op jit(solution)/shard_map/contract/pallas_call | solution.py:186
  165.2 1.9 collective-permute-start.5
  167.2 3.6 %collective-permute-done.5 = f32[768,512]{1,0:T(8,128)S(1)} collective-permute-done((f32[768,512]{1,0:T(8,128)}, f32[768,512]{1,0:T(8,128)S(1)}, u32[]{:S(2)}, u32[]{:S(2)}) %collective-permute-start.5) | collective-permute-done | bytes 1572896 | tf_op jit(solution)/shard_map/ppermute | solution.py:231
  170.7 1.8 add.30
  172.5 38.6 %all_to_all.10 = f32[3,256,512]{2,1,0:T(8,128)S(1)} all-to-all(f32[3,256,512]{2,1,0:T(8,128)S(1)} %bitcast.19), channel_id=1, replica_groups={{0,128,256},{64,192,320},{384,512,640},{448,576,704},{1,129,257},{65,19..., dimensions={0} | all-to-all | bytes 3145728 | tf_op jit(solution)/shard_map/all_to_all | solution.py:232
  211.1 0.1 slice_reduce_fusion
  211.2 6.2 %collective-permute-start.6 = (f32[128,512]{1,0:T(8,128)S(1)}, f32[128,512]{1,0:T(8,128)S(1)}, u32[]{:S(2)}, u32[]{:S(2)}) collective-permute-start(f32[128,512]{1,0:T(8,128)S(1)} %get-tuple-element.31), channel_id=1, source_target_pairs={{0,384},{64,448},{128,512},{192,576},{256,640},{320,704},{384,0},{... | collective-permute-start | bytes 786440 | tf_op jit(solution)/shard_map/ppermute | solution.py:236
  217.5 16.0 %collective-permute-done.6 = f32[128,512]{1,0:T(8,128)S(1)} collective-permute-done((f32[128,512]{1,0:T(8,128)S(1)}, f32[128,512]{1,0:T(8,128)S(1)}, u32[]{:S(2)}, u32[]{:S(2)}) %collective-permute-start.6) | collective-permute-done | bytes 262176 | tf_op jit(solution)/shard_map/ppermute | solution.py:236
  233.5 0.7 add_convert_fusion
  (2 shorter events, 0.1 us)
Async XLA Ops:
  6.5 55.0 %all-gather.3.cloned.1.call-start = ((), (), s32[]{:S(2)}) async-start(), calls=%async_computation.2 | async-start | bytes 1179648 | tf_op jit(solution)/shard_map/all_gather | solution.py:212
  8.1 21.3 %collective-permute-start = (bf16[24,2048]{1,0:T(8,128)(2,1)}, bf16[24,2048]{1,0:T(8,128)(2,1)S(1)}, u32[]{:S(2)}, u32[]{:S(2)}) collective-permute-start(bf16[24,2048]{1,0:T(8,128)(2,1)} %bitcast.24), channel_id=1, source_target_pairs={{0,8},{1,9},{2,10},{3,11},{4,12},{5,13},{6,14},{7,15},{8,0},{9,1},... | collective-permute-start | bytes 294920 | tf_op jit(solution)/shard_map/ppermute | solution.py:213
  24.0 1.2 copy-start
  61.6 16.3 %copy-start.1 = (bf16[256,2048]{1,0:T(8,128)(2,1)S(1)}, bf16[256,2048]{1,0:T(8,128)(2,1)}, u32[]{:S(2)}) copy-start(bf16[256,2048]{1,0:T(8,128)(2,1)} %all-gather.3.cloned.1.call-done) | copy-start | bytes 3145732
  61.6 76.7 %all-to-all-start = ((bf16[64,136,128]{2,1,0:T(8,128)(2,1)}), bf16[64,136,128]{2,1,0:T(8,128)(2,1)}, u32[]{:S(2)}, u32[]{:S(2)}) async-start(bf16[64,136,128]{2,1,0:T(8,128)(2,1)} %slice_dynamic-update-slice_fusion), calls=%async_computation | async-start | bytes 4456448 | tf_op jit(solution)/shard_map/all_to_all | solution.py:218
  77.9 75.8 %all-gather.5.cloned.1.call-start = ((), (), s32[]{:S(2)}) async-start(), calls=%async_computation.3 | async-start | bytes 3932160 | tf_op jit(solution)/shard_map/all_gather | solution.py:221
  78.9 52.0 %collective-permute-start.2 = (bf16[192,2048]{1,0:T(8,128)(2,1)S(1)}, bf16[192,2048]{1,0:T(8,128)(2,1)S(1)}, u32[]{:S(2)}, u32[]{:S(2)}) collective-permute-start(bf16[192,2048]{1,0:T(8,128)(2,1)S(1)} %all_gather.10.near), channel_id=1, source_target_pairs={{0,48},{1,49},{2,50},{3,51},{4,52},{5,53},{6,54},{7,55},{8,56},{9,... | collective-permute-start | bytes 2359304 | tf_op jit(solution)/shard_map/ppermute | solution.py:223
  81.6 51.3 %collective-permute-start.1 = (bf16[192,2048]{1,0:T(8,128)(2,1)S(1)}, bf16[192,2048]{1,0:T(8,128)(2,1)S(1)}, u32[]{:S(2)}, u32[]{:S(2)}) collective-permute-start(bf16[192,2048]{1,0:T(8,128)(2,1)S(1)} %all_gather.10.near), channel_id=1, source_target_pairs={{0,16},{1,17},{2,18},{3,19},{4,20},{5,21},{6,22},{7,23},{8,24},{9,... | collective-permute-start | bytes 2359304 | tf_op jit(solution)/shard_map/ppermute | solution.py:222
  130.9 14.1 %copy-start.2 = (bf16[192,2048]{1,0:T(8,128)(2,1)}, bf16[192,2048]{1,0:T(8,128)(2,1)S(1)}, u32[]{:S(2)}) copy-start(bf16[192,2048]{1,0:T(8,128)(2,1)S(1)} %collective-permute-done.2.right) | copy-start | bytes 2359300
  131.0 19.3 %collective-permute-start.4 = (bf16[96,2048]{1,0:T(8,128)(2,1)S(1)}, bf16[96,2048]{1,0:T(8,128)(2,1)S(1)}, u32[]{:S(2)}, u32[]{:S(2)}) collective-permute-start(bf16[96,2048]{1,0:T(8,128)(2,1)S(1)} %slice.52), channel_id=1, source_target_pairs={{0,48},{1,49},{2,50},{3,51},{4,52},{5,53},{6,54},{7,55},{8,56},{9,... | collective-permute-start | bytes 1179656 | tf_op jit(solution)/shard_map/ppermute | solution.py:226
  132.9 5.2 %copy-start.3 = (bf16[192,2048]{1,0:T(8,128)(2,1)}, bf16[192,2048]{1,0:T(8,128)(2,1)S(1)}, u32[]{:S(2)}) copy-start(bf16[192,2048]{1,0:T(8,128)(2,1)S(1)} %collective-permute-done.1.left) | copy-start | bytes 2359300
  132.9 18.8 %collective-permute-start.3 = (bf16[96,2048]{1,0:T(8,128)(2,1)S(1)}, bf16[96,2048]{1,0:T(8,128)(2,1)S(1)}, u32[]{:S(2)}, u32[]{:S(2)}) collective-permute-start(bf16[96,2048]{1,0:T(8,128)(2,1)S(1)} %slice.51), channel_id=1, source_target_pairs={{0,16},{1,17},{2,18},{3,19},{4,20},{5,21},{6,22},{7,23},{8,24},{9,... | collective-permute-start | bytes 1179656 | tf_op jit(solution)/shard_map/ppermute | solution.py:225
  165.2 5.5 %collective-permute-start.5 = (f32[768,512]{1,0:T(8,128)}, f32[768,512]{1,0:T(8,128)S(1)}, u32[]{:S(2)}, u32[]{:S(2)}) collective-permute-start(f32[768,512]{1,0:T(8,128)} %get-tuple-element.30), channel_id=1, source_target_pairs={{0,64},{64,0},{128,192},{192,128},{256,320},{320,256},{384,448},{4... | collective-permute-start | bytes 4718600 | tf_op jit(solution)/shard_map/ppermute | solution.py:231
  211.2 22.3 %collective-permute-start.6 = (f32[128,512]{1,0:T(8,128)S(1)}, f32[128,512]{1,0:T(8,128)S(1)}, u32[]{:S(2)}, u32[]{:S(2)}) collective-permute-start(f32[128,512]{1,0:T(8,128)S(1)} %get-tuple-element.31), channel_id=1, source_target_pairs={{0,384},{64,448},{128,512},{192,576},{256,640},{320,704},{384,0},{... | collective-permute-start | bytes 786440 | tf_op jit(solution)/shard_map/ppermute | solution.py:236
Sparse Core Ops, SparseCore 0:
  9.7 51.7 all-gather.2
  81.1 72.4 all-gather.4

commit v12 on v9

--- a/solution.py
+++ b/solution.py
@@ -189,7 +189,7 @@
             pltpu.SemaphoreType.DMA((6,)),
             pltpu.SemaphoreType.DMA((NCORE,)),
         ],
-        compiler_params=pltpu.CompilerParams(vmem_limit_bytes=56 << 20),
+        compiler_params=pltpu.CompilerParams(vmem_limit_bytes=52 << 20),
         cost_estimate=pl.CostEstimate(flops=2 * occ * mu_rows * width, bytes_accessed=12 << 20, transcendentals=0),
         name="contract",
     )(where, own, near, left, right, far0, far1, dense)

time: 242 us -> 242 us (level)
  no operation moved by 1% of the time
where the time goes in v12:
time: 242 us; the launch traced here: 239 us
  waiting for transfers between devices  75.5 us (31%)
  blocking collectives  65.3 us (27%)
  starting transfers between devices  53.6 us (22%)
  Pallas kernels  17 us (7%)
  between operations  13.6 us (6%)
  local copies, waits for them, and re-layouts  10.2 us (4%)
  other arithmetic  3.39 us (1%)
    ppermute x1, waiting for transfers between devices, per_device(): right = lax.ppermute(near, 'col', x_shift(-1))  45 us
    all_to_all x1, blocking collectives, per_device(): lax.all_to_all(share.reshape(NEAR, 2 * OUT_ROWS, -1), 'row', split_axis=0...  36.3 us
    all_gather x1, blocking collectives, per_device(): lax.all_gather(theirs, 'col', axis=0, tiled=True, axis_index_groups=Y_GRO...  29 us
    all_to_all x1, starting transfers between devices, per_device(): lax.all_to_all(outgoing, 'col', split_axis=0, concat_axis=0, tiled=True)  16.2 us
    ppermute x1, waiting for transfers between devices, per_device(): lax.ppermute(away, 'row', FAR_SWAP)  16 us
    ppermute x1, starting transfers between devices, per_device(): theirs = lax.ppermute(mine, 'col', PLANE_SWAP)  15.1 us
    pallas_call x1, Pallas kernels, contract(): pl.pallas_call(contract_kernel, out_shape=(shape, shape), in_specs=[SMEM]...  11.6 us
    ppermute x1, waiting for transfers between devices, per_device(): far1 = lax.ppermute(right[cut:], 'col', x_shift(-1))  6.56 us
  transfers between devices with their start and end apart: 10, of which 7 were waited for; matrix products, arithmetic and copies ran while one was open for 2% of the time, Pallas kernels for 2%

profile of v12, /device:TPU:6, one launch (start us, length us, event | category | flops | bytes accessed | tf_op | source)
XLA Modules:
  0.0 238.6 jit_solution(438386814544510521)
XLA Ops:
  6.5 0.0 all-gather.3.cloned.1.call-start
  6.5 1.6 pad.6
  8.1 0.0 all-gather.3.cloned.1.call-update
  8.1 15.1 %collective-permute-start = (bf16[24,2048]{1,0:T(8,128)(2,1)}, bf16[24,2048]{1,0:T(8,128)(2,1)S(1)}, u32[]{:S(2)}, u32[]{:S(2)}) collective-permute-start(bf16[24,2048]{1,0:T(8,128)(2,1)} %bitcast.24), channel_id=1, source_target_pairs={{0,8},{1,9},{2,10},{3,11},{4,12},{5,13},{6,14},{7,15},{8,0},{9,1},... | collective-permute-start | bytes 294920 | tf_op jit(solution)/shard_map/ppermute | solution.py:207
  23.3 0.7 bitcast_add_fusion.route
  24.0 0.0 copy-start.2
  24.0 1.2 copy-done.2
  25.2 2.1 pack.1
  27.3 0.0 copy-start
  27.3 1.4 copy-done
  28.7 0.7 slice_dynamic-update-slice_fusion
  29.4 0.0 collective-permute-done
  29.4 29.0 %all_gather.10.near = bf16[192,2048]{1,0:T(8,128)(2,1)S(1)} all-gather(bf16[24,2048]{1,0:T(8,128)(2,1)S(1)} %collective-permute-done), channel_id=1, replica_groups={{0,1,2,3,4,5,6,7},{8,9,10,11,12,13,14,15},{16,17,18,19,20,21,22,23},{24..., dimensions={0}, use_global_device_ids=true | all-gather | bytes 884736 | tf_op jit(solution)/shard_map/all_gather | solution.py:210
  58.4 2.9 %all-gather.3.cloned.1.call-done = bf16[256,2048]{1,0:T(8,128)(2,1)} async-done(((bf16[32,2048]{1,0:T(8,128)(2,1)}), bf16[256,2048]{1,0:T(8,128)(2,1)}) %all-gather.3.cloned.1.call-update) | async-done | bytes 1048592 | tf_op jit(solution)/shard_map/all_gather | solution.py:206
  61.4 16.2 %all-to-all-start = ((bf16[64,136,128]{2,1,0:T(8,128)(2,1)}), bf16[64,136,128]{2,1,0:T(8,128)(2,1)S(1)}, u32[]{:S(2)}, u32[]{:S(2)}) async-start(bf16[64,136,128]{2,1,0:T(8,128)(2,1)} %slice_dynamic-update-slice_fusion), calls=%async_computation | async-start | bytes 4456448 | tf_op jit(solution)/shard_map/all_to_all | solution.py:212
  77.6 0.0 all-gather.5.cloned.1.call-start
  77.6 2.1 slice.50
  79.7 0.0 all-gather.5.cloned.1.call-update
  79.7 2.7 %collective-permute-start.2 = (bf16[192,2048]{1,0:T(8,128)(2,1)S(1)}, bf16[192,2048]{1,0:T(8,128)(2,1)S(1)}, u32[]{:S(2)}, u32[]{:S(2)}) collective-permute-start(bf16[192,2048]{1,0:T(8,128)(2,1)S(1)} %all_gather.10.near), channel_id=1, source_target_pairs={{0,48},{1,49},{2,50},{3,51},{4,52},{5,53},{6,54},{7,55},{8,56},{9,... | collective-permute-start | bytes 2359304 | tf_op jit(solution)/shard_map/ppermute | solution.py:217
  82.4 4.4 %collective-permute-start.1 = (bf16[192,2048]{1,0:T(8,128)(2,1)S(1)}, bf16[192,2048]{1,0:T(8,128)(2,1)S(1)}, u32[]{:S(2)}, u32[]{:S(2)}) collective-permute-start(bf16[192,2048]{1,0:T(8,128)(2,1)S(1)} %all_gather.10.near), channel_id=1, source_target_pairs={{0,16},{1,17},{2,18},{3,19},{4,20},{5,21},{6,22},{7,23},{8,24},{9,... | collective-permute-start | bytes 2359304 | tf_op jit(solution)/shard_map/ppermute | solution.py:216
  86.8 45.0 %collective-permute-done.2.right = bf16[192,2048]{1,0:T(8,128)(2,1)S(1)} collective-permute-done((bf16[192,2048]{1,0:T(8,128)(2,1)S(1)}, bf16[192,2048]{1,0:T(8,128)(2,1)S(1)}, u32[]{:S(2)}, u32[]{:S(2)}) %collective-permute-start.2) | collective-permute-done | bytes 786464 | tf_op jit(solution)/shard_map/ppermute | solution.py:217
  131.8 0.0 copy-start.3
  131.8 0.8 slice.52
  132.7 1.9 collective-permute-start.4
  134.6 0.0 collective-permute-done.1.left
  134.6 0.0 copy-done.3
  134.6 0.0 copy-start.4
  134.6 0.8 slice.51
  135.5 0.2 copy-done.4
  135.6 5.1 %collective-permute-start.3 = (bf16[96,2048]{1,0:T(8,128)(2,1)}, bf16[96,2048]{1,0:T(8,128)(2,1)}, u32[]{:S(2)}, u32[]{:S(2)}) collective-permute-start(bf16[96,2048]{1,0:T(8,128)(2,1)} %slice.51), channel_id=1, source_target_pairs={{0,16},{1,17},{2,18},{3,19},{4,20},{5,21},{6,22},{7,23},{8,24},{9,... | collective-permute-start | bytes 1179656 | tf_op jit(solution)/shard_map/ppermute | solution.py:219
  140.8 0.1 pad_add_fusion.where
  140.9 0.0 all-to-all-done.arrived
  140.9 3.3 %place.1.dense = bf16[2048,512]{1,0:T(8,128)(2,1)S(1)} custom-call(s32[64,2]{1,0:T(8,128)S(1)} %bitcast.19, bf16[64,136,128]{2,1,0:T(8,128)(2,1)S(1)} %all-to-all-done.arrived), custom_call_target="tpu_custom_call" | custom-call | bytes 4194304 | tf_op jit(solution)/shard_map/place/pallas_call | solution.py:120
  144.3 0.0 copy-start.1
  144.3 1.3 copy-done.1
  145.6 6.6 %collective-permute-done.4.far1 = bf16[96,2048]{1,0:T(8,128)(2,1)S(1)} collective-permute-done((bf16[96,2048]{1,0:T(8,128)(2,1)}, bf16[96,2048]{1,0:T(8,128)(2,1)S(1)}, u32[]{:S(2)}, u32[]{:S(2)}) %collective-permute-start.4) | collective-permute-done | bytes 393248 | tf_op jit(solution)/shard_map/ppermute | solution.py:220
  152.2 0.9 collective-permute-done.3.far0
  153.1 0.4 all-gather.5.cloned.1.call-done.own
  153.5 11.6 %contract.1 = (f32[768,512]{1,0:T(8,128)}, f32[768,512]{1,0:T(8,128)}) custom-call(s32[4]{0:T(128)S(1)} %pad_add_fusion.where, bf16[768,2048]{1,0:T(8,128)(2,1)} %all-gather.5.cloned.1.call-done.own, bf16[192,2048]{1,0:T(8,128)(2,1)S(1)} %all_gather.10.near, bf16[192,2048]{1,0:T(8,128)(2,1)} %copy-done.4, bf16[192,2048]{1,0:T(8,128)(2,1)} %copy-done.3, ...), custom_call_target="tpu_custom_call" | custom-call | flops 3221225472 | bytes 12582912 | tf_op jit(solution)/shard_map/contract/pallas_call | solution.py:180
  165.1 1.9 collective-permute-start.5
  167.0 3.6 %collective-permute-done.5 = f32[768,512]{1,0:T(8,128)S(1)} collective-permute-done((f32[768,512]{1,0:T(8,128)}, f32[768,512]{1,0:T(8,128)S(1)}, u32[]{:S(2)}, u32[]{:S(2)}) %collective-permute-start.5) | collective-permute-done | bytes 1572896 | tf_op jit(solution)/shard_map/ppermute | solution.py:225
  170.6 1.8 add.30
  172.3 36.3 %all_to_all.10 = f32[3,256,512]{2,1,0:T(8,128)S(1)} all-to-all(f32[3,256,512]{2,1,0:T(8,128)S(1)} %bitcast.20), channel_id=1, replica_groups={{0,128,256},{64,192,320},{384,512,640},{448,576,704},{1,129,257},{65,19..., dimensions={0} | all-to-all | bytes 3145728 | tf_op jit(solution)/shard_map/all_to_all | solution.py:226
  208.6 0.1 slice_reduce_fusion
  208.8 6.3 %collective-permute-start.6 = (f32[128,512]{1,0:T(8,128)S(1)}, f32[128,512]{1,0:T(8,128)S(1)}, u32[]{:S(2)}, u32[]{:S(2)}) collective-permute-start(f32[128,512]{1,0:T(8,128)S(1)} %get-tuple-element.31), channel_id=1, source_target_pairs={{0,384},{64,448},{128,512},{192,576},{256,640},{320,704},{384,0},{... | collective-permute-start | bytes 786440 | tf_op jit(solution)/shard_map/ppermute | solution.py:230
  215.0 16.0 %collective-permute-done.6 = f32[128,512]{1,0:T(8,128)S(1)} collective-permute-done((f32[128,512]{1,0:T(8,128)S(1)}, f32[128,512]{1,0:T(8,128)S(1)}, u32[]{:S(2)}, u32[]{:S(2)}) %collective-permute-start.6) | collective-permute-done | bytes 262176 | tf_op jit(solution)/shard_map/ppermute | solution.py:230
  231.1 0.7 add_convert_fusion
  (1 shorter events, 0.0 us)
Async XLA Ops:
  6.5 54.8 %all-gather.3.cloned.1.call-start = ((), (), s32[]{:S(2)}) async-start(), calls=%async_computation.2 | async-start | bytes 1179648 | tf_op jit(solution)/shard_map/all_gather | solution.py:206
  8.1 21.3 %collective-permute-start = (bf16[24,2048]{1,0:T(8,128)(2,1)}, bf16[24,2048]{1,0:T(8,128)(2,1)S(1)}, u32[]{:S(2)}, u32[]{:S(2)}) collective-permute-start(bf16[24,2048]{1,0:T(8,128)(2,1)} %bitcast.24), channel_id=1, source_target_pairs={{0,8},{1,9},{2,10},{3,11},{4,12},{5,13},{6,14},{7,15},{8,0},{9,1},... | collective-permute-start | bytes 294920 | tf_op jit(solution)/shard_map/ppermute | solution.py:207
  24.0 1.2 copy-start.2
  27.3 1.4 copy-start
  61.4 79.5 %all-to-all-start = ((bf16[64,136,128]{2,1,0:T(8,128)(2,1)}), bf16[64,136,128]{2,1,0:T(8,128)(2,1)S(1)}, u32[]{:S(2)}, u32[]{:S(2)}) async-start(bf16[64,136,128]{2,1,0:T(8,128)(2,1)} %slice_dynamic-update-slice_fusion), calls=%async_computation | async-start | bytes 4456448 | tf_op jit(solution)/shard_map/all_to_all | solution.py:212
  77.6 75.9 %all-gather.5.cloned.1.call-start = ((), (), s32[]{:S(2)}) async-start(), calls=%async_computation.3 | async-start | bytes 3932160 | tf_op jit(solution)/shard_map/all_gather | solution.py:215
  79.7 52.1 %collective-permute-start.2 = (bf16[192,2048]{1,0:T(8,128)(2,1)S(1)}, bf16[192,2048]{1,0:T(8,128)(2,1)S(1)}, u32[]{:S(2)}, u32[]{:S(2)}) collective-permute-start(bf16[192,2048]{1,0:T(8,128)(2,1)S(1)} %all_gather.10.near), channel_id=1, source_target_pairs={{0,48},{1,49},{2,50},{3,51},{4,52},{5,53},{6,54},{7,55},{8,56},{9,... | collective-permute-start | bytes 2359304 | tf_op jit(solution)/shard_map/ppermute | solution.py:217
  82.4 52.2 %collective-permute-start.1 = (bf16[192,2048]{1,0:T(8,128)(2,1)S(1)}, bf16[192,2048]{1,0:T(8,128)(2,1)S(1)}, u32[]{:S(2)}, u32[]{:S(2)}) collective-permute-start(bf16[192,2048]{1,0:T(8,128)(2,1)S(1)} %all_gather.10.near), channel_id=1, source_target_pairs={{0,16},{1,17},{2,18},{3,19},{4,20},{5,21},{6,22},{7,23},{8,24},{9,... | collective-permute-start | bytes 2359304 | tf_op jit(solution)/shard_map/ppermute | solution.py:216
  131.8 2.8 %copy-start.3 = (bf16[192,2048]{1,0:T(8,128)(2,1)}, bf16[192,2048]{1,0:T(8,128)(2,1)S(1)}, u32[]{:S(2)}) copy-start(bf16[192,2048]{1,0:T(8,128)(2,1)S(1)} %collective-permute-done.2.right) | copy-start | bytes 2359300
  132.7 19.5 %collective-permute-start.4 = (bf16[96,2048]{1,0:T(8,128)(2,1)}, bf16[96,2048]{1,0:T(8,128)(2,1)S(1)}, u32[]{:S(2)}, u32[]{:S(2)}) collective-permute-start(bf16[96,2048]{1,0:T(8,128)(2,1)} %slice.52), channel_id=1, source_target_pairs={{0,48},{1,49},{2,50},{3,51},{4,52},{5,53},{6,54},{7,55},{8,56},{9,... | collective-permute-start | bytes 1179656 | tf_op jit(solution)/shard_map/ppermute | solution.py:220
  134.6 1.0 copy-start.4
  135.6 17.5 %collective-permute-start.3 = (bf16[96,2048]{1,0:T(8,128)(2,1)}, bf16[96,2048]{1,0:T(8,128)(2,1)}, u32[]{:S(2)}, u32[]{:S(2)}) collective-permute-start(bf16[96,2048]{1,0:T(8,128)(2,1)} %slice.51), channel_id=1, source_target_pairs={{0,16},{1,17},{2,18},{3,19},{4,20},{5,21},{6,22},{7,23},{8,24},{9,... | collective-permute-start | bytes 1179656 | tf_op jit(solution)/shard_map/ppermute | solution.py:219
  144.3 1.4 copy-start.1
  165.1 5.5 %collective-permute-start.5 = (f32[768,512]{1,0:T(8,128)}, f32[768,512]{1,0:T(8,128)S(1)}, u32[]{:S(2)}, u32[]{:S(2)}) collective-permute-start(f32[768,512]{1,0:T(8,128)} %get-tuple-element.30), channel_id=1, source_target_pairs={{0,64},{64,0},{128,192},{192,128},{256,320},{320,256},{384,448},{4... | collective-permute-start | bytes 4718600 | tf_op jit(solution)/shard_map/ppermute | solution.py:225
  208.8 22.3 %collective-permute-start.6 = (f32[128,512]{1,0:T(8,128)S(1)}, f32[128,512]{1,0:T(8,128)S(1)}, u32[]{:S(2)}, u32[]{:S(2)}) collective-permute-start(f32[128,512]{1,0:T(8,128)S(1)} %get-tuple-element.31), channel_id=1, source_target_pairs={{0,384},{64,448},{128,512},{192,576},{256,640},{320,704},{384,0},{... | collective-permute-start | bytes 786440 | tf_op jit(solution)/shard_map/ppermute | solution.py:230
Sparse Core Ops, SparseCore 0:
  9.7 51.5 all-gather.2
  80.8 72.6 all-gather.4
